TPU v7x, 32 devices: a whole 2x2x4 slice. The times are simulated.
32 devices in a mesh: dp: 16 (over z, x, core), tensor: 2 (over y).
Axes of the slice: x: 2, y: 2, z: 4, core: 2. Of those that a mesh axis runs over, the one named last changes fastest.
Arguments:
- inputs: bfloat16 [8192, 2048], P('dp', 'tensor'), may hold values from -6 to 6
- out_grad: bfloat16 [8192, 2048], P('dp', 'tensor'), may hold values from -6 to 6
- lengths: int32 [16], replicated, may hold values from 128 to 512, as said below
- dealing: int32 [16], replicated, may hold values from 0 to 15, each once
- qkv_weight: bfloat16 [3, 2048, 2048], P(None, 'dp', 'tensor'), may hold values from -0.125 to 0.125
- qv_bias: bfloat16 [2, 32, 64], P(None, 'tensor', 'dp'), may hold values from -0.29882812 to 0.29882812
- out_weight: bfloat16 [2048, 2048], P('tensor', 'dp'), may hold values from -2 to 2
- out_bias: bfloat16 [2048], P('dp'), may hold values from -1.796875 to 1.796875
- attn_gain: bfloat16 [2048], P('dp'), may hold values from 0.099609375 to 1.8984375
- attn_shift: bfloat16 [2048], P('dp'), may hold values from -1.796875 to 1.796875
- up_weight: bfloat16 [2048, 8192], P('dp', 'tensor'), may hold values from -0.125 to 0.125
- up_bias: bfloat16 [128, 64], P('tensor', 'dp'), may hold values from -3 to 3
- down_weight: bfloat16 [8192, 2048], P('tensor', 'dp'), may hold values from -0.0625 to 0.0625
- down_bias: bfloat16 [2048], P('dp'), may hold values from -1.796875 to 1.796875
- ffn_gain: bfloat16 [2048], P('dp'), may hold values from 0.099609375 to 1.8984375
- ffn_shift: bfloat16 [2048], P('dp'), may hold values from -1.796875 to 1.796875
Outputs:
- outputs: bfloat16 [8192, 2048], P('dp', 'tensor')
- in_grad: bfloat16 [8192, 2048], P('dp', 'tensor')
- qkv_grad: float32 [3, 2048, 2048], P(None, 'dp', 'tensor')
- qv_bias_grad: float32 [2, 32, 64], P(None, 'tensor', 'dp')
- out_weight_grad: float32 [2048, 2048], P('tensor', 'dp')
- out_bias_grad: float32 [2048], P('dp')
- attn_gain_grad: float32 [2048], P('dp')
- attn_shift_grad: float32 [2048], P('dp')
- up_weight_grad: float32 [2048, 8192], P('dp', 'tensor')
- up_bias_grad: float32 [128, 64], P('tensor', 'dp')
- down_weight_grad: float32 [8192, 2048], P('tensor', 'dp')
- down_bias_grad: float32 [2048], P('dp')
- ffn_gain_grad: float32 [2048], P('dp')
- ffn_shift_grad: float32 [2048], P('dp')
Inputs may be any that keep to these rules, and one draw needn't show every extreme that they name: `lengths`: the longest sequence has exactly 512 tokens. `dealing`: each sequence appears once.
All inputs are finite; a program needn't handle non-finite values.
Results may differ from a plain program's by a relative error of at most 0.02.
Values may be sent and summed in bfloat16 or wider, within the bound.
No kernel may reach another device: no remote copies, remote signals or barrier semaphores. Data moves between devices by JAX's collectives and lax.ppermute only.
A program may use at most 320 MiB of HBM per device.

v0:
```python
import jax
import jax.numpy as jnp
from jax import lax
from jax.sharding import PartitionSpec as P

HD = 128


epsilon = 1e-05
neg_large = -1e30


def gelu_value(values):
    return jax.nn.gelu(values, approximate=True)


def norm_forward(hidden, gain, shift):
    center = hidden - jnp.mean(hidden, axis=-1, keepdims=True)
    inverse = lax.rsqrt(jnp.mean(center * center, axis=-1, keepdims=True) + epsilon)
    normed = center * inverse
    return (normed * gain + shift, normed, inverse)


def norm_backward(grad_rows, normed, inverse, gain):
    scaled = grad_rows * gain
    mean_first = jnp.mean(scaled, axis=-1, keepdims=True)
    mean_second = jnp.mean(scaled * normed, axis=-1, keepdims=True)
    result = inverse * (scaled - mean_first - normed * mean_second)
    return (result, jnp.sum(grad_rows * normed, axis=0), jnp.sum(grad_rows, axis=0))


def local(
    inputs,
    out_grad,
    lengths,
    dealing,
    qkv_weight,
    qv_bias,
    out_weight,
    out_bias,
    attn_gain,
    attn_shift,
    up_weight,
    up_bias,
    down_weight,
    down_bias,
    ffn_gain,
    ffn_shift,
):
    groups = lax.axis_size("dp")
    seq_len = inputs.shape[0]
    half = inputs.shape[1]
    per_peer = seq_len // groups
    group_index = lax.axis_index("dp")
    column_start = lax.axis_index("tensor") * half
    local_rows = inputs.reshape(groups, per_peer, half).swapaxes(0, 1)
    sending = jnp.take(local_rows, dealing, axis=1)
    arrived = lax.all_to_all(sending, "dp", split_axis=1, concat_axis=1, tiled=True)
    token_half = arrived.reshape(seq_len, half)
    token_rows, cotangent = (
        lax.all_gather(token_half, "tensor", axis=1, tiled=True),
        lax.all_gather(out_grad, "tensor", axis=1, tiled=True),
    )
    my_length = jnp.take(lengths, jnp.take(dealing, group_index))
    valid_keys = jnp.arange(seq_len, dtype=jnp.int32) < my_length
    (
        qkv_full,
        qv_full,
        out_full,
        out_bias_full,
        gain_one,
        shift_one,
        up_full,
        up_bias_full,
        down_full,
        down_bias_full,
        gain_two,
        shift_two,
    ) = (
        lax.all_gather(qkv_weight, "dp", axis=1, tiled=True),
        lax.all_gather(qv_bias, "dp", axis=2, tiled=True),
        lax.all_gather(out_weight, "dp", axis=1, tiled=True),
        lax.all_gather(out_bias, "dp", axis=0, tiled=True),
        lax.all_gather(attn_gain, "dp", axis=0, tiled=True),
        lax.all_gather(attn_shift, "dp", axis=0, tiled=True),
        lax.all_gather(up_weight, "dp", axis=0, tiled=True),
        lax.all_gather(up_bias, "dp", axis=1, tiled=True),
        lax.all_gather(down_weight, "dp", axis=1, tiled=True),
        lax.all_gather(down_bias, "dp", axis=0, tiled=True),
        lax.all_gather(ffn_gain, "dp", axis=0, tiled=True),
        lax.all_gather(ffn_shift, "dp", axis=0, tiled=True),
    )
    qv_rows = qv_full.reshape(2, half)
    heads = half // HD
    scale = HD ** (-0.5)
    block = min(512, seq_len)
    count = seq_len // block
    projected = jnp.einsum("ld,cde->cle", token_rows, qkv_full, preferred_element_type=jnp.float32)
    query_rows = (projected[0] + qv_rows[0]).astype(jnp.bfloat16).reshape(seq_len, heads, HD)
    key_rows = projected[1].astype(jnp.bfloat16).reshape(seq_len, heads, HD)
    value_rows = (projected[2] + qv_rows[1]).astype(jnp.bfloat16).reshape(seq_len, heads, HD)

    def block_scores():
        scores = (
            jnp.einsum("qhe,khe->hqk", query_rows, key_rows, preferred_element_type=jnp.float32)
            * scale
        )
        return (query_rows, jnp.where(valid_keys[None, None, :], scores, neg_large))

    def attend(position):
        unused, scores = block_scores()
        top = jnp.max(scores, axis=-1, keepdims=True)
        expo = jnp.exp(scores - top)
        total = jnp.sum(expo, axis=-1, keepdims=True)
        weights = (expo / total).astype(jnp.bfloat16)
        context_block = jnp.einsum(
            "hqk,khe->qhe", weights, value_rows, preferred_element_type=jnp.float32
        )
        return (context_block.astype(jnp.bfloat16), (top + jnp.log(total))[..., 0])

    context_blocks, log_totals = lax.map(attend, jnp.arange(count))
    context = context_blocks.reshape(seq_len, half)
    token_float = token_rows.astype(jnp.float32)
    attended = (
        lax.psum(
            jnp.dot(context, out_full, preferred_element_type=jnp.float32).astype(jnp.bfloat16),
            "tensor",
        ).astype(jnp.float32)
        + out_bias_full
    )
    first, normed_one, inverse_one = norm_forward(token_float + attended, gain_one, shift_one)
    first_low = first.astype(jnp.bfloat16)
    pre_act = jnp.dot(
        first_low, up_full, preferred_element_type=jnp.float32
    ) + up_bias_full.reshape(-1)
    hidden = gelu_value(pre_act).astype(jnp.bfloat16)
    mixed = (
        lax.psum(
            jnp.dot(hidden, down_full, preferred_element_type=jnp.float32).astype(jnp.bfloat16),
            "tensor",
        ).astype(jnp.float32)
        + down_bias_full
    )
    final, normed_two, inverse_two = norm_forward(first + mixed, gain_two, shift_two)
    outputs = lax.dynamic_slice_in_dim(final, column_start, half, 1).astype(jnp.bfloat16)
    second_grad, gain_two_grad, shift_two_grad = norm_backward(
        cotangent.astype(jnp.float32), normed_two, inverse_two, gain_two
    )
    mixed_grad = second_grad.astype(jnp.bfloat16)
    down_bias_grad = jnp.sum(mixed_grad, axis=0, dtype=jnp.float32)
    down_weight_grad = jnp.einsum(
        "lf,ld->fd", hidden, mixed_grad, preferred_element_type=jnp.float32
    )
    hidden_grad = jnp.einsum("ld,fd->lf", mixed_grad, down_full, preferred_element_type=jnp.float32)
    unused_value, gelu_pull = jax.vjp(gelu_value, pre_act)
    pre_grad = gelu_pull(hidden_grad)[0].astype(jnp.bfloat16)
    up_bias_grad = jnp.sum(pre_grad, axis=0, dtype=jnp.float32).reshape(up_bias_full.shape)
    up_weight_grad = jnp.einsum(
        "ld,lf->df", first_low, pre_grad, preferred_element_type=jnp.float32
    )
    first_grad = second_grad + lax.psum(
        jnp.einsum("lf,df->ld", pre_grad, up_full, preferred_element_type=jnp.float32).astype(
            jnp.bfloat16
        ),
        "tensor",
    ).astype(jnp.float32)
    attn_total_grad, gain_one_grad, shift_one_grad = norm_backward(
        first_grad, normed_one, inverse_one, gain_one
    )
    attended_grad = attn_total_grad.astype(jnp.bfloat16)
    out_bias_grad = jnp.sum(attended_grad, axis=0, dtype=jnp.float32)
    out_weight_grad = jnp.einsum(
        "le,ld->ed", context, attended_grad, preferred_element_type=jnp.float32
    )
    context_grad = jnp.einsum(
        "ld,ed->le", attended_grad, out_full, preferred_element_type=jnp.float32
    )
    context_grad = context_grad.astype(jnp.bfloat16).reshape(seq_len, heads, HD)

    def back_step(carry, position):
        key_total, value_total = carry
        query_block, scores = block_scores()
        block_totals = lax.dynamic_index_in_dim(log_totals, position, 0, keepdims=False)
        probs = jnp.exp(scores - block_totals[..., None])
        prob_grad = jnp.einsum(
            "qhe,khe->hqk", context_grad, value_rows, preferred_element_type=jnp.float32
        )
        score_grad = (
            probs * (prob_grad - jnp.sum(prob_grad * probs, axis=-1, keepdims=True))
        ).astype(jnp.bfloat16)
        query_grad = (
            jnp.einsum("hqk,khe->qhe", score_grad, key_rows, preferred_element_type=jnp.float32)
            * scale
        )
        key_total = (
            key_total
            + jnp.einsum(
                "hqk,qhe->khe", score_grad, query_block, preferred_element_type=jnp.float32
            )
            * scale
        )
        value_total = value_total + jnp.einsum(
            "hqk,qhe->khe",
            probs.astype(jnp.bfloat16),
            context_grad,
            preferred_element_type=jnp.float32,
        )
        return ((key_total, value_total), query_grad)

    empty = jnp.zeros((seq_len, heads, HD), jnp.float32)
    (key_grad, value_grad), query_grad = lax.scan(back_step, (empty, empty), jnp.arange(count))
    stacked = jnp.stack(
        [
            query_grad.reshape(seq_len, half),
            key_grad.reshape(seq_len, half),
            value_grad.reshape(seq_len, half),
        ]
    ).astype(jnp.bfloat16)
    qkv_grad = jnp.einsum("ld,cle->cde", token_rows, stacked, preferred_element_type=jnp.float32)
    qv_grad = jnp.sum(stacked[0::2], axis=1, dtype=jnp.float32).reshape(qv_full.shape)
    part_grad = jnp.einsum("cle,cde->ld", stacked, qkv_full, preferred_element_type=jnp.float32)
    in_half = lax.psum_scatter(
        part_grad.astype(jnp.bfloat16), "tensor", scatter_dimension=1, tiled=True
    ).astype(jnp.float32) + lax.dynamic_slice_in_dim(attn_total_grad, column_start, half, 1)
    back_rows = in_half.astype(jnp.bfloat16).reshape(per_peer, groups, half)
    returned = lax.all_to_all(back_rows, "dp", split_axis=1, concat_axis=1, tiled=True)
    inverse_order = (
        jnp.zeros((groups,), jnp.int32).at[dealing].set(jnp.arange(groups, dtype=jnp.int32))
    )
    in_grad = jnp.take(returned, inverse_order, axis=1).swapaxes(0, 1).reshape(seq_len, half)
    every_shard = (
        lax.psum_scatter(qkv_grad, "dp", scatter_dimension=1, tiled=True),
        lax.psum_scatter(qv_grad, "dp", scatter_dimension=2, tiled=True),
        lax.psum_scatter(out_weight_grad, "dp", scatter_dimension=1, tiled=True),
        lax.psum_scatter(out_bias_grad, "dp", scatter_dimension=0, tiled=True),
        lax.psum_scatter(gain_one_grad, "dp", scatter_dimension=0, tiled=True),
        lax.psum_scatter(shift_one_grad, "dp", scatter_dimension=0, tiled=True),
        lax.psum_scatter(up_weight_grad, "dp", scatter_dimension=0, tiled=True),
        lax.psum_scatter(up_bias_grad, "dp", scatter_dimension=1, tiled=True),
        lax.psum_scatter(down_weight_grad, "dp", scatter_dimension=1, tiled=True),
        lax.psum_scatter(down_bias_grad, "dp", scatter_dimension=0, tiled=True),
        lax.psum_scatter(gain_two_grad, "dp", scatter_dimension=0, tiled=True),
        lax.psum_scatter(shift_two_grad, "dp", scatter_dimension=0, tiled=True),
    )
    attn_shards = tuple(every_shard[:6])
    ffn_shards = tuple(every_shard[6:])
    return (outputs, in_grad) + tuple(attn_shards) + tuple(ffn_shards)


def solution(mesh):
    placed = (
        P("dp", "tensor"),
        P("dp", "tensor"),
        P(),
        P(),
        P(None, "dp", "tensor"),
        P(None, "tensor", "dp"),
        P("tensor", "dp"),
        P("dp"),
        P("dp"),
        P("dp"),
        P("dp", "tensor"),
        P("tensor", "dp"),
        P("tensor", "dp"),
        P("dp"),
        P("dp"),
        P("dp"),
    )
    return jax.shard_map(
        local,
        mesh=mesh,
        in_specs=placed,
        out_specs=(
            P("dp", "tensor"),
            P("dp", "tensor"),
            P(None, "dp", "tensor"),
            P(None, "tensor", "dp"),
            P("tensor", "dp"),
            P("dp"),
            P("dp"),
            P("dp"),
            P("dp", "tensor"),
            P("tensor", "dp"),
            P("tensor", "dp"),
            P("dp"),
            P("dp"),
            P("dp"),
        ),
        check_vma=False,
    )
```

profile of v0, /device:TPU:0, one launch (start us, length us, event | category | flops | bytes accessed | tf_op | source)
XLA Modules:
  0.0 2004.1 jit_solution(12210204495245319963)
XLA Ops:
  9.5 32.0 %all_to_all.10 = bf16[32,16,1024]{2,0,1:T(8,128)(2,1)S(1)} all-to-all(bf16[32,16,1024]{2,0,1:T(8,128)(2,1)S(1)} %select_bitcast_fusion), channel_id=1, replica_groups=mesh['dp'=16,'tensor'=2] {'dp'}, dimensions={1} | all-to-all | bytes 2097152 | tf_op jit(solution)/shard_map/all_to_all | solution.py:58
  46.5 20.8 %all_gather.44 = bf16[2,16,64]{1,0,2:T(2,128)(2,1)S(1)} all-gather(bf16[2,16,4]{1,0,2:T(2,128)(2,1)S(1)} %copy.99), channel_id=1, replica_groups=mesh['dp'=16,'tensor'=2] {'dp'}, dimensions={2}, use_global_device_ids=true | all-gather | bytes 4352 | tf_op jit(solution)/shard_map/all_gather | solution.py:81
  68.3 8.4 all-gather.14.cloned.1.call-done
  76.7 103.0 %all-gather.16.cloned.1.call-done = bf16[3,2048,1024]{2,1,0:T(8,128)(2,1)} async-done(((bf16[3,128,1024]{2,1,0:T(8,128)(2,1)}), bf16[3,2048,1024]{2,1,0:T(8,128)(2,1)}) %all-gather.16.cloned.1.call-update) | async-done | bytes 12582928 | tf_op jit(solution)/shard_map/all_gather | solution.py:80
  179.7 9.9 convolution_bitcast_fusion.1
  206.0 27.3 %all-gather.18.cloned.1.call-done = bf16[1024,2048]{1,0:T(8,128)(2,1)} async-done(((bf16[1024,128]{1,0:T(8,128)(2,1)}), bf16[1024,2048]{1,0:T(8,128)(2,1)}) %all-gather.18.cloned.1.call-update) | async-done | bytes 4194320 | tf_op jit(solution)/shard_map/all_gather | solution.py:82
  240.4 18.6 all-gather
  259.0 17.4 all-gather.1
  276.5 18.6 all-gather.2
  295.1 17.6 all-gather.3
  316.4 113.2 %all-gather.20.cloned.1.call-done = bf16[2048,4096]{1,0:T(8,128)(2,1)} async-done(((bf16[128,4096]{1,0:T(8,128)(2,1)}), bf16[2048,4096]{1,0:T(8,128)(2,1)}) %all-gather.20.cloned.1.call-update) | async-done | bytes 16777232 | tf_op jit(solution)/shard_map/all_gather | solution.py:86
  429.6 15.5 fusion.33
  445.1 115.3 %all-gather.22.cloned.1.call-done = bf16[4096,2048]{1,0:T(8,128)(2,1)} async-done(((bf16[4096,128]{1,0:T(8,128)(2,1)}), bf16[4096,2048]{1,0:T(8,128)(2,1)}) %all-gather.22.cloned.1.call-update) | async-done | bytes 16777232 | tf_op jit(solution)/shard_map/all_gather | solution.py:88
  560.4 17.6 convolution_convert_fusion.2
  578.9 19.1 all-gather.4
  598.0 17.7 all-gather.5
  615.8 23.6 %all-reduce.16.cloned.1.call-done = bf16[512,2048]{1,0:T(8,128)(2,1)} async-done(((bf16[512,2048]{1,0:T(8,128)(2,1)}), bf16[512,2048]{1,0:T(8,128)(2,1)}) %all-reduce.16.cloned.1.call-update) | async-done | bytes 2097168 | tf_op jit(solution)/shard_map/psum | solution.py:138
  646.0 28.0 %all-gather.24.cloned.1.call-done = bf16[512,2048]{1,0:T(8,128)(2,1)} async-done(((bf16[512,1024]{1,0:T(8,128)(2,1)}), bf16[512,2048]{1,0:T(8,128)(2,1)}) %all-gather.24.cloned.1.call-update) | async-done | bytes 2097168 | tf_op jit(solution)/shard_map/all_gather | solution.py:62
  685.6 21.2 %convert_reduce_fusion = (f32[4096]{0:T(1024)S(1)}, bf16[512,4096]{1,0:T(8,128)(2,1)}) fusion(f32[512,4096]{1,0:T(8,128)} %fusion.33, f32[4096]{0:T(1024)S(1)} %reshape.235, bf16[4096,2048]{1,0:T(8,128)(2,1)} %all-gather.22.cloned.1.call-done, f32[512,2048]{1,0:T(8,128)} %fusion.13), kind=kOutput, calls=%fused_computation.13 | convolution fusion | flops 8639213568 | bytes 33587200 | tf_op jit(solution)/shard_map/ld,fd->lf/dot_general | solution.py:154
  706.8 14.8 convolution_convert_fusion.1
  721.7 63.0 %all-reduce.18.cloned.1.call-done = bf16[512,2048]{1,0:T(8,128)(2,1)} async-done(((bf16[512,2048]{1,0:T(8,128)(2,1)}), bf16[512,2048]{1,0:T(8,128)(2,1)}) %all-reduce.18.cloned.1.call-update) | async-done | bytes 2097168 | tf_op jit(solution)/shard_map/psum | solution.py:161
  825.2 11.7 bitcast_convert_fusion
  840.7 13.5 convolution_bitcast_fusion
  855.4 7.9 fusion.41
  863.3 20.3 %fusion.44 = f32[4096,2048]{1,0:T(8,128)} fusion(f32[512,2048]{1,0:T(8,128)} %fusion.13, f32[512,4096]{1,0:T(8,128)} %fusion.33, f32[4096]{0:T(1024)S(1)} %reshape.235), kind=kOutput, calls=%fused_computation.104 | convolution fusion | flops 8611954688 | bytes 46153728 | tf_op jit(solution)/shard_map/lf,ld->fd/dot_general | solution.py:151
  884.3 18.1 fusion.31
  914.5 30.9 %all-gather.6 = bf16[16,1,128]{2,1,0:T(2,128)(2,1)S(1)} all-gather(bf16[1,1,128]{2,1,0:T(2,128)(2,1)S(1)} %bitcast.140), channel_id=1, replica_groups=mesh['dp'=16,'tensor'=2] {'dp'}, dimensions={0}, use_global_device_ids=true | all-gather | bytes 4352 | tf_op jit(solution)/shard_map/all_gather | solution.py:91
  948.5 17.7 all-reduce.20.cloned.1.call-done
  978.3 237.0 %reduce-scatter.9.cloned.1.call-done = f32[3,128,1024]{1,2,0:T(8,128)} async-done(((f32[3,2048,1024]{1,2,0:T(8,128)}), f32[3,128,1024]{1,2,0:T(8,128)}) %reduce-scatter.9.cloned.1.call-update) | async-done | bytes 1572880 | tf_op jit(solution)/shard_map/reduce_scatter | solution.py:232
  1218.3 105.6 %reduce-scatter.11.cloned.1.call-done = f32[1024,128]{1,0:T(8,128)} async-done(((f32[1024,2048]{1,0:T(8,128)}), f32[1024,128]{1,0:T(8,128)}) %reduce-scatter.11.cloned.1.call-update) | async-done | bytes 524304 | tf_op jit(solution)/shard_map/reduce_scatter | solution.py:234
  1323.9 337.1 %reduce-scatter.15.cloned.1.call-done = f32[4096,128]{1,0:T(8,128)} async-done(((f32[4096,2048]{1,0:T(8,128)}), f32[4096,128]{1,0:T(8,128)}) %reduce-scatter.15.cloned.1.call-update) | async-done | bytes 2097168 | tf_op jit(solution)/shard_map/reduce_scatter | solution.py:240
  1661.0 336.4 %reduce-scatter.13.cloned.1.call-done = f32[128,4096]{1,0:T(8,128)} async-done(((f32[2048,4096]{1,0:T(8,128)}), f32[128,4096]{1,0:T(8,128)}) %reduce-scatter.13.cloned.1.call-update) | async-done | bytes 2097168 | tf_op jit(solution)/shard_map/reduce_scatter | solution.py:238
  (210 shorter events, 128.1 us)
Async XLA Ops:
  7.2 69.5 %all-gather.14.cloned.1.call-start = ((), (), s32[]{:S(2)}) async-start(), calls=%async_computation.7 | async-start | bytes 3145728 | tf_op jit(solution)/shard_map/all_gather | solution.py:61
  9.3 35.3 %copy-start.39 = (s32[16]{0:T(128)S(1)}, s32[16]{0:T(128)}, u32[]{:S(2)}) copy-start(s32[16]{0:T(128)} %param.21) | copy-start | bytes 196
  9.3 36.6 %copy-start.40 = (s32[16]{0:T(128)S(1)}, s32[16]{0:T(128)}, u32[]{:S(2)}) copy-start(s32[16]{0:T(128)} %param.20) | copy-start | bytes 196
  9.3 37.2 %copy-start.29 = (bf16[2,16,4]{1,2,0:T(4,128)(2,1)S(1)}, bf16[2,16,4]{1,2,0:T(4,128)(2,1)}, u32[]{:S(2)}) copy-start(bf16[2,16,4]{1,2,0:T(4,128)(2,1)} %param.23) | copy-start | bytes 772
  43.1 136.6 %all-gather.16.cloned.1.call-start = ((), (), s32[]{:S(2)}) async-start(), calls=%async_computation.8 | async-start | bytes 13369344 | tf_op jit(solution)/shard_map/all_gather | solution.py:80
  43.8 189.4 %all-gather.18.cloned.1.call-start = ((), (), s32[]{:S(2)}) async-start(), calls=%async_computation.9 | async-start | bytes 4456448 | tf_op jit(solution)/shard_map/all_gather | solution.py:82
  44.6 268.2 %all-reduce.14.cloned.1.call-start = ((), (), s32[]{:S(2)}) async-start(), calls=%async_computation.10 | async-start | bytes 4194304 | tf_op jit(solution)/shard_map/psum | solution.py:125
  67.6 130.4 %copy-start.27 = (f32[8,128]{1,0:T(8,128)}, f32[8,128]{1,0:T(8,128)S(1)}, u32[]{:S(2)}) copy-start(f32[8,128]{1,0:T(8,128)S(1)} %reshape.234) | copy-start | bytes 12292
  205.9 33.2 %copy-start.21 = (bf16[8,128,512]{2,1,0:T(8,128)(2,1)}, bf16[8,128,512]{2,1,0:T(8,128)(2,1)S(1)}, u32[]{:S(2)}) copy-start(bf16[8,128,512]{2,1,0:T(8,128)(2,1)S(1)} %fusion.27) | copy-start | bytes 3145732
  239.2 19.9 copy-start.32
  239.2 37.3 %copy-start.33 = (bf16[128]{0:T(256)(128)(2,1)S(1)}, bf16[128]{0:T(256)(128)(2,1)}, u32[]{:S(2)}) copy-start(bf16[128]{0:T(256)(128)(2,1)} %param.27) | copy-start | bytes 772
  239.2 55.9 %copy-start.30 = (bf16[64,4]{0,1:T(4,128)(2,1)S(1)}, bf16[64,4]{0,1:T(4,128)(2,1)}, u32[]{:S(2)}) copy-start(bf16[64,4]{0,1:T(4,128)(2,1)} %param.29) | copy-start | bytes 1540
  239.2 73.6 %copy-start.3 = (bf16[512,2048]{1,0:T(8,128)(2,1)S(1)}, bf16[512,2048]{1,0:T(8,128)(2,1)}, u32[]{:S(2)}) copy-start(bf16[512,2048]{1,0:T(8,128)(2,1)} %all-gather.14.cloned.1.call-done) | copy-start | bytes 6291460
  239.2 190.4 %all-gather.20.cloned.1.call-start = ((), (), s32[]{:S(2)}) async-start(), calls=%async_computation.11 | async-start | bytes 17825792 | tf_op jit(solution)/shard_map/all_gather | solution.py:86
  239.8 320.6 %all-gather.22.cloned.1.call-start = ((), (), s32[]{:S(2)}) async-start(), calls=%async_computation.12 | async-start | bytes 17825792 | tf_op jit(solution)/shard_map/all_gather | solution.py:88
  240.4 398.9 %all-reduce.16.cloned.1.call-start = ((), (), s32[]{:S(2)}) async-start(), calls=%async_computation.13 | async-start | bytes 4194304 | tf_op jit(solution)/shard_map/psum | solution.py:138
  295.1 379.0 %copy-start.23 = (f32[16,1,128]{2,1,0:T(1,128)}, f32[16,1,128]{2,1,0:T(1,128)S(1)}, u32[]{:S(2)}) copy-start(f32[16,1,128]{2,1,0:T(1,128)S(1)} %convert_element_type.196) | copy-start | bytes 24580
  445.1 133.8 %copy-start.34 = (bf16[128]{0:T(256)(128)(2,1)S(1)}, bf16[128]{0:T(256)(128)(2,1)}, u32[]{:S(2)}) copy-start(bf16[128]{0:T(256)(128)(2,1)} %param.31) | copy-start | bytes 772
  445.1 152.9 %copy-start.35 = (bf16[128]{0:T(256)(128)(2,1)S(1)}, bf16[128]{0:T(256)(128)(2,1)}, u32[]{:S(2)}) copy-start(bf16[128]{0:T(256)(128)(2,1)} %param.32) | copy-start | bytes 772
  578.1 96.0 %all-gather.24.cloned.1.call-start = ((), (), s32[]{:S(2)}) async-start(), calls=%async_computation.14 | async-start | bytes 3145728 | tf_op jit(solution)/shard_map/all_gather | solution.py:62
  578.8 205.8 %all-reduce.18.cloned.1.call-start = ((), (), s32[]{:S(2)}) async-start(), calls=%async_computation.15 | async-start | bytes 4194304 | tf_op jit(solution)/shard_map/psum | solution.py:161
  615.7 65.0 %copy-start.25 = (f32[16,1,128]{2,1,0:T(1,128)}, f32[16,1,128]{2,1,0:T(1,128)S(1)}, u32[]{:S(2)}) copy-start(f32[16,1,128]{2,1,0:T(1,128)S(1)} %convert_element_type.198) | copy-start | bytes 24580
  721.6 180.9 %reduce-scatter.7.cloned.1.call-start = ((), (), s32[]{:S(2)}) async-start(), calls=%async_computation.16 | async-start | bytes 3145728 | tf_op jit(solution)/shard_map/reduce_scatter | solution.py:222
  801.7 10.7 slice-start
  836.9 129.3 %all-reduce.20.cloned.1.call-start = ((), (), s32[]{:S(2)}) async-start(), calls=%async_computation.21 | async-start | bytes 294912
  840.7 374.6 %reduce-scatter.9.cloned.1.call-start = ((), (), s32[]{:S(2)}) async-start(), calls=%async_computation.17 | async-start | bytes 26738688 | tf_op jit(solution)/shard_map/reduce_scatter | solution.py:232
  854.2 469.6 %reduce-scatter.11.cloned.1.call-start = ((), (), s32[]{:S(2)}) async-start(), calls=%async_computation.18 | async-start | bytes 8912896 | tf_op jit(solution)/shard_map/reduce_scatter | solution.py:234
  863.3 797.7 %reduce-scatter.15.cloned.1.call-start = ((), (), s32[]{:S(2)}) async-start(), calls=%async_computation.20 | async-start | bytes 35651584 | tf_op jit(solution)/shard_map/reduce_scatter | solution.py:240
  883.6 1113.7 %reduce-scatter.13.cloned.1.call-start = ((), (), s32[]{:S(2)}) async-start(), calls=%async_computation.19 | async-start | bytes 35651584 | tf_op jit(solution)/shard_map/reduce_scatter | solution.py:238
  902.4 12.1 copy-start.36
  906.2 70.3 %all-to-all-start.1 = ((bf16[32,16,1024]{2,0,1:T(8,128)(2,1)}), bf16[32,16,1024]{2,0,1:T(8,128)(2,1)S(1)}, u32[]{:S(2)}, u32[]{:S(2)}) async-start(bf16[32,16,1024]{2,0,1:T(8,128)(2,1)} %copy.118), calls=%async_computation.2 | async-start | bytes 2097152 | tf_op jit(solution)/shard_map/all_to_all | solution.py:226
  945.5 1051.9 %copy-start.1 = (bf16[512,1024]{1,0:T(8,128)(2,1)S(1)}, bf16[512,1024]{1,0:T(8,128)(2,1)}, u32[]{:S(2)}) copy-start(bf16[512,1024]{1,0:T(8,128)(2,1)} %param.18) | copy-start | bytes 3145732
  (28 other events, 113.2 us)
Sparse Core Ops, SparseCore 0:
  43.2 33.4 all-gather.13
  78.9 100.7 all-gather.15
  181.9 51.3 all-gather.17
  239.3 61.0 all-reduce.13
  302.7 126.8 all-gather.19
  431.9 128.5 all-gather.21
  578.2 61.0 all-reduce.15
  640.9 33.1 all-gather.23
  721.7 62.9 all-reduce.17
  837.0 31.8 reduce-scatter.6
  873.2 92.8 all-reduce.19
  970.1 245.1 reduce-scatter.8
  1219.9 103.8 reduce-scatter.10
  1328.5 332.3 reduce-scatter.14
  1665.6 331.6 reduce-scatter.12
where the time goes:
time: 2010 us; the launch traced here: 2000 us
  waiting for transfers between devices  1520 us (76%)
  blocking collectives  193 us (10%)
  matrix products  179 us (9%)
  local copies, waits for them, and re-layouts  46.3 us (2%)
  other arithmetic  43.9 us (2%)
    reduce_scatter x1, waiting for transfers between devices, local(): lax.psum_scatter(down_weight_grad, 'dp', scatter_dimension=1, tiled=True)  337 us
    reduce_scatter x1, waiting for transfers between devices, local(): lax.psum_scatter(up_weight_grad, 'dp', scatter_dimension=0, tiled=True)  336 us
    reduce_scatter x1, waiting for transfers between devices, local(): lax.psum_scatter(qkv_grad, 'dp', scatter_dimension=1, tiled=True)  237 us
    all_gather x1, waiting for transfers between devices, local(): lax.all_gather(down_weight, 'dp', axis=1, tiled=True)  115 us
    all_gather x1, waiting for transfers between devices, local(): lax.all_gather(up_weight, 'dp', axis=0, tiled=True)  113 us
    reduce_scatter x1, waiting for transfers between devices, local(): lax.psum_scatter(out_weight_grad, 'dp', scatter_dimension=1, tiled=True)  106 us
    all_gather x1, waiting for transfers between devices, local(): lax.all_gather(qkv_weight, 'dp', axis=1, tiled=True)  103 us
    psum x1, waiting for transfers between devices, local(): lax.psum(jnp.einsum('lf,df->ld', pre_grad, up_full, preferred_element_typ...  63 us
  transfers between devices with their start and end apart: 16, of which 13 were waited for; matrix products, arithmetic and copies ran while one was open for 7% of the time, Pallas kernels for 0%

commit v1 on v0

v1 whole, which is shorter than its diff:
```python
import jax
import jax.numpy as jnp
from jax import lax
from jax.sharding import PartitionSpec as P

HD = 128


epsilon = 1e-05
neg_large = -1e30
low = jnp.bfloat16
wide = jnp.float32


def gelu_value(values):
    return jax.nn.gelu(values, approximate=True)


def norm_forward(hidden, gain, shift):
    center = hidden - jnp.mean(hidden, axis=-1, keepdims=True)
    inverse = lax.rsqrt(jnp.mean(center * center, axis=-1, keepdims=True) + epsilon)
    normed = center * inverse
    return (normed * gain + shift, normed, inverse)


def norm_backward(grad_rows, normed, inverse, gain):
    scaled = grad_rows * gain
    mean_first = jnp.mean(scaled, axis=-1, keepdims=True)
    mean_second = jnp.mean(scaled * normed, axis=-1, keepdims=True)
    result = inverse * (scaled - mean_first - normed * mean_second)
    return (result, jnp.sum(grad_rows * normed, axis=0), jnp.sum(grad_rows, axis=0))


def dot(left, right):
    return jnp.dot(left, right, preferred_element_type=wide)


def dot_ta(left, right):
    return jnp.einsum("la,lb->ab", left, right, preferred_element_type=wide)


def dot_tb(left, right):
    return jnp.einsum("la,ba->lb", left, right, preferred_element_type=wide)


def take(array, start, size, axis):
    return lax.dynamic_slice_in_dim(array, start, size, axis)


def local(
    inputs,
    out_grad,
    lengths,
    dealing,
    qkv_weight,
    qv_bias,
    out_weight,
    out_bias,
    attn_gain,
    attn_shift,
    up_weight,
    up_bias,
    down_weight,
    down_bias,
    ffn_gain,
    ffn_shift,
):
    groups = lax.axis_size("dp")
    ring_size = groups // 4
    index = lax.axis_index("dp")
    core, side, ring = index % 2, (index // 2) % 2, index // 4
    lane = lax.axis_index("tensor")
    core_pairs = [(i, i ^ 1) for i in range(groups)]
    side_pairs = [(i, i ^ 2) for i in range(groups)]
    ring_pairs = [(i, (i + 4) % groups) for i in range(groups)]

    def core_swap(array):
        return lax.ppermute(array, "dp", core_pairs)

    def side_swap(array):
        return lax.ppermute(array, "dp", side_pairs)

    def ring_shift(array):
        return lax.ppermute(array, "dp", ring_pairs)

    def lane_swap(array):
        return lax.ppermute(array, "tensor", [(0, 1), (1, 0)])

    def in_order(bit, mine, theirs, axis):
        first = jnp.where(bit == 0, mine, theirs)
        second = jnp.where(bit == 0, theirs, mine)
        return jnp.concatenate([first, second], axis=axis)

    seq_len, half = inputs.shape
    width = 2 * half
    per_peer = seq_len // groups
    shard = width // groups
    block = width // ring_size
    half_block = block // 2
    token_half = seq_len // 2

    small = jnp.concatenate(
        [
            v.reshape(-1)
            for v in (
                qv_bias,
                up_bias,
                out_bias,
                attn_gain,
                attn_shift,
                down_bias,
                ffn_gain,
                ffn_shift,
            )
        ]
    )
    small_all = lax.all_gather(small, "dp", axis=0, tiled=False)
    cut_one = qv_bias.size
    cut_two = cut_one + up_bias.size
    qv_full = (
        small_all[:, :cut_one]
        .reshape((groups,) + qv_bias.shape)
        .transpose(1, 2, 0, 3)
        .reshape(2, half)
    )
    up_bias_full = (
        small_all[:, cut_one:cut_two]
        .reshape((groups,) + up_bias.shape)
        .transpose(1, 0, 2)
        .reshape(-1)
    )
    vectors = (
        small_all[:, cut_two:].reshape(groups, 6, shard).transpose(1, 0, 2).reshape(6, width)
    ).astype(wide)
    out_bias_full, gain_one, shift_one, down_bias_full, gain_two, shift_two = vectors
    quarter = half // 2
    qv_rows = take(qv_full, core * quarter, quarter, 1)
    unit_half = up_bias_full.shape[0] // 2
    up_bias_mine = take(up_bias_full, core * unit_half, unit_half, 0)

    local_rows = inputs.reshape(groups, per_peer, half).swapaxes(0, 1)
    sending = jnp.take(local_rows, dealing, axis=1)
    arrived = lax.all_to_all(sending, "dp", split_axis=1, concat_axis=1, tiled=True)
    tokens = arrived.reshape(seq_len, half)
    own_rows = in_order(lane, tokens, lane_swap(tokens), 1)
    all_rows = in_order(core, own_rows, core_swap(own_rows), 0)
    residual = take(own_rows, lane * token_half, token_half, 0)
    grad_keep = take(out_grad, lane * token_half, token_half, 0)
    grad_send = take(out_grad, (1 - lane) * token_half, token_half, 0)
    cotangent = in_order(lane, grad_keep, lane_swap(grad_send), 1)

    def core_split(weight, unit_axis, width_axis):
        size = weight.shape[unit_axis] // 2
        mine = take(weight, core * size, size, unit_axis)
        sent = take(weight, (1 - core) * size, size, unit_axis)
        return in_order(core, mine, core_swap(sent), width_axis)

    def gather(piece):
        pieces = []
        for step in range(ring_size):
            if step:
                piece = ring_shift(piece)
            pieces.append((piece, side_swap(piece)))
        return pieces

    def assemble(pieces, axis):
        shape = list(pieces[0][0].shape)
        shape[axis] = width
        full = jnp.zeros(shape, low)
        for step, (mine, theirs) in enumerate(pieces):
            place = ((ring - step) % ring_size) * 2
            full = lax.dynamic_update_slice_in_dim(
                full, mine, (place + side) * half_block, axis
            )
            full = lax.dynamic_update_slice_in_dim(
                full, theirs, (place + 1 - side) * half_block, axis
            )
        return full

    qkv_full = assemble(gather(core_split(qkv_weight, 2, 1)), 1)
    out_full = assemble(gather(core_split(out_weight, 0, 1)), 1)
    up_full = assemble(gather(core_split(up_weight, 1, 0)), 0)
    down_full = assemble(gather(core_split(down_weight, 0, 1)), 1)

    def group_sum(partial):
        keep = take(partial, core * seq_len, seq_len, 0)
        sent = take(partial, (1 - core) * seq_len, seq_len, 0).astype(low)
        summed = keep + core_swap(sent).astype(wide)
        keep = take(summed, lane * token_half, token_half, 0)
        sent = take(summed, (1 - lane) * token_half, token_half, 0).astype(low)
        return keep + lane_swap(sent).astype(wide)

    def group_gather(rows):
        own = in_order(lane, rows, lane_swap(rows), 0)
        return own, in_order(core, own, core_swap(own), 0)

    heads = quarter // HD
    scale = HD ** (-0.5)
    rows = 2 * seq_len
    projected = jnp.einsum("ld,cde->cle", all_rows, qkv_full, preferred_element_type=wide)
    split = (2, seq_len, heads, HD)
    query = (projected[0] + qv_rows[0]).astype(low).reshape(split)
    key = projected[1].astype(low).reshape(split)
    value = (projected[2] + qv_rows[1]).astype(low).reshape(split)
    pair_lengths = jnp.take(lengths, take(dealing, (index // 2) * 2, 2, 0))
    valid = jnp.arange(seq_len, dtype=jnp.int32)[None, :] < pair_lengths[:, None]
    scores = (
        jnp.einsum("sqhe,skhe->shqk", query, key, preferred_element_type=wide) * scale
    )
    scores = jnp.where(valid[:, None, None, :], scores, neg_large)
    top = jnp.max(scores, axis=-1, keepdims=True)
    expo = jnp.exp(scores - top)
    probs = expo / jnp.sum(expo, axis=-1, keepdims=True)
    probs_low = probs.astype(low)
    context = (
        jnp.einsum("shqk,skhe->sqhe", probs_low, value, preferred_element_type=wide)
        .astype(low)
        .reshape(rows, quarter)
    )
    attended = group_sum(dot(context, out_full)) + out_bias_full
    first, normed_one, inverse_one = norm_forward(
        residual.astype(wide) + attended, gain_one, shift_one
    )
    unused, first_low = group_gather(first.astype(low))

    pre_act = dot(first_low, up_full) + up_bias_mine
    hidden = gelu_value(pre_act).astype(low)
    mixed = group_sum(dot(hidden, down_full)) + down_bias_full
    final, normed_two, inverse_two = norm_forward(first + mixed, gain_two, shift_two)
    final_low = final.astype(low)
    out_keep = take(final_low, lane * half, half, 1)
    out_send = take(final_low, (1 - lane) * half, half, 1)
    outputs = in_order(lane, out_keep, lane_swap(out_send), 0)

    second_grad, gain_two_grad, shift_two_grad = norm_backward(
        cotangent.astype(wide), normed_two, inverse_two, gain_two
    )
    mixed_low = second_grad.astype(low)
    down_bias_grad = jnp.sum(mixed_low, axis=0, dtype=wide)
    unused, mixed_grad = group_gather(mixed_low)

    def reduce(make, width_axis, unit_axis):
        total = None
        for step in range(ring_size):
            place = ((ring - 1 - step) % ring_size) * block
            partial = make(place)
            keep = take(partial, side * half_block, half_block, width_axis)
            sent = take(partial, (1 - side) * half_block, half_block, width_axis)
            both = keep + side_swap(sent.astype(low)).astype(wide)
            total = both if total is None else both + ring_shift(total.astype(low)).astype(wide)
        keep = take(total, core * shard, shard, width_axis)
        sent = take(total, (1 - core) * shard, shard, width_axis)
        return in_order(core, keep, core_swap(sent.astype(low)).astype(wide), unit_axis)

    down_weight_grad = reduce(
        lambda place: dot_ta(hidden, take(mixed_grad, place, block, 1)), 1, 0
    )
    hidden_grad = dot_tb(mixed_grad, down_full)
    unused_value, gelu_pull = jax.vjp(gelu_value, pre_act)
    pre_grad = gelu_pull(hidden_grad)[0].astype(low)
    up_bias_grad = jnp.sum(pre_grad, axis=0, dtype=wide)
    up_weight_grad = reduce(
        lambda place: dot_ta(take(first_low, place, block, 1), pre_grad), 0, 1
    )
    first_grad = second_grad + group_sum(dot_tb(pre_grad, up_full))
    attn_total_grad, gain_one_grad, shift_one_grad = norm_backward(
        first_grad, normed_one, inverse_one, gain_one
    )
    attended_low = attn_total_grad.astype(low)
    out_bias_grad = jnp.sum(attended_low, axis=0, dtype=wide)
    own_attended, attended_grad = group_gather(attended_low)
    out_weight_grad = reduce(
        lambda place: dot_ta(context, take(attended_grad, place, block, 1)), 1, 0
    )
    context_grad = dot_tb(attended_grad, out_full).astype(low).reshape(split)

    prob_grad = jnp.einsum("sqhe,skhe->shqk", context_grad, value, preferred_element_type=wide)
    score_grad = (
        probs * (prob_grad - jnp.sum(prob_grad * probs, axis=-1, keepdims=True))
    ).astype(low)
    query_grad = (
        jnp.einsum("shqk,skhe->sqhe", score_grad, key, preferred_element_type=wide) * scale
    )
    key_grad = (
        jnp.einsum("shqk,sqhe->skhe", score_grad, query, preferred_element_type=wide) * scale
    )
    value_grad = jnp.einsum(
        "shqk,sqhe->skhe", probs_low, context_grad, preferred_element_type=wide
    )
    stacked = jnp.stack(
        [g.astype(low).reshape(rows, quarter) for g in (query_grad, key_grad, value_grad)]
    )
    qv_grad = jnp.sum(stacked[0::2], axis=1, dtype=wide)
    qkv_grad = reduce(
        lambda place: jnp.einsum(
            "ld,cle->cde", take(all_rows, place, block, 1), stacked, preferred_element_type=wide
        ),
        1,
        2,
    )
    part_grad = jnp.einsum("cle,cde->ld", stacked, qkv_full, preferred_element_type=wide)
    keep = take(part_grad, core * seq_len, seq_len, 0)
    sent = take(part_grad, (1 - core) * seq_len, seq_len, 0).astype(low)
    own_part = keep + core_swap(sent).astype(wide)
    keep = take(own_part, lane * half, half, 1) + take(own_attended, lane * half, half, 1).astype(
        wide
    )
    sent = take(own_part, (1 - lane) * half, half, 1).astype(low)
    in_half = (keep + lane_swap(sent).astype(wide)).astype(low)
    back_rows = in_half.reshape(per_peer, groups, half)
    returned = lax.all_to_all(back_rows, "dp", split_axis=1, concat_axis=1, tiled=True)
    inverse_order = (
        jnp.zeros((groups,), jnp.int32).at[dealing].set(jnp.arange(groups, dtype=jnp.int32))
    )
    in_grad = jnp.take(returned, inverse_order, axis=1).swapaxes(0, 1).reshape(seq_len, half)

    def spread(mine, size):
        full = jnp.zeros(mine.shape[:-1] + (2 * size,), wide)
        return lax.dynamic_update_slice_in_dim(full, mine, core * size, mine.ndim - 1)

    qv_spread = (
        spread(qv_grad, quarter)
        .reshape(2, qv_bias.shape[1], groups, qv_bias.shape[2])
        .transpose(2, 0, 1, 3)
        .reshape(groups, -1)
    )
    up_spread = (
        spread(up_bias_grad, unit_half)
        .reshape(up_bias.shape[0], groups, up_bias.shape[1])
        .transpose(1, 0, 2)
        .reshape(groups, -1)
    )
    vector_spread = (
        jnp.stack(
            [
                out_bias_grad,
                gain_one_grad,
                shift_one_grad,
                down_bias_grad,
                gain_two_grad,
                shift_two_grad,
            ]
        )
        .reshape(6, groups, shard)
        .transpose(1, 0, 2)
        .reshape(groups, -1)
    )
    packed = jnp.concatenate([qv_spread, up_spread, vector_spread], axis=1)
    exchanged = lax.all_to_all(packed, "dp", split_axis=0, concat_axis=0, tiled=True)
    small_sum = jnp.sum(exchanged, axis=0)
    vector_sum = small_sum[cut_two:]
    vector_sum = (vector_sum + lane_swap(vector_sum)).reshape(6, shard)
    return (
        outputs,
        in_grad,
        qkv_grad,
        small_sum[:cut_one].reshape(qv_bias.shape),
        out_weight_grad,
        vector_sum[0],
        vector_sum[1],
        vector_sum[2],
        up_weight_grad,
        small_sum[cut_one:cut_two].reshape(up_bias.shape),
        down_weight_grad,
        vector_sum[3],
        vector_sum[4],
        vector_sum[5],
    )


def solution(mesh):
    placed = (
        P("dp", "tensor"),
        P("dp", "tensor"),
        P(),
        P(),
        P(None, "dp", "tensor"),
        P(None, "tensor", "dp"),
        P("tensor", "dp"),
        P("dp"),
        P("dp"),
        P("dp"),
        P("dp", "tensor"),
        P("tensor", "dp"),
        P("tensor", "dp"),
        P("dp"),
        P("dp"),
        P("dp"),
    )
    return jax.shard_map(
        local,
        mesh=mesh,
        in_specs=placed,
        out_specs=(
            P("dp", "tensor"),
            P("dp", "tensor"),
            P(None, "dp", "tensor"),
            P(None, "tensor", "dp"),
            P("tensor", "dp"),
            P("dp"),
            P("dp"),
            P("dp"),
            P("dp", "tensor"),
            P("tensor", "dp"),
            P("tensor", "dp"),
            P("dp"),
            P("dp"),
            P("dp"),
        ),
        check_vma=False,
    )
```

time: 2010 us -> 1090 us (0.54)
  waiting for transfers between devices: 1520 us -> 536 us
  blocking collectives: 193 us -> 31.1 us
  local copies, waits for them, and re-layouts: 46.3 us -> 164 us
  starting transfers between devices: 6.36 us -> 98.9 us
  other arithmetic: 43.9 us -> 92.4 us
  matrix products: 179 us -> 154 us
    reduce_scatter x5 -> x0, waiting for transfers between devices: 1020 us -> none  [the longest x1 337 us: local(): lax.psum_scatter(down_weight_grad, 'dp', scatter_dimension=1, tiled=True)]
    ppermute x0 -> x83, waiting for transfers between devices: none -> 494 us  [the longest x32 211 us: side_swap(): return lax.ppermute(array, 'dp', side_pairs)]
    all_gather x6 -> x0, waiting for transfers between devices: 395 us -> none  [the longest x1 115 us: local(): lax.all_gather(down_weight, 'dp', axis=1, tiled=True)]
    all_gather x8 -> x1, blocking collectives: 161 us -> 31.1 us  [local(): small_all = lax.all_gather(small, 'dp', axis=0, tiled=False)]
    psum x3 -> x0, waiting for transfers between devices: 86.6 us -> none  [the longest x1 63 us: local(): lax.psum(jnp.einsum('lf,df->ld', pre_grad, up_full, preferred_element_typ...]
    ppermute x0 -> x83, starting transfers between devices: none -> 79.2 us  [the longest x32 41.1 us: side_swap(): return lax.ppermute(array, 'dp', side_pairs)]
    convert_element_type x5 -> x34, local copies, waits for them, and re-layouts: 1.81 us -> 50.2 us  [the longest x16 24.6 us: reduce(): both = keep + side_swap(sent.astype(low)).astype(wide)]
    all_to_all x1 -> x0, blocking collectives: 32 us -> none  [local(): lax.all_to_all(sending, 'dp', split_axis=1, concat_axis=1, tiled=True)]
  transfers between devices with their start and end apart: 16 -> 86, of which waited for: 13 -> 41; matrix products, arithmetic and copies ran while one was open for 7% -> 15% of each run, Pallas kernels for 0% -> 0%
where the time goes in v1:
time: 1090 us; the launch traced here: 1080 us
  waiting for transfers between devices  536 us (49%)
  local copies, waits for them, and re-layouts  164 us (15%)
  matrix products  154 us (14%)
  starting transfers between devices  98.9 us (9%)
  other arithmetic  92.4 us (8%)
  blocking collectives  31.1 us (3%)
    ppermute x32, waiting for transfers between devices, side_swap(): return lax.ppermute(array, 'dp', side_pairs)  211 us
    ppermute x24, waiting for transfers between devices, ring_shift(): return lax.ppermute(array, 'dp', ring_pairs)  206 us
    ppermute x11, waiting for transfers between devices, lane_swap(): return lax.ppermute(array, 'tensor', [(0, 1), (1, 0)])  65.7 us
    dot_general x12, matrix products, dot_ta(): return jnp.einsum('la,lb->ab', left, right, preferred_element_type=wide)  43.2 us
    ppermute x32, starting transfers between devices, side_swap(): return lax.ppermute(array, 'dp', side_pairs)  41.1 us
    dot_general x3, matrix products, dot_tb(): return jnp.einsum('la,ba->lb', left, right, preferred_element_type=wide)  35.5 us
    dot_general x3, matrix products, dot(): return jnp.dot(left, right, preferred_element_type=wide)  31.4 us
    all_gather x1, blocking collectives, local(): small_all = lax.all_gather(small, 'dp', axis=0, tiled=False)  31.1 us
  transfers between devices with their start and end apart: 86, of which 41 were waited for; matrix products, arithmetic and copies ran while one was open for 15% of the time, Pallas kernels for 0%

profile of v1, /device:TPU:0, one launch (start us, length us, event | category | flops | bytes accessed | tf_op | source)
XLA Modules:
  0.0 1080.1 jit_solution(610763843663390682)
XLA Ops:
  13.4 20.9 %all-to-all-done = bf16[32,16,1024]{2,0,1:T(8,128)(2,1)S(1)} async-done(((bf16[32,16,1024]{2,0,1:T(8,128)(2,1)}), bf16[32,16,1024]{2,0,1:T(8,128)(2,1)S(1)}, u32[]{:S(2)}, u32[]{:S(2)}) %all-to-all-start) | async-done | bytes 1048608 | tf_op jit(solution)/shard_map/all_to_all | solution.py:143
  49.9 16.1 %collective-permute-done.12 = bf16[512,256]{1,0:T(8,128)(2,1)S(1)} collective-permute-done((bf16[512,256]{1,0:T(8,128)(2,1)}, bf16[512,256]{1,0:T(8,128)(2,1)S(1)}, u32[]{:S(2)}, u32[]{:S(2)}) %collective-permute-start.12) | collective-permute-done | bytes 262176 | tf_op jit(solution)/shard_map/ppermute | solution.py:84
  75.1 31.1 %all-gather.1 = bf16[16,1,1152]{2,1,0:T(2,128)(2,1)S(1)} all-gather(bf16[1,1,1152]{2,1,0:T(2,128)(2,1)S(1)} %reshape.298), channel_id=2, replica_groups=mesh['dp'=16,'tensor'=2] {'dp'}, dimensions={0}, use_global_device_ids=true | all-gather | bytes 39168 | tf_op jit(solution)/shard_map/all_gather | solution.py:117
  130.1 11.9 %collective-permute-done.17 = bf16[512,256]{1,0:T(8,128)(2,1)S(1)} collective-permute-done((bf16[512,256]{1,0:T(8,128)(2,1)}, bf16[512,256]{1,0:T(8,128)(2,1)S(1)}, u32[]{:S(2)}, u32[]{:S(2)}) %collective-permute-start.17) | collective-permute-done | bytes 262176 | tf_op jit(solution)/shard_map/ppermute | solution.py:81
  164.3 10.2 collective-permute-done.8
  179.5 10.4 fusion.21
  212.8 11.8 %copy.129 = bf16[2,512,4,128]{3,2,1,0:T(4,128)(2,1)S(1)} copy(bf16[2,512,4,128]{1,3,2,0:T(8,128)(2,1)S(1)} %fusion.50) | data formatting | bytes 2097152 | tf_op jit(solution)/shard_map/convert_element_type | solution.py:217
  259.1 11.0 %collective-permute-done.24 = bf16[256,2048]{1,0:T(8,128)(2,1)} collective-permute-done((bf16[256,2048]{1,0:T(8,128)(2,1)}, bf16[256,2048]{1,0:T(8,128)(2,1)}, u32[]{:S(2)}, u32[]{:S(2)}) %collective-permute-start.24) | collective-permute-done | bytes 1048608 | tf_op jit(solution)/shard_map/ppermute | solution.py:84
  271.7 20.0 %collective-permute-done.32 = bf16[2048,256]{1,0:T(8,128)(2,1)} collective-permute-done((bf16[2048,256]{1,0:T(8,128)(2,1)}, bf16[2048,256]{1,0:T(8,128)(2,1)}, u32[]{:S(2)}, u32[]{:S(2)}) %collective-permute-start.32) | collective-permute-done | bytes 1048608 | tf_op jit(solution)/shard_map/ppermute | solution.py:84
  309.0 10.8 %collective-permute-done.26 = bf16[256,2048]{1,0:T(8,128)(2,1)S(1)} collective-permute-done((bf16[256,2048]{1,0:T(8,128)(2,1)}, bf16[256,2048]{1,0:T(8,128)(2,1)S(1)}, u32[]{:S(2)}, u32[]{:S(2)}) %collective-permute-start.26) | collective-permute-done | bytes 1048608 | tf_op jit(solution)/shard_map/ppermute | solution.py:84
  330.4 11.9 %collective-permute-done.34 = bf16[2048,256]{1,0:T(8,128)(2,1)S(1)} collective-permute-done((bf16[2048,256]{1,0:T(8,128)(2,1)}, bf16[2048,256]{1,0:T(8,128)(2,1)S(1)}, u32[]{:S(2)}, u32[]{:S(2)}) %collective-permute-start.34) | collective-permute-done | bytes 1048608 | tf_op jit(solution)/shard_map/ppermute | solution.py:84
  352.0 12.8 %collective-permute-done.28 = bf16[256,2048]{1,0:T(8,128)(2,1)S(1)} collective-permute-done((bf16[256,2048]{1,0:T(8,128)(2,1)S(1)}, bf16[256,2048]{1,0:T(8,128)(2,1)S(1)}, u32[]{:S(2)}, u32[]{:S(2)}) %collective-permute-start.28) | collective-permute-done | bytes 1048608 | tf_op jit(solution)/shard_map/ppermute | solution.py:84
  366.6 18.9 %collective-permute-done.36 = bf16[2048,256]{1,0:T(8,128)(2,1)S(1)} collective-permute-done((bf16[2048,256]{1,0:T(8,128)(2,1)S(1)}, bf16[2048,256]{1,0:T(8,128)(2,1)S(1)}, u32[]{:S(2)}, u32[]{:S(2)}) %collective-permute-start.36) | collective-permute-done | bytes 1048608 | tf_op jit(solution)/shard_map/ppermute | solution.py:84
  396.0 22.2 %collective-permute-done.29 = bf16[256,2048]{1,0:T(8,128)(2,1)S(1)} collective-permute-done((bf16[256,2048]{1,0:T(8,128)(2,1)S(1)}, bf16[256,2048]{1,0:T(8,128)(2,1)S(1)}, u32[]{:S(2)}, u32[]{:S(2)}) %collective-permute-start.29) | collective-permute-done | bytes 1048608 | tf_op jit(solution)/shard_map/ppermute | solution.py:81
  419.2 20.3 %collective-permute-done.37 = bf16[2048,256]{1,0:T(8,128)(2,1)S(1)} collective-permute-done((bf16[2048,256]{1,0:T(8,128)(2,1)S(1)}, bf16[2048,256]{1,0:T(8,128)(2,1)S(1)}, u32[]{:S(2)}, u32[]{:S(2)}) %collective-permute-start.37) | collective-permute-done | bytes 1048608 | tf_op jit(solution)/shard_map/ppermute | solution.py:81
  440.9 18.3 %multiply_convert_fusion.1 = (bf16[1024,2048]{1,0:T(8,128)(2,1)S(1)}, f32[1024,2048]{1,0:T(8,128)}) fusion(f32[2048]{0:T(1024)S(1)} %dynamic-slice_convert_fusion.28, bf16[2048,2048]{1,0:T(8,128)(2,1)} %constant_dynamic-update-slice_fusion.9, bf16[512,2048]{1,0:T(8,128)(2,1)S(1)} %get-tuple-element.81, bf16[512,2048]{1,0:T(8,128)(2,1)S(1)} %get-tuple-element.80), kind=kOutput, calls=%fused_computation.17 | convolution fusion | flops 8619294720 | bytes 25174016 | tf_op jit(solution)/shard_map/dot_general | solution.py:35
  476.3 33.8 %collective-permute-done.41 = bf16[256,1024]{1,0:T(8,128)(2,1)S(1)} collective-permute-done((bf16[256,1024]{1,0:T(8,128)(2,1)S(1)}, bf16[256,1024]{1,0:T(8,128)(2,1)S(1)}, u32[]{:S(2)}, u32[]{:S(2)}) %collective-permute-start.41) | collective-permute-done | bytes 524320 | tf_op jit(solution)/shard_map/ppermute | solution.py:87
  515.1 22.9 %collective-permute-done.42 = bf16[256,2048]{1,0:T(8,128)(2,1)S(1)} collective-permute-done((bf16[256,2048]{1,0:T(8,128)(2,1)S(1)}, bf16[256,2048]{1,0:T(8,128)(2,1)S(1)}, u32[]{:S(2)}, u32[]{:S(2)}) %collective-permute-start.42) | collective-permute-done | bytes 1048608 | tf_op jit(solution)/shard_map/ppermute | solution.py:87
  547.6 18.9 %convert_reduce_fusion = (f32[2048]{0:T(1024)S(1)}, bf16[1024,2048]{1,0:T(8,128)(2,1)S(1)}) fusion(f32[1024,2048]{1,0:T(8,128)} %get-tuple-element.138, f32[2048]{0:T(1024)S(1)} %dynamic-slice_convert_fusion.28, bf16[2048,2048]{1,0:T(8,128)(2,1)} %copy-done.36, bf16[512,2048]{1,0:T(8,128)(2,1)S(1)} %get-tuple-element.79, ...), kind=kOutput, calls=%fused_computation.14 | convolution fusion | flops 8646555648 | bytes 25182208 | tf_op jit(solution)/shard_map/la,ba->lb/dot_general | solution.py:43
  566.5 11.6 %fusion.180 = f32[1024,2048]{1,0:T(8,128)S(1)} fusion(bf16[1024,2048]{1,0:T(8,128)(2,1)S(1)} %get-tuple-element.140, bf16[2048,2048]{1,0:T(8,128)(2,1)} %constant_dynamic-update-slice_fusion.9), kind=kOutput, calls=%fused_computation.399 | convolution fusion | flops 8589934592 | bytes 20971520 | tf_op jit(solution)/shard_map/la,ba->lb/dot_general | solution.py:43
  650.8 65.3 %collective-permute-done.78 = bf16[2048,256]{1,0:T(8,128)(2,1)S(1)} collective-permute-done((bf16[2048,256]{1,0:T(8,128)(2,1)S(1)}, bf16[2048,256]{1,0:T(8,128)(2,1)S(1)}, u32[]{:S(2)}, u32[]{:S(2)}) %collective-permute-start.78) | collective-permute-done | bytes 1048608 | tf_op jit(solution)/shard_map/ppermute | solution.py:81
  724.5 19.7 %collective-permute-done.71 = bf16[256,2048]{1,0:T(8,128)(2,1)} collective-permute-done((bf16[256,2048]{1,0:T(8,128)(2,1)S(1)}, bf16[256,2048]{1,0:T(8,128)(2,1)}, u32[]{:S(2)}, u32[]{:S(2)}) %collective-permute-start.71) | collective-permute-done | bytes 1048608 | tf_op jit(solution)/shard_map/ppermute | solution.py:84
  750.2 14.2 %collective-permute-done.79 = bf16[2048,256]{1,0:T(8,128)(2,1)S(1)} collective-permute-done((bf16[2048,256]{1,0:T(8,128)(2,1)S(1)}, bf16[2048,256]{1,0:T(8,128)(2,1)S(1)}, u32[]{:S(2)}, u32[]{:S(2)}) %collective-permute-start.79) | collective-permute-done | bytes 1048608 | tf_op jit(solution)/shard_map/ppermute | solution.py:84
  775.5 17.1 %collective-permute-done.72 = bf16[256,2048]{1,0:T(8,128)(2,1)} collective-permute-done((bf16[256,2048]{1,0:T(8,128)(2,1)}, bf16[256,2048]{1,0:T(8,128)(2,1)}, u32[]{:S(2)}, u32[]{:S(2)}) %collective-permute-start.72) | collective-permute-done | bytes 1048608 | tf_op jit(solution)/shard_map/ppermute | solution.py:84
  797.7 14.4 %collective-permute-done.80 = bf16[2048,256]{1,0:T(8,128)(2,1)} collective-permute-done((bf16[2048,256]{1,0:T(8,128)(2,1)}, bf16[2048,256]{1,0:T(8,128)(2,1)}, u32[]{:S(2)}, u32[]{:S(2)}) %collective-permute-start.80) | collective-permute-done | bytes 1048608 | tf_op jit(solution)/shard_map/ppermute | solution.py:84
  824.9 15.0 %collective-permute-done.73 = bf16[256,2048]{1,0:T(8,128)(2,1)S(1)} collective-permute-done((bf16[256,2048]{1,0:T(8,128)(2,1)S(1)}, bf16[256,2048]{1,0:T(8,128)(2,1)S(1)}, u32[]{:S(2)}, u32[]{:S(2)}) %collective-permute-start.73) | collective-permute-done | bytes 1048608 | tf_op jit(solution)/shard_map/ppermute | solution.py:84
  842.0 16.5 %collective-permute-done.81 = bf16[2048,256]{1,0:T(8,128)(2,1)S(1)} collective-permute-done((bf16[2048,256]{1,0:T(8,128)(2,1)S(1)}, bf16[2048,256]{1,0:T(8,128)(2,1)S(1)}, u32[]{:S(2)}, u32[]{:S(2)}) %collective-permute-start.81) | collective-permute-done | bytes 1048608 | tf_op jit(solution)/shard_map/ppermute | solution.py:84
  906.3 10.2 convolution_bitcast_fusion
  940.3 9.7 collective-permute-done.53
  959.5 29.2 %collective-permute-done.61 = bf16[512,256]{1,0:T(8,128)(2,1)S(1)} collective-permute-done((bf16[512,256]{1,0:T(8,128)(2,1)}, bf16[512,256]{1,0:T(8,128)(2,1)S(1)}, u32[]{:S(2)}, u32[]{:S(2)}) %collective-permute-start.61) | collective-permute-done | bytes 262176 | tf_op jit(solution)/shard_map/ppermute | solution.py:81
  1014.2 10.5 all-to-all-done.2
  1065.8 10.6 all-to-all-done.1
  (619 shorter events, 498.6 us)
Async XLA Ops:
  66.0 43.0 %collective-permute-start.13 = (bf16[512,256]{1,0:T(8,128)(2,1)S(1)}, bf16[512,256]{1,0:T(8,128)(2,1)}, u32[]{:S(2)}, u32[]{:S(2)}) collective-permute-start(bf16[512,256]{1,0:T(8,128)(2,1)S(1)} %collective-permute-done.12), channel_id=1, source_target_pairs={{0,4},{2,6},{4,0},{6,2},{8,12},{10,14},{12,8},{14,10},{16,20},{18,... | collective-permute-start | bytes 786440 | tf_op jit(solution)/shard_map/ppermute | solution.py:81
  68.2 38.7 %collective-permute-start.14 = (bf16[512,256]{1,0:T(8,128)(2,1)S(1)}, bf16[512,256]{1,0:T(8,128)(2,1)}, u32[]{:S(2)}, u32[]{:S(2)}) collective-permute-start(bf16[512,256]{1,0:T(8,128)(2,1)S(1)} %collective-permute-done.12), channel_id=1, source_target_pairs={{0,8},{2,10},{4,12},{6,14},{8,16},{10,18},{12,20},{14,22},{16,24},... | collective-permute-start | bytes 786440 | tf_op jit(solution)/shard_map/ppermute | solution.py:84
  69.1 54.6 %collective-permute-start.2 = (bf16[3,256,512]{1,2,0:T(8,128)(2,1)}, bf16[3,256,512]{1,2,0:T(8,128)(2,1)}, u32[]{:S(2)}, u32[]{:S(2)}) collective-permute-start(bf16[3,256,512]{1,2,0:T(8,128)(2,1)} %pad_maximum_fusion.22), channel_id=1, source_target_pairs={{0,4},{2,6},{4,0},{6,2},{8,12},{10,14},{12,8},{14,10},{16,20},{18,... | collective-permute-start | bytes 2359304 | tf_op jit(solution)/shard_map/ppermute | solution.py:81
  70.6 38.4 %collective-permute-start.5 = (bf16[3,256,512]{1,2,0:T(8,128)(2,1)}, bf16[3,256,512]{1,2,0:T(8,128)(2,1)}, u32[]{:S(2)}, u32[]{:S(2)}) collective-permute-start(bf16[3,256,512]{1,2,0:T(8,128)(2,1)} %collective-permute-done.3), channel_id=1, source_target_pairs={{0,8},{2,10},{4,12},{6,14},{8,16},{10,18},{12,20},{14,22},{16,24},... | collective-permute-start | bytes 2359304 | tf_op jit(solution)/shard_map/ppermute | solution.py:84
  74.9 101.9 %collective-permute-start.9 = (bf16[512,2048]{1,0:T(8,128)(2,1)}, bf16[512,2048]{1,0:T(8,128)(2,1)}, u32[]{:S(2)}, u32[]{:S(2)}) collective-permute-start(bf16[512,2048]{1,0:T(8,128)(2,1)} %pad_maximum_fusion.7), channel_id=1, source_target_pairs={{0,2},{2,0},{4,6},{6,4},{8,10},{10,8},{12,14},{14,12},{16,18},{18,... | collective-permute-start | bytes 6291464 | tf_op jit(solution)/shard_map/ppermute | solution.py:78
  247.6 44.1 %collective-permute-start.32 = (bf16[2048,256]{1,0:T(8,128)(2,1)}, bf16[2048,256]{1,0:T(8,128)(2,1)}, u32[]{:S(2)}, u32[]{:S(2)}) collective-permute-start(bf16[2048,256]{1,0:T(8,128)(2,1)} %get-tuple-element.107), channel_id=1, source_target_pairs={{0,8},{2,10},{4,12},{6,14},{8,16},{10,18},{12,20},{14,22},{16,24},... | collective-permute-start | bytes 3145736 | tf_op jit(solution)/shard_map/ppermute | solution.py:84
  257.1 40.6 %collective-permute-start.23 = (bf16[256,2048]{1,0:T(8,128)(2,1)}, bf16[256,2048]{1,0:T(8,128)(2,1)S(1)}, u32[]{:S(2)}, u32[]{:S(2)}) collective-permute-start(bf16[256,2048]{1,0:T(8,128)(2,1)} %get-tuple-element.109), channel_id=1, source_target_pairs={{0,4},{2,6},{4,0},{6,2},{8,12},{10,14},{12,8},{14,10},{16,20},{18,... | collective-permute-start | bytes 3145736 | tf_op jit(solution)/shard_map/ppermute | solution.py:81
  258.8 47.0 %collective-permute-start.31 = (bf16[2048,256]{1,0:T(8,128)(2,1)}, bf16[2048,256]{1,0:T(8,128)(2,1)S(1)}, u32[]{:S(2)}, u32[]{:S(2)}) collective-permute-start(bf16[2048,256]{1,0:T(8,128)(2,1)} %get-tuple-element.107), channel_id=1, source_target_pairs={{0,4},{2,6},{4,0},{6,2},{8,12},{10,14},{12,8},{14,10},{16,20},{18,... | collective-permute-start | bytes 3145736 | tf_op jit(solution)/shard_map/ppermute | solution.py:81
  270.0 58.2 %collective-permute-start.25 = (bf16[256,2048]{1,0:T(8,128)(2,1)}, bf16[256,2048]{1,0:T(8,128)(2,1)S(1)}, u32[]{:S(2)}, u32[]{:S(2)}) collective-permute-start(bf16[256,2048]{1,0:T(8,128)(2,1)} %collective-permute-done.24), channel_id=1, source_target_pairs={{0,4},{2,6},{4,0},{6,2},{8,12},{10,14},{12,8},{14,10},{16,20},{18,... | collective-permute-start | bytes 3145736 | tf_op jit(solution)/shard_map/ppermute | solution.py:81
  291.7 50.6 %collective-permute-start.34 = (bf16[2048,256]{1,0:T(8,128)(2,1)}, bf16[2048,256]{1,0:T(8,128)(2,1)S(1)}, u32[]{:S(2)}, u32[]{:S(2)}) collective-permute-start(bf16[2048,256]{1,0:T(8,128)(2,1)} %collective-permute-done.32), channel_id=1, source_target_pairs={{0,8},{2,10},{4,12},{6,14},{8,16},{10,18},{12,20},{14,22},{16,24},... | collective-permute-start | bytes 3145736 | tf_op jit(solution)/shard_map/ppermute | solution.py:84
  297.7 47.3 %collective-permute-start.20 = (bf16[256,2048]{1,0:T(8,128)(2,1)S(1)}, bf16[256,2048]{1,0:T(8,128)(2,1)S(1)}, u32[]{:S(2)}, u32[]{:S(2)}) collective-permute-start(bf16[256,2048]{1,0:T(8,128)(2,1)S(1)} %fusion.33), channel_id=1, source_target_pairs={{0,1},{1,0},{2,3},{3,2},{4,5},{5,4},{6,7},{7,6},{8,9},{9,8},{10,11... | collective-permute-start | bytes 3145736 | tf_op jit(solution)/shard_map/ppermute | solution.py:87
  305.8 44.9 %collective-permute-start.33 = (bf16[2048,256]{1,0:T(8,128)(2,1)}, bf16[2048,256]{1,0:T(8,128)(2,1)S(1)}, u32[]{:S(2)}, u32[]{:S(2)}) collective-permute-start(bf16[2048,256]{1,0:T(8,128)(2,1)} %collective-permute-done.32), channel_id=1, source_target_pairs={{0,4},{2,6},{4,0},{6,2},{8,12},{10,14},{12,8},{14,10},{16,20},{18,... | collective-permute-start | bytes 3145736 | tf_op jit(solution)/shard_map/ppermute | solution.py:81
  319.8 67.4 %collective-permute-start.27 = (bf16[256,2048]{1,0:T(8,128)(2,1)S(1)}, bf16[256,2048]{1,0:T(8,128)(2,1)S(1)}, u32[]{:S(2)}, u32[]{:S(2)}) collective-permute-start(bf16[256,2048]{1,0:T(8,128)(2,1)S(1)} %collective-permute-done.26), channel_id=1, source_target_pairs={{0,4},{2,6},{4,0},{6,2},{8,12},{10,14},{12,8},{14,10},{16,20},{18,... | collective-permute-start | bytes 3145736 | tf_op jit(solution)/shard_map/ppermute | solution.py:81
  342.3 53.4 %collective-permute-start.35 = (bf16[2048,256]{1,0:T(8,128)(2,1)S(1)}, bf16[2048,256]{1,0:T(8,128)(2,1)S(1)}, u32[]{:S(2)}, u32[]{:S(2)}) collective-permute-start(bf16[2048,256]{1,0:T(8,128)(2,1)S(1)} %collective-permute-done.34), channel_id=1, source_target_pairs={{0,4},{2,6},{4,0},{6,2},{8,12},{10,14},{12,8},{14,10},{16,20},{18,... | collective-permute-start | bytes 3145736 | tf_op jit(solution)/shard_map/ppermute | solution.py:81
  345.0 40.5 %collective-permute-start.36 = (bf16[2048,256]{1,0:T(8,128)(2,1)S(1)}, bf16[2048,256]{1,0:T(8,128)(2,1)S(1)}, u32[]{:S(2)}, u32[]{:S(2)}) collective-permute-start(bf16[2048,256]{1,0:T(8,128)(2,1)S(1)} %collective-permute-done.34), channel_id=1, source_target_pairs={{0,8},{2,10},{4,12},{6,14},{8,16},{10,18},{12,20},{14,22},{16,24},... | collective-permute-start | bytes 3145736 | tf_op jit(solution)/shard_map/ppermute | solution.py:84
  350.7 88.9 %collective-permute-start.21 = (bf16[512,2048]{1,0:T(8,128)(2,1)S(1)}, bf16[512,2048]{1,0:T(8,128)(2,1)S(1)}, u32[]{:S(2)}, u32[]{:S(2)}) collective-permute-start(bf16[512,2048]{1,0:T(8,128)(2,1)S(1)} %pad_maximum_fusion.9), channel_id=1, source_target_pairs={{0,2},{2,0},{4,6},{6,4},{8,10},{10,8},{12,14},{14,12},{16,18},{18,... | collective-permute-start | bytes 6291464 | tf_op jit(solution)/shard_map/ppermute | solution.py:78
  364.8 53.4 %collective-permute-start.29 = (bf16[256,2048]{1,0:T(8,128)(2,1)S(1)}, bf16[256,2048]{1,0:T(8,128)(2,1)S(1)}, u32[]{:S(2)}, u32[]{:S(2)}) collective-permute-start(bf16[256,2048]{1,0:T(8,128)(2,1)S(1)} %collective-permute-done.28), channel_id=1, source_target_pairs={{0,4},{2,6},{4,0},{6,2},{8,12},{10,14},{12,8},{14,10},{16,20},{18,... | collective-permute-start | bytes 3145736 | tf_op jit(solution)/shard_map/ppermute | solution.py:81
  385.5 54.0 %collective-permute-start.37 = (bf16[2048,256]{1,0:T(8,128)(2,1)S(1)}, bf16[2048,256]{1,0:T(8,128)(2,1)S(1)}, u32[]{:S(2)}, u32[]{:S(2)}) collective-permute-start(bf16[2048,256]{1,0:T(8,128)(2,1)S(1)} %collective-permute-done.36), channel_id=1, source_target_pairs={{0,4},{2,6},{4,0},{6,2},{8,12},{10,14},{12,8},{14,10},{16,20},{18,... | collective-permute-start | bytes 3145736 | tf_op jit(solution)/shard_map/ppermute | solution.py:81
  619.4 99.4 %collective-permute-start.44 = (bf16[512,2048]{1,0:T(8,128)(2,1)}, bf16[512,2048]{1,0:T(8,128)(2,1)}, u32[]{:S(2)}, u32[]{:S(2)}) collective-permute-start(bf16[512,2048]{1,0:T(8,128)(2,1)} %dynamic-slice_convert_fusion.1), channel_id=1, source_target_pairs={{0,2},{2,0},{4,6},{6,4},{8,10},{10,8},{12,14},{14,12},{16,18},{18,... | collective-permute-start | bytes 6291464 | tf_op jit(solution)/shard_map/ppermute | solution.py:78
  626.2 96.4 %collective-permute-start.69 = (bf16[256,2048]{1,0:T(8,128)(2,1)S(1)}, bf16[256,2048]{1,0:T(8,128)(2,1)S(1)}, u32[]{:S(2)}, u32[]{:S(2)}) collective-permute-start(bf16[256,2048]{1,0:T(8,128)(2,1)S(1)} %dynamic-slice_convert_fusion.9), channel_id=1, source_target_pairs={{0,4},{2,6},{4,0},{6,2},{8,12},{10,14},{12,8},{14,10},{16,20},{18,... | collective-permute-start | bytes 3145736 | tf_op jit(solution)/shard_map/ppermute | solution.py:81
  629.6 144.1 %collective-permute-start.68 = (bf16[256,2048]{1,0:T(8,128)(2,1)}, bf16[256,2048]{1,0:T(8,128)(2,1)}, u32[]{:S(2)}, u32[]{:S(2)}) collective-permute-start(bf16[256,2048]{1,0:T(8,128)(2,1)} %dynamic-slice_convert_fusion.10), channel_id=1, source_target_pairs={{0,4},{2,6},{4,0},{6,2},{8,12},{10,14},{12,8},{14,10},{16,20},{18,... | collective-permute-start | bytes 3145736 | tf_op jit(solution)/shard_map/ppermute | solution.py:81
  631.4 84.8 %collective-permute-start.78 = (bf16[2048,256]{1,0:T(8,128)(2,1)S(1)}, bf16[2048,256]{1,0:T(8,128)(2,1)S(1)}, u32[]{:S(2)}, u32[]{:S(2)}) collective-permute-start(bf16[2048,256]{1,0:T(8,128)(2,1)S(1)} %dynamic-slice_convert_fusion.4), channel_id=1, source_target_pairs={{0,4},{2,6},{4,0},{6,2},{8,12},{10,14},{12,8},{14,10},{16,20},{18,... | collective-permute-start | bytes 3145736 | tf_op jit(solution)/shard_map/ppermute | solution.py:81
  648.8 99.6 %collective-permute-start.77 = (bf16[2048,256]{1,0:T(8,128)(2,1)S(1)}, bf16[2048,256]{1,0:T(8,128)(2,1)}, u32[]{:S(2)}, u32[]{:S(2)}) collective-permute-start(bf16[2048,256]{1,0:T(8,128)(2,1)S(1)} %dynamic-slice_convert_fusion.5), channel_id=1, source_target_pairs={{0,4},{2,6},{4,0},{6,2},{8,12},{10,14},{12,8},{14,10},{16,20},{18,... | collective-permute-start | bytes 3145736 | tf_op jit(solution)/shard_map/ppermute | solution.py:81
  718.8 45.6 %collective-permute-start.79 = (bf16[2048,256]{1,0:T(8,128)(2,1)S(1)}, bf16[2048,256]{1,0:T(8,128)(2,1)S(1)}, u32[]{:S(2)}, u32[]{:S(2)}) collective-permute-start(bf16[2048,256]{1,0:T(8,128)(2,1)S(1)} %add_convert_fusion.2), channel_id=1, source_target_pairs={{0,8},{2,10},{4,12},{6,14},{8,16},{10,18},{12,20},{14,22},{16,24},... | collective-permute-start | bytes 3145736 | tf_op jit(solution)/shard_map/ppermute | solution.py:84
  722.6 102.3 %collective-permute-start.67 = (bf16[256,2048]{1,0:T(8,128)(2,1)}, bf16[256,2048]{1,0:T(8,128)(2,1)}, u32[]{:S(2)}, u32[]{:S(2)}) collective-permute-start(bf16[256,2048]{1,0:T(8,128)(2,1)} %dynamic-slice_convert_fusion.11), channel_id=1, source_target_pairs={{0,4},{2,6},{4,0},{6,2},{8,12},{10,14},{12,8},{14,10},{16,20},{18,... | collective-permute-start | bytes 3145736 | tf_op jit(solution)/shard_map/ppermute | solution.py:81
  748.4 48.4 %collective-permute-start.76 = (bf16[2048,256]{1,0:T(8,128)(2,1)}, bf16[2048,256]{1,0:T(8,128)(2,1)}, u32[]{:S(2)}, u32[]{:S(2)}) collective-permute-start(bf16[2048,256]{1,0:T(8,128)(2,1)} %dynamic-slice_convert_fusion.6), channel_id=1, source_target_pairs={{0,4},{2,6},{4,0},{6,2},{8,12},{10,14},{12,8},{14,10},{16,20},{18,... | collective-permute-start | bytes 3145736 | tf_op jit(solution)/shard_map/ppermute | solution.py:81
  767.5 44.5 %collective-permute-start.80 = (bf16[2048,256]{1,0:T(8,128)(2,1)}, bf16[2048,256]{1,0:T(8,128)(2,1)}, u32[]{:S(2)}, u32[]{:S(2)}) collective-permute-start(bf16[2048,256]{1,0:T(8,128)(2,1)} %add_convert_fusion.1), channel_id=1, source_target_pairs={{0,8},{2,10},{4,12},{6,14},{8,16},{10,18},{12,20},{14,22},{16,24},... | collective-permute-start | bytes 3145736 | tf_op jit(solution)/shard_map/ppermute | solution.py:84
  773.7 68.2 %collective-permute-start.75 = (bf16[2048,256]{1,0:T(8,128)(2,1)}, bf16[2048,256]{1,0:T(8,128)(2,1)S(1)}, u32[]{:S(2)}, u32[]{:S(2)}) collective-permute-start(bf16[2048,256]{1,0:T(8,128)(2,1)} %dynamic-slice_convert_fusion.7), channel_id=1, source_target_pairs={{0,4},{2,6},{4,0},{6,2},{8,12},{10,14},{12,8},{14,10},{16,20},{18,... | collective-permute-start | bytes 3145736 | tf_op jit(solution)/shard_map/ppermute | solution.py:81
  929.1 64.5 %collective-permute-start.48 = (bf16[512,2048]{1,0:T(8,128)(2,1)}, bf16[512,2048]{1,0:T(8,128)(2,1)}, u32[]{:S(2)}, u32[]{:S(2)}) collective-permute-start(bf16[512,2048]{1,0:T(8,128)(2,1)} %dynamic-slice_convert_fusion), channel_id=1, source_target_pairs={{0,2},{2,0},{4,6},{6,4},{8,10},{10,8},{12,14},{14,12},{16,18},{18,... | collective-permute-start | bytes 6291464 | tf_op jit(solution)/shard_map/ppermute | solution.py:78
  932.5 58.0 %collective-permute-start.52 = (bf16[3,256,512]{1,2,0:T(8,128)(2,1)}, bf16[3,256,512]{1,2,0:T(8,128)(2,1)}, u32[]{:S(2)}, u32[]{:S(2)}) collective-permute-start(bf16[3,256,512]{1,2,0:T(8,128)(2,1)} %fusion.120), channel_id=1, source_target_pairs={{0,4},{2,6},{4,0},{6,2},{8,12},{10,14},{12,8},{14,10},{16,20},{18,... | collective-permute-start | bytes 2359304 | tf_op jit(solution)/shard_map/ppermute | solution.py:81
  933.7 96.4 %collective-permute-start.51 = (bf16[3,256,512]{1,2,0:T(8,128)(2,1)}, bf16[3,256,512]{1,2,0:T(8,128)(2,1)}, u32[]{:S(2)}, u32[]{:S(2)}) collective-permute-start(bf16[3,256,512]{1,2,0:T(8,128)(2,1)} %fusion.119), channel_id=1, source_target_pairs={{0,4},{2,6},{4,0},{6,2},{8,12},{10,14},{12,8},{14,10},{16,20},{18,... | collective-permute-start | bytes 2359304 | tf_op jit(solution)/shard_map/ppermute | solution.py:81
  951.2 39.7 %collective-permute-start.54 = (bf16[3,256,512]{1,2,0:T(8,128)(2,1)}, bf16[3,256,512]{1,2,0:T(8,128)(2,1)}, u32[]{:S(2)}, u32[]{:S(2)}) collective-permute-start(bf16[3,256,512]{1,2,0:T(8,128)(2,1)} %fusion.34), channel_id=1, source_target_pairs={{0,8},{2,10},{4,12},{6,14},{8,16},{10,18},{12,20},{14,22},{16,24},... | collective-permute-start | bytes 2359304 | tf_op jit(solution)/shard_map/ppermute | solution.py:84
  (157 other events, 2899.7 us)

commit v2 on v1

v2 whole, which is shorter than its diff:
```python
import functools
import math

import jax
import jax.numpy as jnp
from jax import lax
from jax.experimental import pallas as pl
from jax.experimental.pallas import tpu as pltpu
from jax.sharding import PartitionSpec as P

HD = 128


epsilon = 1e-05
neg_large = -1e30
low = jnp.bfloat16
wide = jnp.float32
COST_SCALE = 8


def norm_forward(hidden, gain, shift):
    center = hidden - jnp.mean(hidden, axis=-1, keepdims=True)
    inverse = lax.rsqrt(jnp.mean(center * center, axis=-1, keepdims=True) + epsilon)
    normed = center * inverse
    return (normed * gain + shift, normed, inverse)


def norm_backward(grad_rows, normed, inverse, gain):
    scaled = grad_rows * gain
    mean_first = jnp.mean(scaled, axis=-1, keepdims=True)
    mean_second = jnp.mean(scaled * normed, axis=-1, keepdims=True)
    result = inverse * (scaled - mean_first - normed * mean_second)
    return (result, jnp.sum(grad_rows * normed, axis=0), jnp.sum(grad_rows, axis=0))


def after(array, *others):
    return lax.optimization_barrier((array,) + others)[0] if others else array


def take(array, start, size, axis):
    return lax.dynamic_slice_in_dim(array, start, size, axis)


kernel_params = pltpu.CompilerParams(vmem_limit_bytes=40 * 1024 * 1024)


def product(left, right, left_axis, right_axis):
    dims = (((left_axis,), (right_axis,)), ((), ()))
    return lax.dot_general(left, right, dims, preferred_element_type=wide)


def call(kernel, flops, out_shape, **settings):
    return pl.pallas_call(
        kernel,
        out_shape=out_shape,
        compiler_params=kernel_params,
        cost_estimate=pl.CostEstimate(
            flops=flops // COST_SCALE, bytes_accessed=0, transcendentals=0
        ),
        **settings,
    )


def masked_probs(query, key, valid):
    scores = jnp.where(valid, product(query, key, 1, 1), neg_large)
    expo = jnp.exp((scores - jnp.max(scores, axis=-1, keepdims=True)) * HD ** (-0.5))
    return expo * (1.0 / jnp.sum(expo, axis=-1, keepdims=True))


def valid_keys(length, shift, rows):
    token = lax.broadcasted_iota(jnp.int32, (rows, rows), 1) + shift
    return jnp.where(token < rows, token, token - rows) < length


def attend_kernel(lengths, query, key, value, context):
    rows, features = query.shape
    valid = valid_keys(lengths[pl.program_id(0)], lengths[pl.num_programs(0)], rows)
    for head in range(features // HD):
        at = slice(head * HD, (head + 1) * HD)
        probs = masked_probs(query[:, at], key[:, at], valid)
        context[:, at] = product(probs.astype(low), value[:, at], 1, 0).astype(low)


def attend_back_kernel(lengths, query, key, value, grad, grads):
    rows, features = query.shape
    valid = valid_keys(lengths[pl.program_id(0)], lengths[pl.num_programs(0)], rows)
    for head in range(features // HD):
        at, key_at, value_at = (
            slice(c * features + head * HD, c * features + (head + 1) * HD) for c in range(3)
        )
        probs = masked_probs(query[:, at], key[:, at], valid)
        grads[:, value_at] = product(probs.astype(low), grad[:, at], 0, 0).astype(low)
        prob_grad = product(grad[:, at], value[:, at], 1, 1)
        mean = jnp.sum(prob_grad * probs, axis=-1, keepdims=True)
        score_grad = (probs * (prob_grad - mean)).astype(low)
        grads[:, at] = (product(score_grad, key[:, at], 1, 0) * HD ** (-0.5)).astype(low)
        grads[:, key_at] = (product(score_grad, query[:, at], 0, 0) * HD ** (-0.5)).astype(low)


def by_sequence(kernel, flops, seq_len, lengths, projected, *arrays):
    rows, columns = projected.shape
    features = columns // 3

    def spec(width, block):
        return pl.BlockSpec((seq_len, width), lambda sequence, lengths: (sequence, block))

    size = columns if arrays else features
    return call(
        kernel,
        flops,
        jax.ShapeDtypeStruct((rows, size), low),
        grid_spec=pltpu.PrefetchScalarGridSpec(
            num_scalar_prefetch=1,
            grid=(rows // seq_len,),
            in_specs=[spec(features, c) for c in range(3)] + [spec(features, 0) for a in arrays],
            out_specs=spec(size, 0),
        ),
    )(lengths, projected, projected, projected, *arrays)


def matmul_kernel(right_axis, left, right, *rest):
    total = product(left[...], right[...], 1, right_axis)
    if len(rest) == 2:
        total = total + rest[0][...]
    rest[-1][...] = total.astype(low)


def right_spec(depth, tile, right_axis, start):
    if right_axis:
        return pl.BlockSpec((tile, depth), lambda j: (j, start // depth))
    return pl.BlockSpec((depth, tile), lambda j: (0, start // tile + j))


def column_spec(rows, tile):
    return pl.BlockSpec((rows, tile), lambda j: (0, j))


def matmul(left, right, right_axis, size, start=0, bias=None):
    rows, depth = left.shape
    tile = math.gcd(size, 512 if right_axis or start % 512 == 0 else 256)
    in_specs = [
        pl.BlockSpec((rows, depth), lambda j: (0, 0)),
        right_spec(depth, tile, right_axis, start),
    ]
    operands = [left, right]
    if bias is not None:
        in_specs.append(column_spec(1, tile))
        operands.append(bias[None])
    return call(
        functools.partial(matmul_kernel, right_axis),
        2 * rows * depth * size,
        jax.ShapeDtypeStruct((rows, size), low),
        grid=(size // tile,),
        in_specs=in_specs,
        out_specs=column_spec(rows, tile),
    )(*operands)


def gelu_tanh(values):
    return jnp.tanh((2.0 / math.pi) ** 0.5 * (values + 0.044715 * values * values * values))


def gelu_slope(values):
    tanh = gelu_tanh(values)
    inner = (2.0 / math.pi) ** 0.5 * (1.0 + 3.0 * 0.044715 * values * values)
    return 0.5 * (1.0 + tanh) + 0.5 * values * (1.0 - tanh * tanh) * inner


def up_kernel(rows, weight, bias, pre_act, hidden):
    values = product(rows[...], weight[...], 1, 0) + bias[...]
    pre_act[...] = values
    hidden[...] = (0.5 * values * (1.0 + gelu_tanh(values))).astype(low)


def up_matmul(rows, weight, bias, tile=256):
    count, units = rows.shape[0], bias.shape[0]
    return call(
        up_kernel,
        2 * rows.size * units,
        [
            jax.ShapeDtypeStruct((count, units), wide),
            jax.ShapeDtypeStruct((count, units), low),
        ],
        grid=(units // tile,),
        in_specs=[
            pl.BlockSpec(rows.shape, lambda j: (0, 0)),
            right_spec(rows.shape[1], tile, 0, 0),
            column_spec(1, tile),
        ],
        out_specs=[column_spec(count, tile)] * 2,
    )(rows, weight, bias[None])


def up_back_kernel(grads, weight, slope, pre_grad, bias_grad):
    values = product(grads[...], weight[...], 1, 0) * slope[...].astype(wide)
    rounded = values.astype(low)
    pre_grad[...] = rounded
    bias_grad[...] = jnp.sum(rounded.astype(wide), axis=0, keepdims=True)


def up_back_matmul(grads, weight, slope, tile=256):
    count, units = slope.shape
    return call(
        up_back_kernel,
        2 * grads.size * units,
        [jax.ShapeDtypeStruct((count, units), low), jax.ShapeDtypeStruct((1, units), wide)],
        grid=(units // tile,),
        in_specs=[
            pl.BlockSpec(grads.shape, lambda j: (0, 0)),
            right_spec(grads.shape[1], tile, 0, weight.shape[1] - units),
            column_spec(count, tile),
        ],
        out_specs=[column_spec(count, tile), column_spec(1, tile)],
    )(grads, weight, slope)


def pair_kernel(left_one, right_one, left_two, right_two, total):
    one = product(left_one[...], right_one[...], 0, 0)
    total[...] = (one + product(left_two[...], right_two[...], 0, 0)).astype(low)


def pair_matmul(lefts, rights, tile=256):
    rows, depth = lefts[0].shape
    columns = rights[0].shape[1]
    specs = [column_spec(rows, tile), pl.BlockSpec((rows, columns), lambda j: (0, 0))]
    return call(
        pair_kernel,
        4 * rows * depth * columns,
        jax.ShapeDtypeStruct((depth, columns), low),
        grid=(depth // tile,),
        in_specs=specs * 2,
        out_specs=pl.BlockSpec((tile, columns), lambda j: (j, 0)),
    )(lefts[0], rights[0], lefts[1], rights[1])


def local(
    inputs,
    out_grad,
    lengths,
    dealing,
    qkv_weight,
    qv_bias,
    out_weight,
    out_bias,
    attn_gain,
    attn_shift,
    up_weight,
    up_bias,
    down_weight,
    down_bias,
    ffn_gain,
    ffn_shift,
):
    groups = lax.axis_size("dp")
    ring_size = groups // 4
    index = lax.axis_index("dp")
    core, side, ring = index % 2, (index // 2) % 2, index // 4
    lane = lax.axis_index("tensor")
    core_pairs = [(i, i ^ 1) for i in range(groups)]
    side_pairs = [(i, i ^ 2) for i in range(groups)]
    ring_groups = [[4 * r + offset for r in range(ring_size)] for offset in range(4)]

    def core_swap(array):
        return lax.ppermute(array, "dp", core_pairs)

    def side_swap(array):
        return lax.ppermute(array, "dp", side_pairs)

    def lane_swap(array):
        return lax.ppermute(array, "tensor", [(0, 1), (1, 0)])

    def in_order(bit, mine, theirs, axis):
        first = jnp.where(bit == 0, mine, theirs)
        second = jnp.where(bit == 0, theirs, mine)
        return jnp.concatenate([first, second], axis=axis)

    def parts(array, bit, axis):
        size = array.shape[axis] // 2
        return take(array, bit * size, size, axis), take(array, (1 - bit) * size, size, axis)

    seq_len, half = inputs.shape
    width = 2 * half
    per_peer = seq_len // groups
    shard = width // groups
    token_half = seq_len // 2
    features = half // 4
    units = up_weight.shape[1] // 4

    def split_weight(weight):
        mine, sent = parts(weight, core, 2)
        weight = in_order(core, mine, core_swap(sent), 0)
        mine, sent = parts(weight, side, 2)
        weight = in_order(side, mine, side_swap(sent), 0)
        return weight.reshape(4 * shard, -1)

    def gather_weight(piece):
        return lax.all_gather(piece, "dp", axis=0, axis_index_groups=ring_groups, tiled=True)

    first_weights = jnp.concatenate([qkv_weight, out_weight.T[None]], axis=0).swapaxes(0, 1)
    first_piece = split_weight(first_weights)
    first_full = gather_weight(first_piece)
    second_weights = after(up_weight, first_piece), after(down_weight, first_piece).T
    second_piece = split_weight(jnp.stack(second_weights, axis=1))
    second_full = gather_weight(second_piece)

    local_rows = inputs.reshape(groups, per_peer, half).swapaxes(0, 1)
    sending = jnp.take(local_rows, dealing, axis=1)
    arrived = lax.all_to_all(sending, "dp", split_axis=1, concat_axis=1, tiled=True)
    tokens = after(arrived, first_piece).reshape(seq_len, half)
    early, late = tokens[:token_half], tokens[token_half:]
    early = in_order(lane, early, lane_swap(early), 1)
    early = jnp.stack([early, side_swap(early)])
    late = jnp.stack([late, side_swap(late)])
    late = in_order(lane, late, lane_swap(late), 2)
    own_rows = jnp.stack([jnp.where(lane == 0, early, late), jnp.where(lane == 0, late, early)], 1)
    own_rows = own_rows.reshape(2 * seq_len, width)
    all_rows = (own_rows, core_swap(own_rows))
    residual = own_rows[:token_half]
    grad_keep, grad_send = parts(out_grad, lane, 0)
    cotangent = in_order(lane, grad_keep, lane_swap(grad_send), 1)

    small = jnp.concatenate(
        [
            v.reshape(-1)
            for v in (
                qv_bias,
                up_bias,
                out_bias,
                attn_gain,
                attn_shift,
                down_bias,
                ffn_gain,
                ffn_shift,
            )
        ]
    )[None]
    small = in_order(core, small, core_swap(after(small, first_piece)), 0)
    small = in_order(side, small, side_swap(small), 0)
    small_all = jnp.zeros((groups, small.shape[1]), low)
    for step in range(ring_size):
        if step:
            small = lax.ppermute(small, "dp", [(i, (i + 4) % groups) for i in range(groups)])
        place = ((ring - step) % ring_size) * 4
        small_all = lax.dynamic_update_slice_in_dim(small_all, small, place, 0)
    cut_one = qv_bias.size
    cut_two = cut_one + up_bias.size
    qv_full = (
        small_all[:, :cut_one]
        .reshape((groups,) + qv_bias.shape)
        .transpose(1, 2, 0, 3)
        .reshape(2, half)
    )
    up_bias_full = (
        small_all[:, cut_one:cut_two]
        .reshape((groups,) + up_bias.shape)
        .transpose(1, 0, 2)
        .reshape(-1)
    )
    vectors = (
        small_all[:, cut_two:].reshape(groups, 6, shard).transpose(1, 0, 2).reshape(6, width)
    ).astype(wide)
    out_bias_full, gain_one, shift_one, down_bias_full, gain_two, shift_two = vectors
    place = core * 2 + side
    qv_rows = take(qv_full, place * features, features, 1)
    up_bias_mine = take(up_bias_full, place * units, units, 0)

    def core_parts(left, right, start=0):
        theirs = core_swap(matmul(left[1], right, 1, width, start))
        mine = matmul(left[0], right, 1, width, start)
        return mine, theirs

    def added(both, pick):
        mine, theirs = (pick(array.reshape(2, 2, token_half, width)) for array in both)
        return mine.astype(wide) + theirs.astype(wide)

    def group_sum(both, beside_one=(), beside_two=()):
        one = side_swap(added(both, lambda a: a[1, ..., :half]).astype(low))
        two = lane_swap(added(both, lambda a: a[:, 1, :, half:]).astype(low))
        one = added(both, lambda a: a[0, ..., :half]) + after(one, *beside_one).astype(wide)
        two = added(both, lambda a: a[:, 0, :, half:]) + after(two, *beside_one).astype(wide)
        one = one[0] + after(lane_swap(one[1].astype(low)), *beside_two).astype(wide)
        two = two[0] + after(side_swap(two[1].astype(low)), *beside_two).astype(wide)
        return jnp.concatenate([one, two], axis=1)

    def group_gather(rows, beside_one=(), beside_two=()):
        one, two = rows[:, :half], rows[:, half:]
        one = jnp.stack([one, after(lane_swap(one), *beside_one)])
        two = jnp.stack([two, after(side_swap(two), *beside_one)])
        one = jnp.stack([one, after(side_swap(one), *beside_two)])
        two = jnp.stack([two, after(lane_swap(two), *beside_two)], axis=1)
        own = jnp.concatenate([one, two], axis=3).reshape(2 * seq_len, width)
        return own, core_swap(own)

    sequences = jnp.stack([index, index ^ 2, index ^ 1, index ^ 3])
    group_lengths = jnp.take(lengths, jnp.take(dealing, sequences)).reshape(2, 2)
    group_lengths = jnp.concatenate(
        [group_lengths, jnp.full((2, 1), lane * token_half, jnp.int32)], axis=1
    )
    qkv_bias = jnp.concatenate([qv_rows[0], jnp.zeros_like(qv_rows[0]), qv_rows[1]]).astype(wide)
    flops = 4 * 2 * seq_len * seq_len * features
    all_rows = tuple(after(rows, second_piece) for rows in all_rows)
    projected = [matmul(rows, first_full, 0, 3 * features, bias=qkv_bias) for rows in all_rows]
    context = [
        by_sequence(attend_kernel, 4 * flops, seq_len, group_lengths[i], projected[i])
        for i in range(2)
    ]
    attended = group_sum(core_parts(context, first_full, 3 * features)) + out_bias_full
    first, normed_one, inverse_one = norm_forward(
        residual.astype(wide) + attended, gain_one, shift_one
    )
    first_low = group_gather(first.astype(low))

    pre_act, hidden = zip(
        *[up_matmul(rows, second_full, up_bias_mine.astype(wide)) for rows in first_low], strict=True
    )
    mixed_parts = core_parts(hidden, second_full, units)
    slope = [gelu_slope(after(values, *mixed_parts)).astype(low) for values in pre_act]
    mixed = group_sum(mixed_parts, slope) + down_bias_full
    final, normed_two, inverse_two = norm_forward(first + mixed, gain_two, shift_two)
    second_grad, gain_two_grad, shift_two_grad = norm_backward(
        cotangent.astype(wide), normed_two, inverse_two, gain_two
    )
    mixed_low = second_grad.astype(low)
    down_bias_grad = jnp.sum(mixed_low, axis=0, dtype=wide)
    mixed_grad = group_gather(mixed_low)

    def scatter(partial):
        return lax.psum_scatter(
            partial, "dp", scatter_dimension=0, axis_index_groups=ring_groups, tiled=True
        )

    def join_grad(total, kinds):
        total = total.reshape(4 * shard, kinds, -1)
        mine, sent = parts(total, side, 0)
        total = in_order(side, mine, side_swap(sent), 2)
        mine, sent = parts(total, core, 0)
        return in_order(core, mine, core_swap(sent), 2).astype(wide)

    down_partial = pair_matmul(mixed_grad, hidden)
    down_sum = scatter(down_partial)
    pre_grad, up_bias_grad = zip(
        *[
            up_back_matmul(after(mixed_grad[i], down_partial), second_full, slope[i])
            for i in range(2)
        ],
        strict=True,
    )
    both = core_parts(pre_grad, second_full)
    up_partial = pair_matmul(first_low, [after(grads, *both) for grads in pre_grad])
    up_sum = scatter(up_partial)
    first_grad = second_grad + group_sum(both, [up_partial], [down_sum])
    attn_total_grad, gain_one_grad, shift_one_grad = norm_backward(
        first_grad, normed_one, inverse_one, gain_one
    )
    attended_low = attn_total_grad.astype(low)
    out_bias_grad = jnp.sum(attended_low, axis=0, dtype=wide)
    attended_grad = group_gather(attended_low)
    out_partial = pair_matmul(attended_grad, context)
    out_sum = scatter(out_partial)
    context_grad = [
        matmul(after(rows, out_partial), first_full, 0, features, 3 * features)
        for rows in attended_grad
    ]
    stacked = [
        by_sequence(
            attend_back_kernel,
            8 * flops,
            seq_len,
            group_lengths[i],
            projected[i],
            context_grad[i],
        )
        for i in range(2)
    ]
    both = core_parts((stacked[0], after(stacked[1], up_sum)), first_full)
    own_part = sum(array.astype(wide) for array in both).astype(low)
    own_part = own_part.reshape(2, 2, token_half, width)
    early, late = (
        jnp.where(lane == bit, own_part[:, 0], own_part[:, 1]) for bit in range(2)
    )
    early_sent = early[1]
    late, late_sent = parts(late, lane, 2)
    qkv_partial = pair_matmul(all_rows, [after(g, early_sent, late_sent) for g in stacked])
    qkv_sum = scatter(qkv_partial)
    early = early[0].astype(wide) + side_swap(early_sent).astype(wide)
    late = late.astype(wide) + after(lane_swap(late_sent), qkv_partial).astype(wide)
    early, early_sent = parts(early, lane, 1)
    early_sent, late_sent = early_sent.astype(low), late[1].astype(low)
    early = early + lane_swap(early_sent).astype(wide)
    late = late[0] + side_swap(late_sent).astype(wide)
    own_attended = take(attended_grad[0][:seq_len], lane * half, half, 1)
    own_attended = in_order(lane, own_attended[:token_half], own_attended[token_half:], 0)
    in_half = (jnp.concatenate([early, late], axis=0) + own_attended.astype(wide)).astype(low)
    qkv_bias_sum = sum(jnp.sum(after(s, early_sent), axis=0, dtype=wide) for s in stacked)
    qkv_bias_sum = qkv_bias_sum.reshape(3, features)
    qv_grad = jnp.stack([qkv_bias_sum[0], qkv_bias_sum[2]])
    out_keep, out_send = parts(final.astype(low), lane, 1)
    outputs = in_order(lane, out_keep, lane_swap(after(out_send, early_sent)), 0)

    back_rows = in_half.reshape(per_peer, groups, half)
    returned = lax.all_to_all(back_rows, "dp", split_axis=1, concat_axis=1, tiled=True)
    inverse_order = (
        jnp.zeros((groups,), jnp.int32).at[dealing].set(jnp.arange(groups, dtype=jnp.int32))
    )
    in_grad = jnp.take(returned, inverse_order, axis=1).swapaxes(0, 1).reshape(seq_len, half)

    down_weight_grad = join_grad(after(down_sum, qkv_partial), 1)[:, 0].T
    up_weight_grad = join_grad(after(up_sum, qkv_partial), 1)[:, 0]
    out_weight_grad = join_grad(after(out_sum, early_sent), 1)[:, 0].T
    qkv_grad = join_grad(qkv_sum, 3).swapaxes(0, 1)

    def spread(mine, size):
        full = jnp.zeros(mine.shape[:-1] + (4 * size,), wide)
        return lax.dynamic_update_slice_in_dim(full, mine, place * size, mine.ndim - 1)

    qv_spread = (
        spread(qv_grad, features)
        .reshape(2, qv_bias.shape[1], groups, qv_bias.shape[2])
        .transpose(2, 0, 1, 3)
        .reshape(groups, -1)
    )
    up_spread = (
        spread((up_bias_grad[0] + up_bias_grad[1])[0], units)
        .reshape(up_bias.shape[0], groups, up_bias.shape[1])
        .transpose(1, 0, 2)
        .reshape(groups, -1)
    )
    vector_spread = (
        jnp.stack(
            [
                out_bias_grad,
                gain_one_grad,
                shift_one_grad,
                down_bias_grad,
                gain_two_grad,
                shift_two_grad,
            ]
        )
        .reshape(6, groups, shard)
        .transpose(1, 0, 2)
        .reshape(groups, -1)
    )
    packed = jnp.concatenate([qv_spread, up_spread, vector_spread], axis=1)
    exchanged = lax.all_to_all(packed, "dp", split_axis=0, concat_axis=0, tiled=True)
    small_sum = jnp.sum(exchanged, axis=0)
    vector_sum = small_sum[cut_two:]
    vector_sum = (vector_sum + lane_swap(vector_sum)).reshape(6, shard)
    return (
        outputs,
        in_grad,
        qkv_grad,
        small_sum[:cut_one].reshape(qv_bias.shape),
        out_weight_grad,
        vector_sum[0],
        vector_sum[1],
        vector_sum[2],
        up_weight_grad,
        small_sum[cut_one:cut_two].reshape(up_bias.shape),
        down_weight_grad,
        vector_sum[3],
        vector_sum[4],
        vector_sum[5],
    )


def solution(mesh):
    placed = (
        P("dp", "tensor"),
        P("dp", "tensor"),
        P(),
        P(),
        P(None, "dp", "tensor"),
        P(None, "tensor", "dp"),
        P("tensor", "dp"),
        P("dp"),
        P("dp"),
        P("dp"),
        P("dp", "tensor"),
        P("tensor", "dp"),
        P("tensor", "dp"),
        P("dp"),
        P("dp"),
        P("dp"),
    )
    return jax.shard_map(
        local,
        mesh=mesh,
        in_specs=placed,
        out_specs=(
            P("dp", "tensor"),
            P("dp", "tensor"),
            P(None, "dp", "tensor"),
            P(None, "tensor", "dp"),
            P("tensor", "dp"),
            P("dp"),
            P("dp"),
            P("dp"),
            P("dp", "tensor"),
            P("tensor", "dp"),
            P("tensor", "dp"),
            P("dp"),
            P("dp"),
            P("dp"),
        ),
        check_vma=False,
    )
```

time: 1090 us -> 784 us (0.72)
  waiting for transfers between devices: 536 us -> 360 us
  matrix products: 154 us -> 0 us
  Pallas kernels: 0 us -> 150 us
  local copies, waits for them, and re-layouts: 164 us -> 93.6 us
  starting transfers between devices: 98.9 us -> 65.8 us
  blocking collectives: 31.1 us -> 0 us
  between operations: 3.39 us -> 16.5 us
    ppermute x24 -> x3, waiting for transfers between devices: 206 us -> 16.5 us  [local(): lax.ppermute(small, 'dp', [(i, (i + 4) % groups) for i in range(groups)])]
    dot_general x30 -> x0, matrix products: 154 us -> none  [the longest x12 43.2 us: dot_ta(): return jnp.einsum('la,lb->ab', left, right, preferred_element_type=wide)]
    pallas_call x0 -> x24, Pallas kernels: none -> 150 us  [the longest x12 61.3 us: matmul(): call(functools.partial(matmul_kernel, right_axis), 2 * rows * depth * siz...]
    convert_element_type x33 -> x9, local copies, waits for them, and re-layouts: 50.2 us -> 7.25 us  [the longest x3 2.01 us: group_sum(): two[1].astype(low)]
    all_gather x0 -> x2, waiting for transfers between devices: none -> 40.1 us  [gather_weight(): lax.all_gather(piece, 'dp', axis=0, axis_index_groups=ring_groups, tiled=...]
    all_gather x1 -> x0, blocking collectives: 31.1 us -> none  [local(): small_all = lax.all_gather(small, 'dp', axis=0, tiled=False)]
    dynamic_update_slice x31 -> x4, local copies, waits for them, and re-layouts: 31.2 us -> 0.35 us  [the longest x1 0.3 us: spread(): lax.dynamic_update_slice_in_dim(full, mine, place * size, mine.ndim - 1)]
    ppermute x11 -> x19, waiting for transfers between devices: 65.7 us -> 88.6 us  [lane_swap(): return lax.ppermute(array, 'tensor', [(0, 1), (1, 0)])]
  transfers between devices with their start and end apart: 86 -> 69, of which waited for: 41 -> 40; matrix products, arithmetic and copies ran while one was open for 15% -> 17% of each run, Pallas kernels for 0% -> 13%
where the time goes in v2:
time: 784 us; the launch traced here: 775 us
  waiting for transfers between devices  360 us (46%)
  Pallas kernels  150 us (19%)
  local copies, waits for them, and re-layouts  93.6 us (12%)
  other arithmetic  88.7 us (11%)
  starting transfers between devices  65.8 us (8%)
  between operations  16.5 us (2%)
    ppermute x23, waiting for transfers between devices, side_swap(): return lax.ppermute(array, 'dp', side_pairs)  194 us
    ppermute x19, waiting for transfers between devices, lane_swap(): return lax.ppermute(array, 'tensor', [(0, 1), (1, 0)])  88.6 us
    pallas_call x12, Pallas kernels, matmul(): call(functools.partial(matmul_kernel, right_axis), 2 * rows * depth * siz...  61.3 us
    unnamed x185, local copies, waits for them, and re-layouts  49.9 us
    all_gather x2, waiting for transfers between devices, gather_weight(): lax.all_gather(piece, 'dp', axis=0, axis_index_groups=ring_groups, tiled=...  40.1 us
    pallas_call x4, Pallas kernels, pair_matmul(): call(pair_kernel, 4 * rows * depth * columns, jax.ShapeDtypeStruct((depth...  39.4 us
    ppermute x23, starting transfers between devices, side_swap(): return lax.ppermute(array, 'dp', side_pairs)  28.9 us
    ppermute x15, waiting for transfers between devices, core_swap(): return lax.ppermute(array, 'dp', core_pairs)  21.1 us
  transfers between devices with their start and end apart: 69, of which 40 were waited for; matrix products, arithmetic and copies ran while one was open for 17% of the time, Pallas kernels for 13%

profile of v2, /device:TPU:0, one launch (start us, length us, event | category | flops | bytes accessed | tf_op | source)
XLA Modules:
  0.0 774.8 jit_solution(14357487919200438634)
XLA Ops:
  10.4 7.4 all-to-all-start
  23.5 19.9 %collective-permute-done.1 = bf16[256,4,256]{2,0,1:T(8,128)(2,1)S(1)} collective-permute-done((bf16[256,4,256]{2,0,1:T(8,128)(2,1)S(1)}, bf16[256,4,256]{2,0,1:T(8,128)(2,1)S(1)}, u32[]{:S(2)}, u32[]{:S(2)}) %collective-permute-start.1) | collective-permute-done | bytes 524320 | tf_op jit(solution)/shard_map/ppermute | solution.py:267
  49.2 10.1 %collective-permute-done.4 = bf16[256,1024]{1,0:T(8,128)(2,1)S(1)} collective-permute-done((bf16[256,1024]{1,0:T(8,128)(2,1)S(1)}, bf16[256,1024]{1,0:T(8,128)(2,1)S(1)}, u32[]{:S(2)}, u32[]{:S(2)}) %collective-permute-start.4) | collective-permute-done | bytes 524320 | tf_op jit(solution)/shard_map/ppermute | solution.py:267
  67.8 17.3 %collective-permute-done.5 = bf16[2,256,1024]{2,1,0:T(8,128)(2,1)S(1)} collective-permute-done((bf16[2,256,1024]{2,1,0:T(8,128)(2,1)}, bf16[2,256,1024]{2,1,0:T(8,128)(2,1)S(1)}, u32[]{:S(2)}, u32[]{:S(2)}) %collective-permute-start.5) | collective-permute-done | bytes 1048608 | tf_op jit(solution)/shard_map/ppermute | solution.py:270
  169.9 23.8 %collective-permute-done.15 = bf16[2,256,1024]{2,1,0:T(8,128)(2,1)S(1)} collective-permute-done((bf16[2,256,1024]{2,1,0:T(8,128)(2,1)S(1)}, bf16[2,256,1024]{2,1,0:T(8,128)(2,1)S(1)}, u32[]{:S(2)}, u32[]{:S(2)}) %collective-permute-start.15) | collective-permute-done | bytes 1048608 | tf_op jit(solution)/shard_map/ppermute | solution.py:267
  200.7 11.7 %collective-permute-done.18 = bf16[256,1024]{1,0:T(8,128)(2,1)} collective-permute-done((bf16[256,1024]{1,0:T(8,128)(2,1)}, bf16[256,1024]{1,0:T(8,128)(2,1)}, u32[]{:S(2)}, u32[]{:S(2)}) %collective-permute-start.18) | collective-permute-done | bytes 524320 | tf_op jit(solution)/shard_map/ppermute | solution.py:267
  219.9 11.0 %collective-permute-done.21 = bf16[256,1024]{1,0:T(8,128)(2,1)S(1)} collective-permute-done((bf16[256,1024]{1,0:T(8,128)(2,1)S(1)}, bf16[256,1024]{1,0:T(8,128)(2,1)S(1)}, u32[]{:S(2)}, u32[]{:S(2)}) %collective-permute-start.21) | collective-permute-done | bytes 524320 | tf_op jit(solution)/shard_map/ppermute | solution.py:267
  233.3 20.7 %collective-permute-done.22 = bf16[2,256,1024]{2,1,0:T(8,128)(2,1)S(1)} collective-permute-done((bf16[2,256,1024]{2,1,0:T(8,128)(2,1)S(1)}, bf16[2,256,1024]{2,1,0:T(8,128)(2,1)S(1)}, u32[]{:S(2)}, u32[]{:S(2)}) %collective-permute-start.22) | collective-permute-done | bytes 1048608 | tf_op jit(solution)/shard_map/ppermute | solution.py:270
  257.9 40.1 %all-gather.5.cloned.1.call-done.weight.right = bf16[2048,2048]{1,0:T(8,128)(2,1)} async-done(((bf16[512,2048]{1,0:T(8,128)(2,1)}), bf16[2048,2048]{1,0:T(8,128)(2,1)}) %all-gather.5.cloned.1.call-update) | async-done | bytes 8388624 | tf_op jit(solution)/shard_map/all_gather | solution.py:297
  298.0 8.8 %shard_map.271 = (f32[1024,1024]{1,0:T(8,128)S(1)}, bf16[1024,1024]{1,0:T(8,128)(2,1)S(1)}) custom-call(bf16[1024,2048]{1,0:T(8,128)(2,1)} %collective-permute-done.23.rows.left_two, bf16[2048,2048]{1,0:T(8,128)(2,1)} %all-gather.5.cloned.1.call-done.weight.right, f32[1,1024]{1,0:T(1,128)S(1)} %bitcast.331), custom_call_target="tpu_custom_call" | custom-call | flops 536870912 | tf_op jit(solution)/shard_map/pallas_call | solution.py:177
  308.7 8.6 %shard_map.272 = bf16[1024,2048]{1,0:T(8,128)(2,1)} custom-call(bf16[1024,1024]{1,0:T(8,128)(2,1)S(1)} %get-tuple-element.61.left.right_two, bf16[2048,2048]{1,0:T(8,128)(2,1)} %all-gather.5.cloned.1.call-done.weight.right), custom_call_target="tpu_custom_call" | custom-call | flops 536870912 | tf_op jit(solution)/shard_map/pallas_call | solution.py:149
  320.8 9.2 %shard_map.269 = (f32[1024,1024]{1,0:T(8,128)S(1)}, bf16[1024,1024]{1,0:T(8,128)(2,1)S(1)}) custom-call(bf16[1024,2048]{1,0:T(8,128)(2,1)} %bitcast.52.rows.left_one, bf16[2048,2048]{1,0:T(8,128)(2,1)} %all-gather.5.cloned.1.call-done.weight.right, f32[1,1024]{1,0:T(1,128)S(1)} %bitcast.332), custom_call_target="tpu_custom_call" | custom-call | flops 536870912 | tf_op jit(solution)/shard_map/pallas_call | solution.py:177
  349.0 16.2 %collective-permute-done.25 = bf16[2,256,1024]{2,1,0:T(8,128)(2,1)S(1)} collective-permute-done((bf16[2,256,1024]{2,1,0:T(8,128)(2,1)S(1)}, bf16[2,256,1024]{2,1,0:T(8,128)(2,1)S(1)}, u32[]{:S(2)}, u32[]{:S(2)}) %collective-permute-start.25) | collective-permute-done | bytes 1048608 | tf_op jit(solution)/shard_map/ppermute | solution.py:267
  372.1 10.3 %collective-permute-done.28 = bf16[256,1024]{1,0:T(8,128)(2,1)S(1)} collective-permute-done((bf16[256,1024]{1,0:T(8,128)(2,1)S(1)}, bf16[256,1024]{1,0:T(8,128)(2,1)S(1)}, u32[]{:S(2)}, u32[]{:S(2)}) %collective-permute-start.28) | collective-permute-done | bytes 524320 | tf_op jit(solution)/shard_map/ppermute | solution.py:267
  388.2 9.7 %collective-permute-done.32 = bf16[256,1024]{1,0:T(8,128)(2,1)S(1)} collective-permute-done((bf16[256,1024]{1,0:T(8,128)(2,1)S(1)}, bf16[256,1024]{1,0:T(8,128)(2,1)S(1)}, u32[]{:S(2)}, u32[]{:S(2)}) %collective-permute-start.32) | collective-permute-done | bytes 524320 | tf_op jit(solution)/shard_map/ppermute | solution.py:267
  400.5 21.0 %collective-permute-done.33 = bf16[2,256,1024]{2,1,0:T(8,128)(2,1)S(1)} collective-permute-done((bf16[2,256,1024]{2,1,0:T(8,128)(2,1)S(1)}, bf16[2,256,1024]{2,1,0:T(8,128)(2,1)S(1)}, u32[]{:S(2)}, u32[]{:S(2)}) %collective-permute-start.33) | collective-permute-done | bytes 1048608 | tf_op jit(solution)/shard_map/ppermute | solution.py:270
  422.5 7.1 collective-permute-done.34.left_two.grads
  431.6 11.8 %shard_map.273 = bf16[2048,1024]{1,0:T(8,128)(2,1)S(1)} custom-call(bf16[1024,2048]{1,0:T(8,128)(2,1)S(1)} %bitcast.320, bf16[1024,1024]{1,0:T(8,128)(2,1)S(1)} %get-tuple-element.60.left.right_one, bf16[1024,2048]{1,0:T(8,128)(2,1)} %copy-done.18, bf16[1024,1024]{1,0:T(8,128)(2,1)S(1)} %copy-done.28), custom_call_target="tpu_custom_call" | custom-call | flops 1073741824 | tf_op jit(solution)/shard_map/pallas_call | solution.py:226
  451.6 6.7 shard_map.276
  458.4 8.0 %shard_map.277 = bf16[1024,2048]{1,0:T(8,128)(2,1)} custom-call(bf16[1024,1024]{1,0:T(8,128)(2,1)S(1)} %get-tuple-element.73.left.right_two, bf16[2048,2048]{1,0:T(8,128)(2,1)} %all-gather.5.cloned.1.call-done.weight.right), custom_call_target="tpu_custom_call" | custom-call | flops 536870912 | tf_op jit(solution)/shard_map/pallas_call | solution.py:149
  466.5 6.7 shard_map.274
  473.2 6.7 shard_map.275
  487.8 11.7 %shard_map.278 = bf16[2048,1024]{1,0:T(8,128)(2,1)S(1)} custom-call(bf16[1024,2048]{1,0:T(8,128)(2,1)} %bitcast.52.rows.left_one, bf16[1024,1024]{1,0:T(8,128)(2,1)S(1)} %get-tuple-element.72.left.right_one, bf16[1024,2048]{1,0:T(8,128)(2,1)} %collective-permute-done.23.rows.left_two, bf16[1024,1024]{1,0:T(8,128)(2,1)S(1)} %get-tuple-element.73.left.right_two), custom_call_target="tpu_custom_call" | custom-call | flops 1073741824 | tf_op jit(solution)/shard_map/pallas_call | solution.py:226
  501.6 7.5 collective-permute-done.36
  520.2 10.5 %collective-permute-done.39 = bf16[256,1024]{1,0:T(8,128)(2,1)} collective-permute-done((bf16[256,1024]{1,0:T(8,128)(2,1)}, bf16[256,1024]{1,0:T(8,128)(2,1)}, u32[]{:S(2)}, u32[]{:S(2)}) %collective-permute-start.39) | collective-permute-done | bytes 524320 | tf_op jit(solution)/shard_map/ppermute | solution.py:267
  541.1 10.2 %collective-permute-done.42 = bf16[256,1024]{1,0:T(8,128)(2,1)S(1)} collective-permute-done((bf16[256,1024]{1,0:T(8,128)(2,1)S(1)}, bf16[256,1024]{1,0:T(8,128)(2,1)S(1)}, u32[]{:S(2)}, u32[]{:S(2)}) %collective-permute-start.42) | collective-permute-done | bytes 524320 | tf_op jit(solution)/shard_map/ppermute | solution.py:267
  553.3 21.7 %collective-permute-done.43 = bf16[2,256,1024]{2,1,0:T(8,128)(2,1)S(1)} collective-permute-done((bf16[2,256,1024]{2,1,0:T(8,128)(2,1)S(1)}, bf16[2,256,1024]{2,1,0:T(8,128)(2,1)S(1)}, u32[]{:S(2)}, u32[]{:S(2)}) %collective-permute-start.43) | collective-permute-done | bytes 1048608 | tf_op jit(solution)/shard_map/ppermute | solution.py:270
  578.1 7.2 collective-permute-done.44.left_two.left
  640.7 10.0 %shard_map.286 = bf16[2048,768]{1,0:T(8,128)(2,1)S(1)} custom-call(bf16[1024,2048]{1,0:T(8,128)(2,1)} %bitcast.16.left.left_one, bf16[1024,768]{1,0:T(8,128)(2,1)S(1)} %shard_map.281.left.right_one, bf16[1024,2048]{1,0:T(8,128)(2,1)} %collective-permute-done.13.left.left_two, bf16[1024,768]{1,0:T(8,128)(2,1)S(1)} %copy-done.16), custom_call_target="tpu_custom_call" | custom-call | flops 805306368 | tf_op jit(solution)/shard_map/pallas_call | solution.py:226
  669.3 11.2 %collective-permute-done.56 = bf16[256,1,1024]{2,0,1:T(8,128)(2,1)} collective-permute-done((bf16[256,1,1024]{2,0,1:T(8,128)(2,1)}, bf16[256,1,1024]{2,0,1:T(8,128)(2,1)}, u32[]{:S(2)}, u32[]{:S(2)}) %collective-permute-start.56) | collective-permute-done | bytes 524320 | tf_op jit(solution)/shard_map/ppermute | solution.py:267
  684.9 17.7 %collective-permute-done.46 = bf16[256,2048]{1,0:T(8,128)(2,1)} collective-permute-done((bf16[256,2048]{1,0:T(8,128)(2,1)}, bf16[256,2048]{1,0:T(8,128)(2,1)}, u32[]{:S(2)}, u32[]{:S(2)}) %collective-permute-start.46) | collective-permute-done | bytes 1048608 | tf_op jit(solution)/shard_map/ppermute | solution.py:267
  747.9 12.8 %collective-permute-done.51 = bf16[256,3,256]{0,2,1:T(8,128)(2,1)} collective-permute-done((bf16[256,3,256]{0,2,1:T(8,128)(2,1)}, bf16[256,3,256]{0,2,1:T(8,128)(2,1)}, u32[]{:S(2)}, u32[]{:S(2)}) %collective-permute-start.51) | collective-permute-done | bytes 393248 | tf_op jit(solution)/shard_map/ppermute | solution.py:267
  (515 shorter events, 344.9 us)
Async XLA Ops:
  10.4 34.4 %all-to-all-start = ((bf16[32,16,1024]{2,0,1:T(8,128)(2,1)}), bf16[32,16,1024]{2,0,1:T(8,128)(2,1)S(1)}, u32[]{:S(2)}, u32[]{:S(2)}) async-start(bf16[32,16,1024]{2,0,1:T(8,128)(2,1)} %select_bitcast_fusion), calls=%async_computation | async-start | bytes 2097152 | tf_op jit(solution)/shard_map/all_to_all | solution.py:308
  17.8 116.9 %all-gather.3.cloned.1.call-start = ((), (), s32[]{:S(2)}) async-start(), calls=%async_computation.7 | async-start | bytes 5242880 | tf_op jit(solution)/shard_map/all_gather | solution.py:297
  21.5 21.9 %collective-permute-start.1 = (bf16[256,4,256]{2,0,1:T(8,128)(2,1)S(1)}, bf16[256,4,256]{2,0,1:T(8,128)(2,1)S(1)}, u32[]{:S(2)}, u32[]{:S(2)}) collective-permute-start(bf16[256,4,256]{2,0,1:T(8,128)(2,1)S(1)} %fusion.57), channel_id=1, source_target_pairs={{0,4},{2,6},{4,0},{6,2},{8,12},{10,14},{12,8},{14,10},{16,20},{18,... | collective-permute-start | bytes 1572872 | tf_op jit(solution)/shard_map/ppermute | solution.py:267
  49.2 248.8 %all-gather.5.cloned.1.call-start = ((), (), s32[]{:S(2)}) async-start(), calls=%async_computation.8 | async-start | bytes 10485760 | tf_op jit(solution)/shard_map/all_gather | solution.py:297
  60.4 24.7 %collective-permute-start.5 = (bf16[2,256,1024]{2,1,0:T(8,128)(2,1)}, bf16[2,256,1024]{2,1,0:T(8,128)(2,1)S(1)}, u32[]{:S(2)}, u32[]{:S(2)}) collective-permute-start(bf16[2,256,1024]{2,1,0:T(8,128)(2,1)} %pad_maximum_fusion.5), channel_id=1, source_target_pairs={{0,1},{1,0},{2,3},{3,2},{4,5},{5,4},{6,7},{7,6},{8,9},{9,8},{10,11... | collective-permute-start | bytes 3145736 | tf_op jit(solution)/shard_map/ppermute | solution.py:270
  63.3 24.5 %collective-permute-start.3 = (bf16[256,2048]{1,0:T(8,128)(2,1)}, bf16[256,2048]{1,0:T(8,128)(2,1)}, u32[]{:S(2)}, u32[]{:S(2)}) collective-permute-start(bf16[256,2048]{1,0:T(8,128)(2,1)} %get-tuple-element.243), channel_id=1, source_target_pairs={{0,4},{2,6},{4,0},{6,2},{8,12},{10,14},{12,8},{14,10},{16,20},{18,... | collective-permute-start | bytes 3145736 | tf_op jit(solution)/shard_map/ppermute | solution.py:267
  92.7 42.0 %collective-permute-start.13 = (bf16[1024,2048]{1,0:T(8,128)(2,1)}, bf16[1024,2048]{1,0:T(8,128)(2,1)}, u32[]{:S(2)}, u32[]{:S(2)}) collective-permute-start(bf16[1024,2048]{1,0:T(8,128)(2,1)} %bitcast.16.left.left_one), channel_id=1, source_target_pairs={{0,2},{2,0},{4,6},{6,4},{8,10},{10,8},{12,14},{14,12},{16,18},{18,... | collective-permute-start | bytes 12582920 | tf_op jit(solution)/shard_map/ppermute | solution.py:264
  105.8 24.5 %collective-permute-start.7 = (bf16[256,2,1024]{0,2,1:T(8,128)(2,1)S(1)}, bf16[256,2,1024]{0,2,1:T(8,128)(2,1)}, u32[]{:S(2)}, u32[]{:S(2)}) collective-permute-start(bf16[256,2,1024]{0,2,1:T(8,128)(2,1)S(1)} %fusion.31), channel_id=1, source_target_pairs={{0,4},{2,6},{4,0},{6,2},{8,12},{10,14},{12,8},{14,10},{16,20},{18,... | collective-permute-start | bytes 3145736 | tf_op jit(solution)/shard_map/ppermute | solution.py:267
  150.3 380.4 %reduce-scatter.5.cloned.1.call-start = ((), (), s32[]{:S(2)}) async-start(), calls=%async_computation.9 | async-start | bytes 5242880 | tf_op jit(solution)/shard_map/reduce_scatter | solution.py:428
  168.0 25.7 %collective-permute-start.15 = (bf16[2,256,1024]{2,1,0:T(8,128)(2,1)S(1)}, bf16[2,256,1024]{2,1,0:T(8,128)(2,1)S(1)}, u32[]{:S(2)}, u32[]{:S(2)}) collective-permute-start(bf16[2,256,1024]{2,1,0:T(8,128)(2,1)S(1)} %fusion.25), channel_id=1, source_target_pairs={{0,4},{2,6},{4,0},{6,2},{8,12},{10,14},{12,8},{14,10},{16,20},{18,... | collective-permute-start | bytes 3145736 | tf_op jit(solution)/shard_map/ppermute | solution.py:267
  169.4 25.3 %collective-permute-start.17 = (bf16[2,256,1024]{2,1,0:T(8,128)(2,1)S(1)}, bf16[2,256,1024]{2,1,0:T(8,128)(2,1)S(1)}, u32[]{:S(2)}, u32[]{:S(2)}) collective-permute-start(bf16[2,256,1024]{2,1,0:T(8,128)(2,1)S(1)} %fusion.26), channel_id=1, source_target_pairs={{0,1},{1,0},{2,3},{3,2},{4,5},{5,4},{6,7},{7,6},{8,9},{9,8},{10,11... | collective-permute-start | bytes 3145736 | tf_op jit(solution)/shard_map/ppermute | solution.py:270
  231.0 23.0 %collective-permute-start.22 = (bf16[2,256,1024]{2,1,0:T(8,128)(2,1)S(1)}, bf16[2,256,1024]{2,1,0:T(8,128)(2,1)S(1)}, u32[]{:S(2)}, u32[]{:S(2)}) collective-permute-start(bf16[2,256,1024]{2,1,0:T(8,128)(2,1)S(1)} %get-tuple-element.241), channel_id=1, source_target_pairs={{0,1},{1,0},{2,3},{3,2},{4,5},{5,4},{6,7},{7,6},{8,9},{9,8},{10,11... | collective-permute-start | bytes 3145736 | tf_op jit(solution)/shard_map/ppermute | solution.py:270
  231.6 22.6 %collective-permute-start.20 = (bf16[2,256,1024]{2,1,0:T(8,128)(2,1)S(1)}, bf16[2,256,1024]{2,1,0:T(8,128)(2,1)S(1)}, u32[]{:S(2)}, u32[]{:S(2)}) collective-permute-start(bf16[2,256,1024]{2,1,0:T(8,128)(2,1)S(1)} %get-tuple-element.235), channel_id=1, source_target_pairs={{0,4},{2,6},{4,0},{6,2},{8,12},{10,14},{12,8},{14,10},{16,20},{18,... | collective-permute-start | bytes 3145736 | tf_op jit(solution)/shard_map/ppermute | solution.py:267
  257.0 41.0 %collective-permute-start.23 = (bf16[1024,2048]{1,0:T(8,128)(2,1)}, bf16[1024,2048]{1,0:T(8,128)(2,1)}, u32[]{:S(2)}, u32[]{:S(2)}) collective-permute-start(bf16[1024,2048]{1,0:T(8,128)(2,1)} %bitcast.52.rows.left_one), channel_id=1, source_target_pairs={{0,2},{2,0},{4,6},{6,4},{8,10},{10,8},{12,14},{14,12},{16,18},{18,... | collective-permute-start | bytes 12582920 | tf_op jit(solution)/shard_map/ppermute | solution.py:264
  319.3 51.5 %collective-permute-start.29 = (bf16[256,1024]{1,0:T(8,128)(2,1)}, bf16[256,1024]{1,0:T(8,128)(2,1)}, u32[]{:S(2)}, u32[]{:S(2)}) collective-permute-start(bf16[256,1024]{1,0:T(8,128)(2,1)} %constant_dynamic-slice_fusion.1), channel_id=1, source_target_pairs={{0,1},{1,0},{2,3},{3,2},{4,5},{5,4},{6,7},{7,6},{8,9},{9,8},{10,11... | collective-permute-start | bytes 1572872 | tf_op jit(solution)/shard_map/ppermute | solution.py:270
  340.0 25.3 %collective-permute-start.25 = (bf16[2,256,1024]{2,1,0:T(8,128)(2,1)S(1)}, bf16[2,256,1024]{2,1,0:T(8,128)(2,1)S(1)}, u32[]{:S(2)}, u32[]{:S(2)}) collective-permute-start(bf16[2,256,1024]{2,1,0:T(8,128)(2,1)S(1)} %fusion.27), channel_id=1, source_target_pairs={{0,4},{2,6},{4,0},{6,2},{8,12},{10,14},{12,8},{14,10},{16,20},{18,... | collective-permute-start | bytes 3145736 | tf_op jit(solution)/shard_map/ppermute | solution.py:267
  341.5 25.0 %collective-permute-start.27 = (bf16[2,256,1024]{2,1,0:T(8,128)(2,1)S(1)}, bf16[2,256,1024]{2,1,0:T(8,128)(2,1)S(1)}, u32[]{:S(2)}, u32[]{:S(2)}) collective-permute-start(bf16[2,256,1024]{2,1,0:T(8,128)(2,1)S(1)} %fusion.28), channel_id=1, source_target_pairs={{0,1},{1,0},{2,3},{3,2},{4,5},{5,4},{6,7},{7,6},{8,9},{9,8},{10,11... | collective-permute-start | bytes 3145736 | tf_op jit(solution)/shard_map/ppermute | solution.py:270
  398.1 23.4 %collective-permute-start.33 = (bf16[2,256,1024]{2,1,0:T(8,128)(2,1)S(1)}, bf16[2,256,1024]{2,1,0:T(8,128)(2,1)S(1)}, u32[]{:S(2)}, u32[]{:S(2)}) collective-permute-start(bf16[2,256,1024]{2,1,0:T(8,128)(2,1)S(1)} %get-tuple-element.233), channel_id=1, source_target_pairs={{0,1},{1,0},{2,3},{3,2},{4,5},{5,4},{6,7},{7,6},{8,9},{9,8},{10,11... | collective-permute-start | bytes 3145736 | tf_op jit(solution)/shard_map/ppermute | solution.py:270
  447.5 160.1 %reduce-scatter.7.cloned.1.call-start = ((), (), s32[]{:S(2)}) async-start(), calls=%async_computation.10 | async-start | bytes 5242880 | tf_op jit(solution)/shard_map/reduce_scatter | solution.py:428
  483.3 25.8 %collective-permute-start.36 = (bf16[2,256,1024]{2,1,0:T(8,128)(2,1)}, bf16[2,256,1024]{2,1,0:T(8,128)(2,1)}, u32[]{:S(2)}, u32[]{:S(2)}) collective-permute-start(bf16[2,256,1024]{2,1,0:T(8,128)(2,1)} %fusion.29), channel_id=1, source_target_pairs={{0,4},{2,6},{4,0},{6,2},{8,12},{10,14},{12,8},{14,10},{16,20},{18,... | collective-permute-start | bytes 3145736 | tf_op jit(solution)/shard_map/ppermute | solution.py:267
  486.7 25.5 %collective-permute-start.38 = (bf16[2,256,1024]{2,1,0:T(8,128)(2,1)}, bf16[2,256,1024]{2,1,0:T(8,128)(2,1)}, u32[]{:S(2)}, u32[]{:S(2)}) collective-permute-start(bf16[2,256,1024]{2,1,0:T(8,128)(2,1)} %fusion.30), channel_id=1, source_target_pairs={{0,1},{1,0},{2,3},{3,2},{4,5},{5,4},{6,7},{7,6},{8,9},{9,8},{10,11... | collective-permute-start | bytes 3145736 | tf_op jit(solution)/shard_map/ppermute | solution.py:270
  520.2 196.2 %reduce-scatter.11.cloned.1.call-start = ((), (), s32[]{:S(2)}) async-start(), calls=%async_computation.12 | async-start | bytes 1310720 | tf_op jit(solution)/shard_map/reduce_scatter | solution.py:428
  551.4 23.7 %collective-permute-start.43 = (bf16[2,256,1024]{2,1,0:T(8,128)(2,1)S(1)}, bf16[2,256,1024]{2,1,0:T(8,128)(2,1)S(1)}, u32[]{:S(2)}, u32[]{:S(2)}) collective-permute-start(bf16[2,256,1024]{2,1,0:T(8,128)(2,1)S(1)} %get-tuple-element.225), channel_id=1, source_target_pairs={{0,1},{1,0},{2,3},{3,2},{4,5},{5,4},{6,7},{7,6},{8,9},{9,8},{10,11... | collective-permute-start | bytes 3145736 | tf_op jit(solution)/shard_map/ppermute | solution.py:270
  553.2 22.5 %collective-permute-start.41 = (bf16[2,256,1024]{2,1,0:T(8,128)(2,1)S(1)}, bf16[2,256,1024]{2,1,0:T(8,128)(2,1)S(1)}, u32[]{:S(2)}, u32[]{:S(2)}) collective-permute-start(bf16[2,256,1024]{2,1,0:T(8,128)(2,1)S(1)} %get-tuple-element.219), channel_id=1, source_target_pairs={{0,4},{2,6},{4,0},{6,2},{8,12},{10,14},{12,8},{14,10},{16,20},{18,... | collective-permute-start | bytes 3145736 | tf_op jit(solution)/shard_map/ppermute | solution.py:267
  617.4 123.8 %reduce-scatter.9.cloned.1.call-start = ((), (), s32[]{:S(2)}) async-start(), calls=%async_computation.11 | async-start | bytes 3932160 | tf_op jit(solution)/shard_map/reduce_scatter | solution.py:428
  656.8 23.7 %collective-permute-start.56 = (bf16[256,1,1024]{2,0,1:T(8,128)(2,1)}, bf16[256,1,1024]{2,0,1:T(8,128)(2,1)}, u32[]{:S(2)}, u32[]{:S(2)}) collective-permute-start(bf16[256,1,1024]{2,0,1:T(8,128)(2,1)} %dynamic-slice_bitcast_fusion.2), channel_id=1, source_target_pairs={{0,4},{2,6},{4,0},{6,2},{8,12},{10,14},{12,8},{14,10},{16,20},{18,... | collective-permute-start | bytes 1572872 | tf_op jit(solution)/shard_map/ppermute | solution.py:267
  658.2 44.4 %collective-permute-start.46 = (bf16[256,2048]{1,0:T(8,128)(2,1)}, bf16[256,2048]{1,0:T(8,128)(2,1)}, u32[]{:S(2)}, u32[]{:S(2)}) collective-permute-start(bf16[256,2048]{1,0:T(8,128)(2,1)} %slice_bitcast_fusion.3), channel_id=1, source_target_pairs={{0,4},{2,6},{4,0},{6,2},{8,12},{10,14},{12,8},{14,10},{16,20},{18,... | collective-permute-start | bytes 3145736 | tf_op jit(solution)/shard_map/ppermute | solution.py:267
  666.9 40.4 %collective-permute-start.49 = (bf16[2,256,1024]{2,1,0:T(8,128)(2,1)}, bf16[2,256,1024]{2,1,0:T(8,128)(2,1)}, u32[]{:S(2)}, u32[]{:S(2)}) collective-permute-start(bf16[2,256,1024]{2,1,0:T(8,128)(2,1)} %dynamic-slice_bitcast_fusion), channel_id=1, source_target_pairs={{0,1},{1,0},{2,3},{3,2},{4,5},{5,4},{6,7},{7,6},{8,9},{9,8},{10,11... | collective-permute-start | bytes 3145736 | tf_op jit(solution)/shard_map/ppermute | solution.py:270
  683.6 37.6 %collective-permute-start.57 = (bf16[128,1,2048]{2,0,1:T(8,128)(2,1)}, bf16[128,1,2048]{2,0,1:T(8,128)(2,1)}, u32[]{:S(2)}, u32[]{:S(2)}) collective-permute-start(bf16[128,1,2048]{2,0,1:T(8,128)(2,1)} %fusion.55), channel_id=1, source_target_pairs={{0,2},{2,0},{4,6},{6,4},{8,10},{10,8},{12,14},{14,12},{16,18},{18,... | collective-permute-start | bytes 1572872 | tf_op jit(solution)/shard_map/ppermute | solution.py:264
  684.4 32.9 %collective-permute-start.59 = (bf16[128,1,2048]{2,0,1:T(8,128)(2,1)}, bf16[128,1,2048]{2,0,1:T(8,128)(2,1)}, u32[]{:S(2)}, u32[]{:S(2)}) collective-permute-start(bf16[128,1,2048]{2,0,1:T(8,128)(2,1)} %fusion.53), channel_id=1, source_target_pairs={{0,2},{2,0},{4,6},{6,4},{8,10},{10,8},{12,14},{14,12},{16,18},{18,... | collective-permute-start | bytes 1572872 | tf_op jit(solution)/shard_map/ppermute | solution.py:264
  706.1 40.5 %collective-permute-start.47 = (bf16[256,1024]{1,0:T(8,128)(2,1)}, bf16[256,1024]{1,0:T(8,128)(2,1)}, u32[]{:S(2)}, u32[]{:S(2)}) collective-permute-start(bf16[256,1024]{1,0:T(8,128)(2,1)} %constant_dynamic-slice_fusion.2), channel_id=1, source_target_pairs={{0,1},{1,0},{2,3},{3,2},{4,5},{5,4},{6,7},{7,6},{8,9},{9,8},{10,11... | collective-permute-start | bytes 1572872 | tf_op jit(solution)/shard_map/ppermute | solution.py:270
  732.1 31.7 %all-to-all-start.1 = ((bf16[32,16,1024]{2,0,1:T(8,128)(2,1)}), bf16[32,16,1024]{2,0,1:T(8,128)(2,1)S(1)}, u32[]{:S(2)}, u32[]{:S(2)}) async-start(bf16[32,16,1024]{2,0,1:T(8,128)(2,1)} %copy.235), calls=%async_computation.3 | async-start | bytes 2097152 | tf_op jit(solution)/shard_map/all_to_all | solution.py:501
  (123 other events, 861.6 us)
Sparse Core Ops, SparseCore 0:
  49.3 79.8 all-gather.2
  150.4 147.5 all-gather.4
  447.6 74.1 reduce-scatter.4
  524.0 77.2 reduce-scatter.6
  617.5 24.9 reduce-scatter.10
  668.7 58.2 reduce-scatter.8

commit v3 on v2

--- a/solution.py
+++ b/solution.py
@@ -266,6 +266,9 @@
     def side_swap(array):
         return lax.ppermute(array, "dp", side_pairs)
 
+    def ring_send(array, steps):
+        return lax.ppermute(array, "dp", [(i, (i + 4 * steps) % groups) for i in range(groups)])
+
     def lane_swap(array):
         return lax.ppermute(array, "tensor", [(0, 1), (1, 0)])
 
@@ -302,22 +305,6 @@
     second_weights = after(up_weight, first_piece), after(down_weight, first_piece).T
     second_piece = split_weight(jnp.stack(second_weights, axis=1))
     second_full = gather_weight(second_piece)
-
-    local_rows = inputs.reshape(groups, per_peer, half).swapaxes(0, 1)
-    sending = jnp.take(local_rows, dealing, axis=1)
-    arrived = lax.all_to_all(sending, "dp", split_axis=1, concat_axis=1, tiled=True)
-    tokens = after(arrived, first_piece).reshape(seq_len, half)
-    early, late = tokens[:token_half], tokens[token_half:]
-    early = in_order(lane, early, lane_swap(early), 1)
-    early = jnp.stack([early, side_swap(early)])
-    late = jnp.stack([late, side_swap(late)])
-    late = in_order(lane, late, lane_swap(late), 2)
-    own_rows = jnp.stack([jnp.where(lane == 0, early, late), jnp.where(lane == 0, late, early)], 1)
-    own_rows = own_rows.reshape(2 * seq_len, width)
-    all_rows = (own_rows, core_swap(own_rows))
-    residual = own_rows[:token_half]
-    grad_keep, grad_send = parts(out_grad, lane, 0)
-    cotangent = in_order(lane, grad_keep, lane_swap(grad_send), 1)
 
     small = jnp.concatenate(
         [
@@ -336,12 +323,29 @@
     )[None]
     small = in_order(core, small, core_swap(after(small, first_piece)), 0)
     small = in_order(side, small, side_swap(small), 0)
-    small_all = jnp.zeros((groups, small.shape[1]), low)
-    for step in range(ring_size):
-        if step:
-            small = lax.ppermute(small, "dp", [(i, (i + 4) % groups) for i in range(groups)])
+    small_all = lax.dynamic_update_slice_in_dim(
+        jnp.zeros((groups, small.shape[1]), low), small, ring * 4, 0
+    )
+    for step in range(1, ring_size):
         place = ((ring - step) % ring_size) * 4
-        small_all = lax.dynamic_update_slice_in_dim(small_all, small, place, 0)
+        small_all = lax.dynamic_update_slice_in_dim(small_all, ring_send(small, step), place, 0)
+
+    local_rows = inputs.reshape(groups, per_peer, half).swapaxes(0, 1)
+    sending = jnp.take(local_rows, dealing, axis=1)
+    arrived = lax.all_to_all(sending, "dp", split_axis=1, concat_axis=1, tiled=True)
+    tokens = after(arrived, first_piece).reshape(seq_len, half)
+    early, late = tokens[:token_half], tokens[token_half:]
+    early = in_order(lane, early, lane_swap(early), 1)
+    early = jnp.stack([early, side_swap(early)])
+    late = jnp.stack([late, side_swap(late)])
+    late = in_order(lane, late, lane_swap(late), 2)
+    own_rows = jnp.stack([jnp.where(lane == 0, early, late), jnp.where(lane == 0, late, early)], 1)
+    own_rows = after(own_rows.reshape(2 * seq_len, width), second_piece, small_all)
+    all_rows = (own_rows, core_swap(own_rows))
+    residual = own_rows[:token_half]
+    grad_keep, grad_send = parts(out_grad, lane, 0)
+    cotangent = in_order(lane, grad_keep, lane_swap(grad_send), 1)
+
     cut_one = qv_bias.size
     cut_two = cut_one + up_bias.size
     qv_full = (
@@ -382,13 +386,14 @@
         two = two[0] + after(side_swap(two[1].astype(low)), *beside_two).astype(wide)
         return jnp.concatenate([one, two], axis=1)
 
-    def group_gather(rows, beside_one=(), beside_two=()):
+    def group_gather(rows, beside_own=()):
         one, two = rows[:, :half], rows[:, half:]
-        one = jnp.stack([one, after(lane_swap(one), *beside_one)])
-        two = jnp.stack([two, after(side_swap(two), *beside_one)])
-        one = jnp.stack([one, after(side_swap(one), *beside_two)])
-        two = jnp.stack([two, after(lane_swap(two), *beside_two)], axis=1)
+        one = jnp.stack([one, lane_swap(one)])
+        two = jnp.stack([two, side_swap(two)])
+        one = jnp.stack([one, side_swap(one)])
+        two = jnp.stack([two, lane_swap(two)], axis=1)
         own = jnp.concatenate([one, two], axis=3).reshape(2 * seq_len, width)
+        own = after(own, *beside_own)
         return own, core_swap(own)
 
     sequences = jnp.stack([index, index ^ 2, index ^ 1, index ^ 3])
@@ -398,21 +403,24 @@
     )
     qkv_bias = jnp.concatenate([qv_rows[0], jnp.zeros_like(qv_rows[0]), qv_rows[1]]).astype(wide)
     flops = 4 * 2 * seq_len * seq_len * features
-    all_rows = tuple(after(rows, second_piece) for rows in all_rows)
-    projected = [matmul(rows, first_full, 0, 3 * features, bias=qkv_bias) for rows in all_rows]
-    context = [
-        by_sequence(attend_kernel, 4 * flops, seq_len, group_lengths[i], projected[i])
-        for i in range(2)
-    ]
+    projected, context = [], []
+    for i in range(2):
+        rows = after(all_rows[i], *context)
+        projected.append(matmul(rows, first_full, 0, 3 * features, bias=qkv_bias))
+        context.append(
+            by_sequence(attend_kernel, 4 * flops, seq_len, group_lengths[i], projected[i])
+        )
     attended = group_sum(core_parts(context, first_full, 3 * features)) + out_bias_full
     first, normed_one, inverse_one = norm_forward(
         residual.astype(wide) + attended, gain_one, shift_one
     )
-    first_low = group_gather(first.astype(low))
-
-    pre_act, hidden = zip(
-        *[up_matmul(rows, second_full, up_bias_mine.astype(wide)) for rows in first_low], strict=True
-    )
+    first_low = group_gather(first.astype(low), [second_full])
+
+    pre_act, hidden = [], []
+    for i in range(2):
+        values, outs = up_matmul(after(first_low[i], *hidden), second_full, up_bias_mine.astype(wide))
+        pre_act.append(values)
+        hidden.append(outs)
     mixed_parts = core_parts(hidden, second_full, units)
     slope = [gelu_slope(after(values, *mixed_parts)).astype(low) for values in pre_act]
     mixed = group_sum(mixed_parts, slope) + down_bias_full
@@ -429,22 +437,24 @@
             partial, "dp", scatter_dimension=0, axis_index_groups=ring_groups, tiled=True
         )
 
-    def join_grad(total, kinds):
+    def side_send(total, kinds):
         total = total.reshape(4 * shard, kinds, -1)
         mine, sent = parts(total, side, 0)
-        total = in_order(side, mine, side_swap(sent), 2)
+        return mine, side_swap(sent)
+
+    def side_join(mine, theirs):
+        return in_order(side, mine, theirs, 2)
+
+    def core_join(total):
         mine, sent = parts(total, core, 0)
         return in_order(core, mine, core_swap(sent), 2).astype(wide)
 
+    pre_grad = [up_back_matmul(mixed_grad[0], second_full, slope[0])]
+    mixed_grad = (mixed_grad[0], after(mixed_grad[1], pre_grad[0][0]))
     down_partial = pair_matmul(mixed_grad, hidden)
     down_sum = scatter(down_partial)
-    pre_grad, up_bias_grad = zip(
-        *[
-            up_back_matmul(after(mixed_grad[i], down_partial), second_full, slope[i])
-            for i in range(2)
-        ],
-        strict=True,
-    )
+    pre_grad.append(up_back_matmul(after(mixed_grad[1], down_partial), second_full, slope[1]))
+    pre_grad, up_bias_grad = zip(*pre_grad, strict=True)
     both = core_parts(pre_grad, second_full)
     up_partial = pair_matmul(first_low, [after(grads, *both) for grads in pre_grad])
     up_sum = scatter(up_partial)
@@ -455,60 +465,70 @@
     attended_low = attn_total_grad.astype(low)
     out_bias_grad = jnp.sum(attended_low, axis=0, dtype=wide)
     attended_grad = group_gather(attended_low)
-    out_partial = pair_matmul(attended_grad, context)
-    out_sum = scatter(out_partial)
-    context_grad = [
-        matmul(after(rows, out_partial), first_full, 0, features, 3 * features)
-        for rows in attended_grad
-    ]
-    stacked = [
-        by_sequence(
-            attend_back_kernel,
-            8 * flops,
-            seq_len,
-            group_lengths[i],
-            projected[i],
-            context_grad[i],
+    down_sum = side_send(down_sum, 1)
+    stacked = []
+    for i in range(2):
+        rows = attended_grad[i]
+        if i:
+            attended_grad = (attended_grad[0], after(rows, *stacked, down_sum[1]))
+            out_partial = pair_matmul(attended_grad, context)
+            out_sum = scatter(out_partial)
+            rows = after(attended_grad[1], out_partial)
+        context_grad = matmul(rows, first_full, 0, features, 3 * features)
+        stacked.append(
+            by_sequence(
+                attend_back_kernel,
+                8 * flops,
+                seq_len,
+                group_lengths[i],
+                projected[i],
+                context_grad,
+            )
         )
-        for i in range(2)
-    ]
-    both = core_parts((stacked[0], after(stacked[1], up_sum)), first_full)
-    own_part = sum(array.astype(wide) for array in both).astype(low)
-    own_part = own_part.reshape(2, 2, token_half, width)
-    early, late = (
-        jnp.where(lane == bit, own_part[:, 0], own_part[:, 1]) for bit in range(2)
-    )
-    early_sent = early[1]
-    late, late_sent = parts(late, lane, 2)
-    qkv_partial = pair_matmul(all_rows, [after(g, early_sent, late_sent) for g in stacked])
+    theirs = matmul(after(stacked[1], up_sum), first_full, 1, width)
+    qkv_partial = pair_matmul(all_rows, [after(grads, theirs) for grads in stacked])
     qkv_sum = scatter(qkv_partial)
-    early = early[0].astype(wide) + side_swap(early_sent).astype(wide)
-    late = late.astype(wide) + after(lane_swap(late_sent), qkv_partial).astype(wide)
-    early, early_sent = parts(early, lane, 1)
-    early_sent, late_sent = early_sent.astype(low), late[1].astype(low)
-    early = early + lane_swap(early_sent).astype(wide)
-    late = late[0] + side_swap(late_sent).astype(wide)
+    theirs = core_swap(theirs)
+    mine = matmul(after(stacked[0], qkv_partial), first_full, 1, width)
+    up_sum = side_send(up_sum, 1)
+
+    quarter = half // 2
+    both = tuple(array.reshape(2, seq_len, width) for array in (after(mine, up_sum[1]), theirs))
+
+    def summed(pick):
+        return sum(pick(array).astype(wide) for array in both)
+
+    def across(array):
+        return jnp.concatenate([array[..., :quarter], array[..., half : half + quarter]], axis=-1)
+
+    def of_lane(bit):
+        return lambda array: take(array, bit * half + quarter, quarter, 2)
+
+    def lane_swap_rows(array):
+        array = lane_swap(array)
+        return jnp.concatenate([array[..., token_half:, :], array[..., :token_half, :]], axis=-2)
+
+    one_sent = summed(lambda array: across(array[1])).astype(low)
+    two_sent = summed(of_lane(1 - lane)).astype(low)
+    one, two = side_swap(one_sent), lane_swap_rows(two_sent)
+    one = summed(lambda array: across(array[0])) + one.astype(wide)
+    two = summed(of_lane(lane)) + two.astype(wide)
+    one_sent = take(one, (1 - lane) * quarter, quarter, 1).astype(low)
+    two_sent = two[1].astype(low)
+    one = take(one, lane * quarter, quarter, 1) + lane_swap_rows(one_sent).astype(wide)
+    two = two[0] + side_swap(two_sent).astype(wide)
     own_attended = take(attended_grad[0][:seq_len], lane * half, half, 1)
-    own_attended = in_order(lane, own_attended[:token_half], own_attended[token_half:], 0)
-    in_half = (jnp.concatenate([early, late], axis=0) + own_attended.astype(wide)).astype(low)
-    qkv_bias_sum = sum(jnp.sum(after(s, early_sent), axis=0, dtype=wide) for s in stacked)
+    in_half = (jnp.concatenate([one, two], axis=1) + own_attended.astype(wide)).astype(low)
+    in_half = in_order(lane, in_half[:token_half], in_half[token_half:], 0)
+    down_weight_grad = core_join(after(side_join(*down_sum), one_sent))[:, 0].T
+    up_weight_grad = core_join(after(side_join(*up_sum), one_sent))[:, 0]
+    in_half = after(in_half, down_weight_grad, up_weight_grad)
+    back_rows = in_half.reshape(per_peer, groups, half)
+    out_keep, out_send = parts(final.astype(low), lane, 1)
+    outputs = in_order(lane, out_keep, lane_swap(after(out_send, back_rows)), 0)
+    qkv_bias_sum = sum(jnp.sum(after(s, back_rows), axis=0, dtype=wide) for s in stacked)
     qkv_bias_sum = qkv_bias_sum.reshape(3, features)
     qv_grad = jnp.stack([qkv_bias_sum[0], qkv_bias_sum[2]])
-    out_keep, out_send = parts(final.astype(low), lane, 1)
-    outputs = in_order(lane, out_keep, lane_swap(after(out_send, early_sent)), 0)
-
-    back_rows = in_half.reshape(per_peer, groups, half)
-    returned = lax.all_to_all(back_rows, "dp", split_axis=1, concat_axis=1, tiled=True)
-    inverse_order = (
-        jnp.zeros((groups,), jnp.int32).at[dealing].set(jnp.arange(groups, dtype=jnp.int32))
-    )
-    in_grad = jnp.take(returned, inverse_order, axis=1).swapaxes(0, 1).reshape(seq_len, half)
-
-    down_weight_grad = join_grad(after(down_sum, qkv_partial), 1)[:, 0].T
-    up_weight_grad = join_grad(after(up_sum, qkv_partial), 1)[:, 0]
-    out_weight_grad = join_grad(after(out_sum, early_sent), 1)[:, 0].T
-    qkv_grad = join_grad(qkv_sum, 3).swapaxes(0, 1)
-
     def spread(mine, size):
         full = jnp.zeros(mine.shape[:-1] + (4 * size,), wide)
         return lax.dynamic_update_slice_in_dim(full, mine, place * size, mine.ndim - 1)
@@ -541,8 +561,27 @@
         .reshape(groups, -1)
     )
     packed = jnp.concatenate([qv_spread, up_spread, vector_spread], axis=1)
-    exchanged = lax.all_to_all(packed, "dp", split_axis=0, concat_axis=0, tiled=True)
-    small_sum = jnp.sum(exchanged, axis=0)
+    packed = after(packed, back_rows)
+
+    returned = lax.all_to_all(back_rows, "dp", split_axis=1, concat_axis=1, tiled=True)
+    inverse_order = (
+        jnp.zeros((groups,), jnp.int32).at[dealing].set(jnp.arange(groups, dtype=jnp.int32))
+    )
+    in_grad = jnp.take(returned, inverse_order, axis=1).swapaxes(0, 1).reshape(seq_len, half)
+
+    out_weight_grad = core_join(side_join(*side_send(after(out_sum, two_sent), 1)))[:, 0].T
+    qkv_grad = core_join(side_join(*side_send(qkv_sum, 3))).swapaxes(0, 1)
+
+    packed = packed.reshape(ring_size, 2, 2, packed.shape[1])
+    mine, sent = parts(packed, core, 2)
+    packed = (mine + core_swap(sent))[:, :, 0]
+    mine, sent = parts(packed, side, 1)
+    packed = (mine + side_swap(sent))[:, 0]
+    small_sum = take(packed, ring, 1, 0)
+    for step in range(1, ring_size):
+        sent = take(packed, (ring + step) % ring_size, 1, 0)
+        small_sum = small_sum + ring_send(sent, step)
+    small_sum = small_sum[0]
     vector_sum = small_sum[cut_two:]
     vector_sum = (vector_sum + lane_swap(vector_sum)).reshape(6, shard)
     return (

time: 784 us -> 750 us (0.957)
  waiting for transfers between devices: 360 us -> 323 us
    ppermute x3 -> x6, waiting for transfers between devices: 16.5 us -> 1.03 us  [ring_send(): lax.ppermute(array, 'dp', [(i, (i + 4 * steps) % groups) for i in range(g...]
    ppermute x15 -> x16, waiting for transfers between devices: 21.1 us -> 6.73 us  [core_swap(): return lax.ppermute(array, 'dp', core_pairs)]
    ppermute x3 -> x6, starting transfers between devices: 0.76 us -> 11.6 us  [ring_send(): lax.ppermute(array, 'dp', [(i, (i + 4 * steps) % groups) for i in range(g...]
    ppermute x23 -> x24, waiting for transfers between devices: 194 us -> 186 us  [side_swap(): return lax.ppermute(array, 'dp', side_pairs)]
    unnamed x185 -> x201, local copies, waits for them, and re-layouts: 49.9 us -> 54 us
    ppermute x23 -> x24, starting transfers between devices: 28.9 us -> 27.9 us  [side_swap(): return lax.ppermute(array, 'dp', side_pairs)]
  transfers between devices with their start and end apart: 69 -> 73, of which waited for: 40 -> 41; matrix products, arithmetic and copies ran while one was open for 17% -> 17% of each run, Pallas kernels for 13% -> 15%
where the time goes in v3:
time: 750 us; the launch traced here: 741 us
  waiting for transfers between devices  323 us (43%)
  Pallas kernels  147 us (20%)
  local copies, waits for them, and re-layouts  98.6 us (13%)
  other arithmetic  83.6 us (11%)
  starting transfers between devices  72.9 us (10%)
  between operations  16.4 us (2%)
    ppermute x24, waiting for transfers between devices, side_swap(): return lax.ppermute(array, 'dp', side_pairs)  186 us
    ppermute x19, waiting for transfers between devices, lane_swap(): return lax.ppermute(array, 'tensor', [(0, 1), (1, 0)])  87.1 us
    pallas_call x12, Pallas kernels, matmul(): call(functools.partial(matmul_kernel, right_axis), 2 * rows * depth * siz...  59.2 us
    unnamed x201, local copies, waits for them, and re-layouts  54 us
    all_gather x2, waiting for transfers between devices, gather_weight(): lax.all_gather(piece, 'dp', axis=0, axis_index_groups=ring_groups, tiled=...  41.1 us
    pallas_call x4, Pallas kernels, pair_matmul(): call(pair_kernel, 4 * rows * depth * columns, jax.ShapeDtypeStruct((depth...  39.6 us
    ppermute x24, starting transfers between devices, side_swap(): return lax.ppermute(array, 'dp', side_pairs)  27.9 us
    ppermute x19, starting transfers between devices, lane_swap(): return lax.ppermute(array, 'tensor', [(0, 1), (1, 0)])  21.1 us
  transfers between devices with their start and end apart: 73, of which 41 were waited for; matrix products, arithmetic and copies ran while one was open for 17% of the time, Pallas kernels for 15%

profile of v3, /device:TPU:0, one launch (start us, length us, event | category | flops | bytes accessed | tf_op | source)
XLA Modules:
  0.0 740.8 jit_solution(4470724108716535531)
XLA Ops:
  25.2 6.8 collective-permute-done.1
  53.0 8.9 %collective-permute-done.4 = bf16[256,1024]{1,0:T(8,128)(2,1)S(1)} collective-permute-done((bf16[256,1024]{1,0:T(8,128)(2,1)S(1)}, bf16[256,1024]{1,0:T(8,128)(2,1)S(1)}, u32[]{:S(2)}, u32[]{:S(2)}) %collective-permute-start.4) | collective-permute-done | bytes 524320 | tf_op jit(solution)/shard_map/ppermute | solution.py:267
  68.3 16.1 %collective-permute-done.7 = bf16[256,2,1024]{0,2,1:T(8,128)(2,1)S(1)} collective-permute-done((bf16[256,2,1024]{0,2,1:T(8,128)(2,1)S(1)}, bf16[256,2,1024]{0,2,1:T(8,128)(2,1)S(1)}, u32[]{:S(2)}, u32[]{:S(2)}) %collective-permute-start.7) | collective-permute-done | bytes 1048608 | tf_op jit(solution)/shard_map/ppermute | solution.py:267
  89.4 17.3 %collective-permute-done.3 = bf16[256,2048]{1,0:T(8,128)(2,1)} collective-permute-done((bf16[256,2048]{1,0:T(8,128)(2,1)}, bf16[256,2048]{1,0:T(8,128)(2,1)}, u32[]{:S(2)}, u32[]{:S(2)}) %collective-permute-start.3) | collective-permute-done | bytes 1048608 | tf_op jit(solution)/shard_map/ppermute | solution.py:267
  113.5 11.0 %all-gather.3.cloned.1.call-done.right = bf16[2048,1024]{1,0:T(8,128)(2,1)} async-done(((bf16[512,1024]{1,0:T(8,128)(2,1)}), bf16[2048,1024]{1,0:T(8,128)(2,1)}) %all-gather.3.cloned.1.call-update) | async-done | bytes 4194320 | tf_op jit(solution)/shard_map/all_gather | solution.py:300
  126.7 6.8 shard_map.263.query.key.value
  160.4 22.1 %collective-permute-done.15 = bf16[2,256,1024]{2,1,0:T(8,128)(2,1)S(1)} collective-permute-done((bf16[2,256,1024]{2,1,0:T(8,128)(2,1)S(1)}, bf16[2,256,1024]{2,1,0:T(8,128)(2,1)S(1)}, u32[]{:S(2)}, u32[]{:S(2)}) %collective-permute-start.15) | collective-permute-done | bytes 1048608 | tf_op jit(solution)/shard_map/ppermute | solution.py:267
  189.2 10.3 %collective-permute-done.18 = bf16[256,1024]{1,0:T(8,128)(2,1)} collective-permute-done((bf16[256,1024]{1,0:T(8,128)(2,1)}, bf16[256,1024]{1,0:T(8,128)(2,1)}, u32[]{:S(2)}, u32[]{:S(2)}) %collective-permute-start.18) | collective-permute-done | bytes 524320 | tf_op jit(solution)/shard_map/ppermute | solution.py:267
  208.0 9.4 %collective-permute-done.21 = bf16[256,1024]{1,0:T(8,128)(2,1)S(1)} collective-permute-done((bf16[256,1024]{1,0:T(8,128)(2,1)S(1)}, bf16[256,1024]{1,0:T(8,128)(2,1)S(1)}, u32[]{:S(2)}, u32[]{:S(2)}) %collective-permute-start.21) | collective-permute-done | bytes 524320 | tf_op jit(solution)/shard_map/ppermute | solution.py:267
  220.4 20.0 %collective-permute-done.22 = bf16[2,256,1024]{2,1,0:T(8,128)(2,1)S(1)} collective-permute-done((bf16[2,256,1024]{2,1,0:T(8,128)(2,1)S(1)}, bf16[2,256,1024]{2,1,0:T(8,128)(2,1)S(1)}, u32[]{:S(2)}, u32[]{:S(2)}) %collective-permute-start.22) | collective-permute-done | bytes 1048608 | tf_op jit(solution)/shard_map/ppermute | solution.py:273
  244.3 30.0 %all-gather.5.cloned.1.call-done.weight.right = bf16[2048,2048]{1,0:T(8,128)(2,1)} async-done(((bf16[512,2048]{1,0:T(8,128)(2,1)}), bf16[2048,2048]{1,0:T(8,128)(2,1)}) %all-gather.5.cloned.1.call-update) | async-done | bytes 8388624 | tf_op jit(solution)/shard_map/all_gather | solution.py:300
  277.5 7.6 %shard_map.269 = (f32[1024,1024]{1,0:T(8,128)S(1)}, bf16[1024,1024]{1,0:T(8,128)(2,1)S(1)}) custom-call(bf16[1024,2048]{1,0:T(8,128)(2,1)S(1)} %bitcast.315, bf16[2048,2048]{1,0:T(8,128)(2,1)} %all-gather.5.cloned.1.call-done.weight.right, f32[1,1024]{1,0:T(1,128)S(1)} %bitcast.328), custom_call_target="tpu_custom_call" | custom-call | flops 536870912 | tf_op jit(solution)/shard_map/pallas_call | solution.py:177
  288.4 8.8 %shard_map.271 = (f32[1024,1024]{1,0:T(8,128)S(1)}, bf16[1024,1024]{1,0:T(8,128)(2,1)S(1)}) custom-call(bf16[1024,2048]{1,0:T(8,128)(2,1)} %collective-permute-done.23.rows.left_two, bf16[2048,2048]{1,0:T(8,128)(2,1)} %all-gather.5.cloned.1.call-done.weight.right, f32[1,1024]{1,0:T(1,128)S(1)} %bitcast.329), custom_call_target="tpu_custom_call" | custom-call | flops 536870912 | tf_op jit(solution)/shard_map/pallas_call | solution.py:177
  299.1 8.6 %shard_map.272 = bf16[1024,2048]{1,0:T(8,128)(2,1)} custom-call(bf16[1024,1024]{1,0:T(8,128)(2,1)S(1)} %get-tuple-element.68.left.right_two, bf16[2048,2048]{1,0:T(8,128)(2,1)} %all-gather.5.cloned.1.call-done.weight.right), custom_call_target="tpu_custom_call" | custom-call | flops 536870912 | tf_op jit(solution)/shard_map/pallas_call | solution.py:149
  313.1 6.7 shard_map.270
  331.6 16.5 %collective-permute-done.25 = bf16[2,256,1024]{2,1,0:T(8,128)(2,1)S(1)} collective-permute-done((bf16[2,256,1024]{2,1,0:T(8,128)(2,1)S(1)}, bf16[2,256,1024]{2,1,0:T(8,128)(2,1)S(1)}, u32[]{:S(2)}, u32[]{:S(2)}) %collective-permute-start.25) | collective-permute-done | bytes 1048608 | tf_op jit(solution)/shard_map/ppermute | solution.py:267
  355.1 9.8 %collective-permute-done.28 = bf16[256,1024]{1,0:T(8,128)(2,1)S(1)} collective-permute-done((bf16[256,1024]{1,0:T(8,128)(2,1)S(1)}, bf16[256,1024]{1,0:T(8,128)(2,1)S(1)}, u32[]{:S(2)}, u32[]{:S(2)}) %collective-permute-start.28) | collective-permute-done | bytes 524320 | tf_op jit(solution)/shard_map/ppermute | solution.py:267
  370.6 9.2 %collective-permute-done.32 = bf16[256,1024]{1,0:T(8,128)(2,1)S(1)} collective-permute-done((bf16[256,1024]{1,0:T(8,128)(2,1)S(1)}, bf16[256,1024]{1,0:T(8,128)(2,1)S(1)}, u32[]{:S(2)}, u32[]{:S(2)}) %collective-permute-start.32) | collective-permute-done | bytes 524320 | tf_op jit(solution)/shard_map/ppermute | solution.py:267
  383.0 20.5 %collective-permute-done.33 = bf16[2,256,1024]{2,1,0:T(8,128)(2,1)S(1)} collective-permute-done((bf16[2,256,1024]{2,1,0:T(8,128)(2,1)S(1)}, bf16[2,256,1024]{2,1,0:T(8,128)(2,1)S(1)}, u32[]{:S(2)}, u32[]{:S(2)}) %collective-permute-start.33) | collective-permute-done | bytes 1048608 | tf_op jit(solution)/shard_map/ppermute | solution.py:273
  404.6 6.8 shard_map.273
  414.7 11.9 %shard_map.275 = bf16[2048,1024]{1,0:T(8,128)(2,1)S(1)} custom-call(bf16[1024,2048]{1,0:T(8,128)(2,1)S(1)} %bitcast.313, bf16[1024,1024]{1,0:T(8,128)(2,1)S(1)} %copy-done.24, bf16[1024,2048]{1,0:T(8,128)(2,1)} %copy-done.14, bf16[1024,1024]{1,0:T(8,128)(2,1)S(1)} %copy-done.26), custom_call_target="tpu_custom_call" | custom-call | flops 1073741824 | tf_op jit(solution)/shard_map/pallas_call | solution.py:226
  433.0 6.9 shard_map.276
  440.0 6.9 shard_map.277
  447.2 6.7 shard_map.274
  459.3 11.8 %shard_map.278 = bf16[2048,1024]{1,0:T(8,128)(2,1)S(1)} custom-call(bf16[1024,2048]{1,0:T(8,128)(2,1)S(1)} %bitcast.316, bf16[1024,1024]{1,0:T(8,128)(2,1)S(1)} %copy-done.28, bf16[1024,2048]{1,0:T(8,128)(2,1)} %collective-permute-done.23.rows.left_two, bf16[1024,1024]{1,0:T(8,128)(2,1)S(1)} %get-tuple-element.80.left.right_two), custom_call_target="tpu_custom_call" | custom-call | flops 1073741824 | tf_op jit(solution)/shard_map/pallas_call | solution.py:226
  473.2 8.0 %collective-permute-done.36 = bf16[2,256,1024]{2,1,0:T(8,128)(2,1)} collective-permute-done((bf16[2,256,1024]{2,1,0:T(8,128)(2,1)}, bf16[2,256,1024]{2,1,0:T(8,128)(2,1)}, u32[]{:S(2)}, u32[]{:S(2)}) %collective-permute-start.36) | collective-permute-done | bytes 1048608 | tf_op jit(solution)/shard_map/ppermute | solution.py:267
  491.7 11.4 %collective-permute-done.39 = bf16[256,1024]{1,0:T(8,128)(2,1)} collective-permute-done((bf16[256,1024]{1,0:T(8,128)(2,1)}, bf16[256,1024]{1,0:T(8,128)(2,1)}, u32[]{:S(2)}, u32[]{:S(2)}) %collective-permute-start.39) | collective-permute-done | bytes 524320 | tf_op jit(solution)/shard_map/ppermute | solution.py:267
  513.2 10.7 %collective-permute-done.42 = bf16[256,1024]{1,0:T(8,128)(2,1)S(1)} collective-permute-done((bf16[256,1024]{1,0:T(8,128)(2,1)S(1)}, bf16[256,1024]{1,0:T(8,128)(2,1)S(1)}, u32[]{:S(2)}, u32[]{:S(2)}) %collective-permute-start.42) | collective-permute-done | bytes 524320 | tf_op jit(solution)/shard_map/ppermute | solution.py:267
  527.2 20.8 %collective-permute-done.43 = bf16[2,256,1024]{2,1,0:T(8,128)(2,1)S(1)} collective-permute-done((bf16[2,256,1024]{2,1,0:T(8,128)(2,1)S(1)}, bf16[2,256,1024]{2,1,0:T(8,128)(2,1)S(1)}, u32[]{:S(2)}, u32[]{:S(2)}) %collective-permute-start.43) | collective-permute-done | bytes 1048608 | tf_op jit(solution)/shard_map/ppermute | solution.py:273
  604.0 10.0 %shard_map.285 = bf16[2048,768]{1,0:T(8,128)(2,1)S(1)} custom-call(bf16[1024,2048]{1,0:T(8,128)(2,1)} %bitcast.16.left.left_one, bf16[1024,768]{1,0:T(8,128)(2,1)S(1)} %copy-done.11, bf16[1024,2048]{1,0:T(8,128)(2,1)} %collective-permute-done.13.left.left_two, bf16[1024,768]{1,0:T(8,128)(2,1)S(1)} %shard_map.283.left.right_two), custom_call_target="tpu_custom_call" | custom-call | flops 805306368 | tf_op jit(solution)/shard_map/pallas_call | solution.py:226
  634.8 16.4 %collective-permute-done.50 = bf16[2,512,512]{2,1,0:T(8,128)(2,1)} collective-permute-done((bf16[2,512,512]{2,1,0:T(8,128)(2,1)}, bf16[2,512,512]{2,1,0:T(8,128)(2,1)}, u32[]{:S(2)}, u32[]{:S(2)}) %collective-permute-start.50) | collective-permute-done | bytes 1048608 | tf_op jit(solution)/shard_map/ppermute | solution.py:273
  713.7 13.1 %collective-permute-done.55 = bf16[256,3,256]{0,2,1:T(8,128)(2,1)S(1)} collective-permute-done((bf16[256,3,256]{0,2,1:T(8,128)(2,1)}, bf16[256,3,256]{0,2,1:T(8,128)(2,1)S(1)}, u32[]{:S(2)}, u32[]{:S(2)}) %collective-permute-start.55) | collective-permute-done | bytes 393248 | tf_op jit(solution)/shard_map/ppermute | solution.py:267
  (549 shorter events, 336.5 us)
Async XLA Ops:
  18.1 28.6 %all-to-all-start = ((bf16[32,16,1024]{2,0,1:T(8,128)(2,1)}), bf16[32,16,1024]{2,0,1:T(8,128)(2,1)S(1)}, u32[]{:S(2)}, u32[]{:S(2)}) async-start(bf16[32,16,1024]{2,0,1:T(8,128)(2,1)} %select_bitcast_fusion), calls=%async_computation | async-start | bytes 2097152 | tf_op jit(solution)/shard_map/all_to_all | solution.py:335
  23.1 101.4 %all-gather.3.cloned.1.call-start = ((), (), s32[]{:S(2)}) async-start(), calls=%async_computation.6 | async-start | bytes 5242880 | tf_op jit(solution)/shard_map/all_gather | solution.py:300
  40.8 233.5 %all-gather.5.cloned.1.call-start = ((), (), s32[]{:S(2)}) async-start(), calls=%async_computation.7 | async-start | bytes 10485760 | tf_op jit(solution)/shard_map/all_gather | solution.py:300
  40.9 27.4 %collective-permute-start.11 = (bf16[4,1152]{1,0:T(4,128)(2,1)S(1)}, bf16[4,1152]{1,0:T(4,128)(2,1)S(1)}, u32[]{:S(2)}, u32[]{:S(2)}) collective-permute-start(bf16[4,1152]{1,0:T(4,128)(2,1)S(1)} %get-tuple-element.267), channel_id=1, source_target_pairs={{0,16},{2,18},{4,20},{6,22},{8,24},{10,26},{12,28},{14,30},{16,0},... | collective-permute-start | bytes 27656 | tf_op jit(solution)/shard_map/ppermute | solution.py:270
  45.7 22.6 %collective-permute-start.12 = (bf16[4,1152]{1,0:T(4,128)(2,1)S(1)}, bf16[4,1152]{1,0:T(4,128)(2,1)S(1)}, u32[]{:S(2)}, u32[]{:S(2)}) collective-permute-start(bf16[4,1152]{1,0:T(4,128)(2,1)S(1)} %get-tuple-element.267), channel_id=1, source_target_pairs={{0,24},{2,26},{4,28},{6,30},{8,0},{10,2},{12,4},{14,6},{16,8},{18,... | collective-permute-start | bytes 27656 | tf_op jit(solution)/shard_map/ppermute | solution.py:270
  52.9 31.4 %collective-permute-start.7 = (bf16[256,2,1024]{0,2,1:T(8,128)(2,1)S(1)}, bf16[256,2,1024]{0,2,1:T(8,128)(2,1)S(1)}, u32[]{:S(2)}, u32[]{:S(2)}) collective-permute-start(bf16[256,2,1024]{0,2,1:T(8,128)(2,1)S(1)} %fusion.31), channel_id=1, source_target_pairs={{0,4},{2,6},{4,0},{6,2},{8,12},{10,14},{12,8},{14,10},{16,20},{18,... | collective-permute-start | bytes 3145736 | tf_op jit(solution)/shard_map/ppermute | solution.py:267
  63.0 25.0 %collective-permute-start.5 = (bf16[2,256,1024]{2,1,0:T(8,128)(2,1)}, bf16[2,256,1024]{2,1,0:T(8,128)(2,1)}, u32[]{:S(2)}, u32[]{:S(2)}) collective-permute-start(bf16[2,256,1024]{2,1,0:T(8,128)(2,1)} %pad_maximum_fusion.5), channel_id=1, source_target_pairs={{0,1},{1,0},{2,3},{3,2},{4,5},{5,4},{6,7},{7,6},{8,9},{9,8},{10,11... | collective-permute-start | bytes 3145736 | tf_op jit(solution)/shard_map/ppermute | solution.py:273
  66.3 40.4 %collective-permute-start.3 = (bf16[256,2048]{1,0:T(8,128)(2,1)}, bf16[256,2048]{1,0:T(8,128)(2,1)}, u32[]{:S(2)}, u32[]{:S(2)}) collective-permute-start(bf16[256,2048]{1,0:T(8,128)(2,1)} %get-tuple-element.247), channel_id=1, source_target_pairs={{0,4},{2,6},{4,0},{6,2},{8,12},{10,14},{12,8},{14,10},{16,20},{18,... | collective-permute-start | bytes 3145736 | tf_op jit(solution)/shard_map/ppermute | solution.py:267
  111.1 25.8 %collective-permute-start.13 = (bf16[1024,2048]{1,0:T(8,128)(2,1)}, bf16[1024,2048]{1,0:T(8,128)(2,1)}, u32[]{:S(2)}, u32[]{:S(2)}) collective-permute-start(bf16[1024,2048]{1,0:T(8,128)(2,1)} %bitcast.16.left.left_one), channel_id=1, source_target_pairs={{0,2},{2,0},{4,6},{6,4},{8,10},{10,8},{12,14},{14,12},{16,18},{18,... | collective-permute-start | bytes 12582920 | tf_op jit(solution)/shard_map/ppermute | solution.py:264
  111.9 391.2 %reduce-scatter.5.cloned.1.call-start = ((), (), s32[]{:S(2)}) async-start(), calls=%async_computation.8 | async-start | bytes 5242880 | tf_op jit(solution)/shard_map/reduce_scatter | solution.py:436
  157.3 25.3 %collective-permute-start.15 = (bf16[2,256,1024]{2,1,0:T(8,128)(2,1)S(1)}, bf16[2,256,1024]{2,1,0:T(8,128)(2,1)S(1)}, u32[]{:S(2)}, u32[]{:S(2)}) collective-permute-start(bf16[2,256,1024]{2,1,0:T(8,128)(2,1)S(1)} %fusion.25), channel_id=1, source_target_pairs={{0,4},{2,6},{4,0},{6,2},{8,12},{10,14},{12,8},{14,10},{16,20},{18,... | collective-permute-start | bytes 3145736 | tf_op jit(solution)/shard_map/ppermute | solution.py:267
  158.9 24.9 %collective-permute-start.17 = (bf16[2,256,1024]{2,1,0:T(8,128)(2,1)S(1)}, bf16[2,256,1024]{2,1,0:T(8,128)(2,1)S(1)}, u32[]{:S(2)}, u32[]{:S(2)}) collective-permute-start(bf16[2,256,1024]{2,1,0:T(8,128)(2,1)S(1)} %fusion.26), channel_id=1, source_target_pairs={{0,1},{1,0},{2,3},{3,2},{4,5},{5,4},{6,7},{7,6},{8,9},{9,8},{10,11... | collective-permute-start | bytes 3145736 | tf_op jit(solution)/shard_map/ppermute | solution.py:273
  217.6 22.9 %collective-permute-start.22 = (bf16[2,256,1024]{2,1,0:T(8,128)(2,1)S(1)}, bf16[2,256,1024]{2,1,0:T(8,128)(2,1)S(1)}, u32[]{:S(2)}, u32[]{:S(2)}) collective-permute-start(bf16[2,256,1024]{2,1,0:T(8,128)(2,1)S(1)} %get-tuple-element.245), channel_id=1, source_target_pairs={{0,1},{1,0},{2,3},{3,2},{4,5},{5,4},{6,7},{7,6},{8,9},{9,8},{10,11... | collective-permute-start | bytes 3145736 | tf_op jit(solution)/shard_map/ppermute | solution.py:273
  219.3 22.2 %collective-permute-start.20 = (bf16[2,256,1024]{2,1,0:T(8,128)(2,1)S(1)}, bf16[2,256,1024]{2,1,0:T(8,128)(2,1)S(1)}, u32[]{:S(2)}, u32[]{:S(2)}) collective-permute-start(bf16[2,256,1024]{2,1,0:T(8,128)(2,1)S(1)} %get-tuple-element.239), channel_id=1, source_target_pairs={{0,4},{2,6},{4,0},{6,2},{8,12},{10,14},{12,8},{14,10},{16,20},{18,... | collective-permute-start | bytes 3145736 | tf_op jit(solution)/shard_map/ppermute | solution.py:267
  310.1 43.6 %collective-permute-start.29 = (bf16[256,1024]{1,0:T(8,128)(2,1)}, bf16[256,1024]{1,0:T(8,128)(2,1)}, u32[]{:S(2)}, u32[]{:S(2)}) collective-permute-start(bf16[256,1024]{1,0:T(8,128)(2,1)} %constant_dynamic-slice_fusion.9), channel_id=1, source_target_pairs={{0,1},{1,0},{2,3},{3,2},{4,5},{5,4},{6,7},{7,6},{8,9},{9,8},{10,11... | collective-permute-start | bytes 1572872 | tf_op jit(solution)/shard_map/ppermute | solution.py:273
  323.3 24.9 %collective-permute-start.25 = (bf16[2,256,1024]{2,1,0:T(8,128)(2,1)S(1)}, bf16[2,256,1024]{2,1,0:T(8,128)(2,1)S(1)}, u32[]{:S(2)}, u32[]{:S(2)}) collective-permute-start(bf16[2,256,1024]{2,1,0:T(8,128)(2,1)S(1)} %fusion.27), channel_id=1, source_target_pairs={{0,4},{2,6},{4,0},{6,2},{8,12},{10,14},{12,8},{14,10},{16,20},{18,... | collective-permute-start | bytes 3145736 | tf_op jit(solution)/shard_map/ppermute | solution.py:267
  324.8 24.6 %collective-permute-start.27 = (bf16[2,256,1024]{2,1,0:T(8,128)(2,1)S(1)}, bf16[2,256,1024]{2,1,0:T(8,128)(2,1)S(1)}, u32[]{:S(2)}, u32[]{:S(2)}) collective-permute-start(bf16[2,256,1024]{2,1,0:T(8,128)(2,1)S(1)} %fusion.28), channel_id=1, source_target_pairs={{0,1},{1,0},{2,3},{3,2},{4,5},{5,4},{6,7},{7,6},{8,9},{9,8},{10,11... | collective-permute-start | bytes 3145736 | tf_op jit(solution)/shard_map/ppermute | solution.py:273
  380.0 23.4 %collective-permute-start.33 = (bf16[2,256,1024]{2,1,0:T(8,128)(2,1)S(1)}, bf16[2,256,1024]{2,1,0:T(8,128)(2,1)S(1)}, u32[]{:S(2)}, u32[]{:S(2)}) collective-permute-start(bf16[2,256,1024]{2,1,0:T(8,128)(2,1)S(1)} %get-tuple-element.237), channel_id=1, source_target_pairs={{0,1},{1,0},{2,3},{3,2},{4,5},{5,4},{6,7},{7,6},{8,9},{9,8},{10,11... | collective-permute-start | bytes 3145736 | tf_op jit(solution)/shard_map/ppermute | solution.py:273
  382.9 20.6 %collective-permute-start.31 = (bf16[2,256,1024]{2,1,0:T(8,128)(2,1)S(1)}, bf16[2,256,1024]{2,1,0:T(8,128)(2,1)S(1)}, u32[]{:S(2)}, u32[]{:S(2)}) collective-permute-start(bf16[2,256,1024]{2,1,0:T(8,128)(2,1)S(1)} %get-tuple-element.231), channel_id=1, source_target_pairs={{0,4},{2,6},{4,0},{6,2},{8,12},{10,14},{12,8},{14,10},{16,20},{18,... | collective-permute-start | bytes 3145736 | tf_op jit(solution)/shard_map/ppermute | solution.py:267
  428.7 157.9 %reduce-scatter.7.cloned.1.call-start = ((), (), s32[]{:S(2)}) async-start(), calls=%async_computation.9 | async-start | bytes 5242880 | tf_op jit(solution)/shard_map/reduce_scatter | solution.py:436
  455.5 25.7 %collective-permute-start.36 = (bf16[2,256,1024]{2,1,0:T(8,128)(2,1)}, bf16[2,256,1024]{2,1,0:T(8,128)(2,1)}, u32[]{:S(2)}, u32[]{:S(2)}) collective-permute-start(bf16[2,256,1024]{2,1,0:T(8,128)(2,1)} %fusion.29), channel_id=1, source_target_pairs={{0,4},{2,6},{4,0},{6,2},{8,12},{10,14},{12,8},{14,10},{16,20},{18,... | collective-permute-start | bytes 3145736 | tf_op jit(solution)/shard_map/ppermute | solution.py:267
  458.7 25.6 %collective-permute-start.38 = (bf16[2,256,1024]{2,1,0:T(8,128)(2,1)}, bf16[2,256,1024]{2,1,0:T(8,128)(2,1)}, u32[]{:S(2)}, u32[]{:S(2)}) collective-permute-start(bf16[2,256,1024]{2,1,0:T(8,128)(2,1)} %fusion.30), channel_id=1, source_target_pairs={{0,1},{1,0},{2,3},{3,2},{4,5},{5,4},{6,7},{7,6},{8,9},{9,8},{10,11... | collective-permute-start | bytes 3145736 | tf_op jit(solution)/shard_map/ppermute | solution.py:273
  491.7 170.6 %reduce-scatter.11.cloned.1.call-start = ((), (), s32[]{:S(2)}) async-start(), calls=%async_computation.11 | async-start | bytes 1310720 | tf_op jit(solution)/shard_map/reduce_scatter | solution.py:436
  524.0 24.0 %collective-permute-start.43 = (bf16[2,256,1024]{2,1,0:T(8,128)(2,1)S(1)}, bf16[2,256,1024]{2,1,0:T(8,128)(2,1)S(1)}, u32[]{:S(2)}, u32[]{:S(2)}) collective-permute-start(bf16[2,256,1024]{2,1,0:T(8,128)(2,1)S(1)} %get-tuple-element.229), channel_id=1, source_target_pairs={{0,1},{1,0},{2,3},{3,2},{4,5},{5,4},{6,7},{7,6},{8,9},{9,8},{10,11... | collective-permute-start | bytes 3145736 | tf_op jit(solution)/shard_map/ppermute | solution.py:273
  525.7 23.9 %collective-permute-start.41 = (bf16[2,256,1024]{2,1,0:T(8,128)(2,1)S(1)}, bf16[2,256,1024]{2,1,0:T(8,128)(2,1)S(1)}, u32[]{:S(2)}, u32[]{:S(2)}) collective-permute-start(bf16[2,256,1024]{2,1,0:T(8,128)(2,1)S(1)} %get-tuple-element.223), channel_id=1, source_target_pairs={{0,4},{2,6},{4,0},{6,2},{8,12},{10,14},{12,8},{14,10},{16,20},{18,... | collective-permute-start | bytes 3145736 | tf_op jit(solution)/shard_map/ppermute | solution.py:267
  594.1 28.4 %collective-permute-start.47 = (bf16[1024,2048]{1,0:T(8,128)(2,1)}, bf16[1024,2048]{1,0:T(8,128)(2,1)}, u32[]{:S(2)}, u32[]{:S(2)}) collective-permute-start(bf16[1024,2048]{1,0:T(8,128)(2,1)} %shard_map.284), channel_id=1, source_target_pairs={{0,2},{2,0},{4,6},{6,4},{8,10},{10,8},{12,14},{14,12},{16,18},{18,... | collective-permute-start | bytes 12582920 | tf_op jit(solution)/shard_map/ppermute | solution.py:264
  597.7 109.5 %reduce-scatter.9.cloned.1.call-start = ((), (), s32[]{:S(2)}) async-start(), calls=%async_computation.10 | async-start | bytes 3932160 | tf_op jit(solution)/shard_map/reduce_scatter | solution.py:436
  599.7 22.8 %collective-permute-start.46 = (bf16[256,1,1024]{2,0,1:T(8,128)(2,1)}, bf16[256,1,1024]{2,0,1:T(8,128)(2,1)}, u32[]{:S(2)}, u32[]{:S(2)}) collective-permute-start(bf16[256,1,1024]{2,0,1:T(8,128)(2,1)} %dynamic-slice_bitcast_fusion), channel_id=1, source_target_pairs={{0,4},{2,6},{4,0},{6,2},{8,12},{10,14},{12,8},{14,10},{16,20},{18,... | collective-permute-start | bytes 1572872 | tf_op jit(solution)/shard_map/ppermute | solution.py:267
  625.9 25.3 %collective-permute-start.50 = (bf16[2,512,512]{2,1,0:T(8,128)(2,1)}, bf16[2,512,512]{2,1,0:T(8,128)(2,1)}, u32[]{:S(2)}, u32[]{:S(2)}) collective-permute-start(bf16[2,512,512]{2,1,0:T(8,128)(2,1)} %add_convert_fusion), channel_id=1, source_target_pairs={{0,1},{1,0},{2,3},{3,2},{4,5},{5,4},{6,7},{7,6},{8,9},{9,8},{10,11... | collective-permute-start | bytes 3145736 | tf_op jit(solution)/shard_map/ppermute | solution.py:273
  631.6 25.1 %collective-permute-start.48 = (bf16[512,1024]{1,0:T(8,128)(2,1)}, bf16[512,1024]{1,0:T(8,128)(2,1)}, u32[]{:S(2)}, u32[]{:S(2)}) collective-permute-start(bf16[512,1024]{1,0:T(8,128)(2,1)} %add_convert_fusion.1), channel_id=1, source_target_pairs={{0,4},{2,6},{4,0},{6,2},{8,12},{10,14},{12,8},{14,10},{16,20},{18,... | collective-permute-start | bytes 3145736 | tf_op jit(solution)/shard_map/ppermute | solution.py:267
  700.7 26.5 %collective-permute-start.54 = (bf16[256,1024]{1,0:T(8,128)(2,1)S(1)}, bf16[256,1024]{1,0:T(8,128)(2,1)S(1)}, u32[]{:S(2)}, u32[]{:S(2)}) collective-permute-start(bf16[256,1024]{1,0:T(8,128)(2,1)S(1)} %copy-done.81), channel_id=1, source_target_pairs={{0,1},{1,0},{2,3},{3,2},{4,5},{5,4},{6,7},{7,6},{8,9},{9,8},{10,11... | collective-permute-start | bytes 1572872 | tf_op jit(solution)/shard_map/ppermute | solution.py:273
  702.3 28.5 %all-to-all-start.1 = ((bf16[32,16,1024]{2,0,1:T(8,128)(2,1)}), bf16[32,16,1024]{2,0,1:T(8,128)(2,1)}, u32[]{:S(2)}, u32[]{:S(2)}) async-start(bf16[32,16,1024]{2,0,1:T(8,128)(2,1)} %copy.170), calls=%async_computation.3 | async-start | bytes 2097152 | tf_op jit(solution)/shard_map/all_to_all | solution.py:566
  (135 other events, 922.7 us)
Sparse Core Ops, SparseCore 0:
  40.9 83.5 all-gather.2
  126.1 148.1 all-gather.4
  428.8 73.4 reduce-scatter.4
  504.5 77.2 reduce-scatter.6
  597.8 26.7 reduce-scatter.10
  634.9 60.6 reduce-scatter.8

commit v4 on v3

--- a/solution.py
+++ b/solution.py
@@ -302,9 +302,6 @@
     first_weights = jnp.concatenate([qkv_weight, out_weight.T[None]], axis=0).swapaxes(0, 1)
     first_piece = split_weight(first_weights)
     first_full = gather_weight(first_piece)
-    second_weights = after(up_weight, first_piece), after(down_weight, first_piece).T
-    second_piece = split_weight(jnp.stack(second_weights, axis=1))
-    second_full = gather_weight(second_piece)
 
     small = jnp.concatenate(
         [
@@ -334,6 +331,9 @@
     sending = jnp.take(local_rows, dealing, axis=1)
     arrived = lax.all_to_all(sending, "dp", split_axis=1, concat_axis=1, tiled=True)
     tokens = after(arrived, first_piece).reshape(seq_len, half)
+    second_weights = after(up_weight, arrived), after(down_weight, arrived).T
+    second_piece = split_weight(jnp.stack(second_weights, axis=1))
+    second_full = gather_weight(second_piece)
     early, late = tokens[:token_half], tokens[token_half:]
     early = in_order(lane, early, lane_swap(early), 1)
     early = jnp.stack([early, side_swap(early)])
@@ -466,14 +466,11 @@
     out_bias_grad = jnp.sum(attended_low, axis=0, dtype=wide)
     attended_grad = group_gather(attended_low)
     down_sum = side_send(down_sum, 1)
-    stacked = []
+    stacked, parts_grad = [], []
     for i in range(2):
-        rows = attended_grad[i]
+        rows = after(attended_grad[i], *parts_grad)
         if i:
-            attended_grad = (attended_grad[0], after(rows, *stacked, down_sum[1]))
-            out_partial = pair_matmul(attended_grad, context)
-            out_sum = scatter(out_partial)
-            rows = after(attended_grad[1], out_partial)
+            rows = after(rows, down_sum[1])
         context_grad = matmul(rows, first_full, 0, features, 3 * features)
         stacked.append(
             by_sequence(
@@ -485,13 +482,15 @@
                 context_grad,
             )
         )
-    theirs = matmul(after(stacked[1], up_sum), first_full, 1, width)
+        parts_grad.append(matmul(stacked[i], first_full, 1, width))
+    mine, theirs = parts_grad
     qkv_partial = pair_matmul(all_rows, [after(grads, theirs) for grads in stacked])
     qkv_sum = scatter(qkv_partial)
     theirs = core_swap(theirs)
-    mine = matmul(after(stacked[0], qkv_partial), first_full, 1, width)
     up_sum = side_send(up_sum, 1)
-
+    out_partial = pair_matmul(attended_grad, [after(rows, qkv_partial) for rows in context])
+    out_sum = scatter(out_partial)
+    theirs = after(theirs, out_partial, up_sum[1])
     quarter = half // 2
     both = tuple(array.reshape(2, seq_len, width) for array in (after(mine, up_sum[1]), theirs))
 
@@ -515,18 +514,19 @@
     two = summed(of_lane(lane)) + two.astype(wide)
     one_sent = take(one, (1 - lane) * quarter, quarter, 1).astype(low)
     two_sent = two[1].astype(low)
-    one = take(one, lane * quarter, quarter, 1) + lane_swap_rows(one_sent).astype(wide)
+    down_weight_grad = core_join(after(side_join(*down_sum), one_sent))[:, 0].T
+    up_weight_grad = core_join(after(side_join(*up_sum), one_sent))[:, 0]
+    one_theirs = after(lane_swap(one_sent), down_weight_grad, up_weight_grad)
+    one_theirs = jnp.concatenate([one_theirs[token_half:], one_theirs[:token_half]], axis=0)
+    one = take(one, lane * quarter, quarter, 1) + one_theirs.astype(wide)
     two = two[0] + side_swap(two_sent).astype(wide)
     own_attended = take(attended_grad[0][:seq_len], lane * half, half, 1)
     in_half = (jnp.concatenate([one, two], axis=1) + own_attended.astype(wide)).astype(low)
     in_half = in_order(lane, in_half[:token_half], in_half[token_half:], 0)
-    down_weight_grad = core_join(after(side_join(*down_sum), one_sent))[:, 0].T
-    up_weight_grad = core_join(after(side_join(*up_sum), one_sent))[:, 0]
-    in_half = after(in_half, down_weight_grad, up_weight_grad)
-    back_rows = in_half.reshape(per_peer, groups, half)
+    back_rows = after(in_half, qkv_sum).reshape(per_peer, groups, half)
     out_keep, out_send = parts(final.astype(low), lane, 1)
-    outputs = in_order(lane, out_keep, lane_swap(after(out_send, back_rows)), 0)
-    qkv_bias_sum = sum(jnp.sum(after(s, back_rows), axis=0, dtype=wide) for s in stacked)
+    outputs = in_order(lane, out_keep, lane_swap(after(out_send, qkv_sum)), 0)
+    qkv_bias_sum = sum(jnp.sum(after(s, two_sent), axis=0, dtype=wide) for s in stacked)
     qkv_bias_sum = qkv_bias_sum.reshape(3, features)
     qv_grad = jnp.stack([qkv_bias_sum[0], qkv_bias_sum[2]])
     def spread(mine, size):
@@ -561,7 +561,7 @@
         .reshape(groups, -1)
     )
     packed = jnp.concatenate([qv_spread, up_spread, vector_spread], axis=1)
-    packed = after(packed, back_rows)
+    packed = after(packed, qkv_sum)
 
     returned = lax.all_to_all(back_rows, "dp", split_axis=1, concat_axis=1, tiled=True)
     inverse_order = (
@@ -569,7 +569,7 @@
     )
     in_grad = jnp.take(returned, inverse_order, axis=1).swapaxes(0, 1).reshape(seq_len, half)
 
-    out_weight_grad = core_join(side_join(*side_send(after(out_sum, two_sent), 1)))[:, 0].T
+    out_weight_grad = core_join(side_join(*side_send(after(out_sum, qkv_sum), 1)))[:, 0].T
     qkv_grad = core_join(side_join(*side_send(qkv_sum, 3))).swapaxes(0, 1)
 
     packed = packed.reshape(ring_size, 2, 2, packed.shape[1])

time: 750 us -> 740 us (0.987)
  local copies, waits for them, and re-layouts: 98.6 us -> 89.7 us
    ppermute x24, waiting for transfers between devices: 186 us -> 166 us  [side_swap(): return lax.ppermute(array, 'dp', side_pairs)]
    ppermute x19, waiting for transfers between devices: 87.1 us -> 107 us  [lane_swap(): return lax.ppermute(array, 'tensor', [(0, 1), (1, 0)])]
    ppermute x6, waiting for transfers between devices: 1.03 us -> 10.4 us  [ring_send(): lax.ppermute(array, 'dp', [(i, (i + 4 * steps) % groups) for i in range(g...]
    all_gather x2, waiting for transfers between devices: 41.1 us -> 31.8 us  [gather_weight(): lax.all_gather(piece, 'dp', axis=0, axis_index_groups=ring_groups, tiled=...]
    unnamed x201 -> x181, local copies, waits for them, and re-layouts: 54 us -> 45.7 us
  transfers between devices with their start and end apart: 73 -> 73, of which waited for: 41 -> 42; matrix products, arithmetic and copies ran while one was open for 17% -> 17% of each run, Pallas kernels for 15% -> 16%
where the time goes in v4:
time: 740 us; the launch traced here: 731 us
  waiting for transfers between devices  326 us (44%)
  Pallas kernels  144 us (19%)
  local copies, waits for them, and re-layouts  89.7 us (12%)
  other arithmetic  81.7 us (11%)
  starting transfers between devices  73.3 us (10%)
  between operations  16.5 us (2%)
    ppermute x24, waiting for transfers between devices, side_swap(): return lax.ppermute(array, 'dp', side_pairs)  166 us
    ppermute x19, waiting for transfers between devices, lane_swap(): return lax.ppermute(array, 'tensor', [(0, 1), (1, 0)])  107 us
    pallas_call x12, Pallas kernels, matmul(): call(functools.partial(matmul_kernel, right_axis), 2 * rows * depth * siz...  56.4 us
    unnamed x181, local copies, waits for them, and re-layouts  45.7 us
    pallas_call x4, Pallas kernels, pair_matmul(): call(pair_kernel, 4 * rows * depth * columns, jax.ShapeDtypeStruct((depth...  39.5 us
    all_gather x2, waiting for transfers between devices, gather_weight(): lax.all_gather(piece, 'dp', axis=0, axis_index_groups=ring_groups, tiled=...  31.8 us
    ppermute x24, starting transfers between devices, side_swap(): return lax.ppermute(array, 'dp', side_pairs)  28.6 us
    ppermute x19, starting transfers between devices, lane_swap(): return lax.ppermute(array, 'tensor', [(0, 1), (1, 0)])  20.8 us
  transfers between devices with their start and end apart: 73, of which 42 were waited for; matrix products, arithmetic and copies ran while one was open for 17% of the time, Pallas kernels for 16%

profile of v4, /device:TPU:0, one launch (start us, length us, event | category | flops | bytes accessed | tf_op | source)
XLA Modules:
  0.0 730.6 jit_solution(2983841348282510313)
XLA Ops:
  53.1 8.8 %collective-permute-done.4 = bf16[256,1024]{1,0:T(8,128)(2,1)} collective-permute-done((bf16[256,1024]{1,0:T(8,128)(2,1)S(1)}, bf16[256,1024]{1,0:T(8,128)(2,1)}, u32[]{:S(2)}, u32[]{:S(2)}) %collective-permute-start.4) | collective-permute-done | bytes 524320 | tf_op jit(solution)/shard_map/ppermute | solution.py:267
  68.7 19.7 %collective-permute-done.5 = bf16[2,256,1024]{2,1,0:T(8,128)(2,1)S(1)} collective-permute-done((bf16[2,256,1024]{2,1,0:T(8,128)(2,1)S(1)}, bf16[2,256,1024]{2,1,0:T(8,128)(2,1)S(1)}, u32[]{:S(2)}, u32[]{:S(2)}) %collective-permute-start.5) | collective-permute-done | bytes 1048608 | tf_op jit(solution)/shard_map/ppermute | solution.py:273
  95.5 18.1 %collective-permute-done.7 = bf16[256,2,1024]{0,2,1:T(8,128)(2,1)S(1)} collective-permute-done((bf16[256,2,1024]{0,2,1:T(8,128)(2,1)S(1)}, bf16[256,2,1024]{0,2,1:T(8,128)(2,1)S(1)}, u32[]{:S(2)}, u32[]{:S(2)}) %collective-permute-start.7) | collective-permute-done | bytes 1048608 | tf_op jit(solution)/shard_map/ppermute | solution.py:267
  133.5 6.5 shard_map.266.query.key.value
  156.9 22.1 %collective-permute-done.15 = bf16[2,256,1024]{2,1,0:T(8,128)(2,1)S(1)} collective-permute-done((bf16[2,256,1024]{2,1,0:T(8,128)(2,1)S(1)}, bf16[2,256,1024]{2,1,0:T(8,128)(2,1)S(1)}, u32[]{:S(2)}, u32[]{:S(2)}) %collective-permute-start.15) | collective-permute-done | bytes 1048608 | tf_op jit(solution)/shard_map/ppermute | solution.py:267
  185.7 10.2 %collective-permute-done.18 = bf16[256,1024]{1,0:T(8,128)(2,1)} collective-permute-done((bf16[256,1024]{1,0:T(8,128)(2,1)}, bf16[256,1024]{1,0:T(8,128)(2,1)}, u32[]{:S(2)}, u32[]{:S(2)}) %collective-permute-start.18) | collective-permute-done | bytes 524320 | tf_op jit(solution)/shard_map/ppermute | solution.py:267
  204.5 9.4 %collective-permute-done.21 = bf16[256,1024]{1,0:T(8,128)(2,1)S(1)} collective-permute-done((bf16[256,1024]{1,0:T(8,128)(2,1)S(1)}, bf16[256,1024]{1,0:T(8,128)(2,1)S(1)}, u32[]{:S(2)}, u32[]{:S(2)}) %collective-permute-start.21) | collective-permute-done | bytes 524320 | tf_op jit(solution)/shard_map/ppermute | solution.py:267
  216.9 20.0 %collective-permute-done.22 = bf16[2,256,1024]{2,1,0:T(8,128)(2,1)S(1)} collective-permute-done((bf16[2,256,1024]{2,1,0:T(8,128)(2,1)S(1)}, bf16[2,256,1024]{2,1,0:T(8,128)(2,1)S(1)}, u32[]{:S(2)}, u32[]{:S(2)}) %collective-permute-start.22) | collective-permute-done | bytes 1048608 | tf_op jit(solution)/shard_map/ppermute | solution.py:273
  240.7 29.9 %all-gather.5.cloned.1.call-done.weight.right = bf16[2048,2048]{1,0:T(8,128)(2,1)} async-done(((bf16[512,2048]{1,0:T(8,128)(2,1)}), bf16[2048,2048]{1,0:T(8,128)(2,1)}) %all-gather.5.cloned.1.call-update) | async-done | bytes 8388624 | tf_op jit(solution)/shard_map/all_gather | solution.py:300
  273.9 7.6 %shard_map.269 = (f32[1024,1024]{1,0:T(8,128)S(1)}, bf16[1024,1024]{1,0:T(8,128)(2,1)S(1)}) custom-call(bf16[1024,2048]{1,0:T(8,128)(2,1)S(1)} %bitcast.319, bf16[2048,2048]{1,0:T(8,128)(2,1)} %all-gather.5.cloned.1.call-done.weight.right, f32[1,1024]{1,0:T(1,128)S(1)} %bitcast.332), custom_call_target="tpu_custom_call" | custom-call | flops 536870912 | tf_op jit(solution)/shard_map/pallas_call | solution.py:177
  284.8 8.8 %shard_map.271 = (f32[1024,1024]{1,0:T(8,128)S(1)}, bf16[1024,1024]{1,0:T(8,128)(2,1)S(1)}) custom-call(bf16[1024,2048]{1,0:T(8,128)(2,1)} %collective-permute-done.23.rows.left_two, bf16[2048,2048]{1,0:T(8,128)(2,1)} %all-gather.5.cloned.1.call-done.weight.right, f32[1,1024]{1,0:T(1,128)S(1)} %bitcast.333), custom_call_target="tpu_custom_call" | custom-call | flops 536870912 | tf_op jit(solution)/shard_map/pallas_call | solution.py:177
  295.6 8.6 %shard_map.272 = bf16[1024,2048]{1,0:T(8,128)(2,1)} custom-call(bf16[1024,1024]{1,0:T(8,128)(2,1)S(1)} %get-tuple-element.70.left.right_two, bf16[2048,2048]{1,0:T(8,128)(2,1)} %all-gather.5.cloned.1.call-done.weight.right), custom_call_target="tpu_custom_call" | custom-call | flops 536870912 | tf_op jit(solution)/shard_map/pallas_call | solution.py:149
  309.5 6.7 shard_map.270
  328.0 16.6 %collective-permute-done.25 = bf16[2,256,1024]{2,1,0:T(8,128)(2,1)S(1)} collective-permute-done((bf16[2,256,1024]{2,1,0:T(8,128)(2,1)S(1)}, bf16[2,256,1024]{2,1,0:T(8,128)(2,1)S(1)}, u32[]{:S(2)}, u32[]{:S(2)}) %collective-permute-start.25) | collective-permute-done | bytes 1048608 | tf_op jit(solution)/shard_map/ppermute | solution.py:267
  351.4 9.8 %collective-permute-done.28 = bf16[256,1024]{1,0:T(8,128)(2,1)S(1)} collective-permute-done((bf16[256,1024]{1,0:T(8,128)(2,1)S(1)}, bf16[256,1024]{1,0:T(8,128)(2,1)S(1)}, u32[]{:S(2)}, u32[]{:S(2)}) %collective-permute-start.28) | collective-permute-done | bytes 524320 | tf_op jit(solution)/shard_map/ppermute | solution.py:267
  367.1 9.2 %collective-permute-done.32 = bf16[256,1024]{1,0:T(8,128)(2,1)S(1)} collective-permute-done((bf16[256,1024]{1,0:T(8,128)(2,1)S(1)}, bf16[256,1024]{1,0:T(8,128)(2,1)S(1)}, u32[]{:S(2)}, u32[]{:S(2)}) %collective-permute-start.32) | collective-permute-done | bytes 524320 | tf_op jit(solution)/shard_map/ppermute | solution.py:267
  379.4 20.5 %collective-permute-done.33 = bf16[2,256,1024]{2,1,0:T(8,128)(2,1)S(1)} collective-permute-done((bf16[2,256,1024]{2,1,0:T(8,128)(2,1)S(1)}, bf16[2,256,1024]{2,1,0:T(8,128)(2,1)S(1)}, u32[]{:S(2)}, u32[]{:S(2)}) %collective-permute-start.33) | collective-permute-done | bytes 1048608 | tf_op jit(solution)/shard_map/ppermute | solution.py:273
  401.0 6.8 shard_map.273
  411.2 11.9 %shard_map.275 = bf16[2048,1024]{1,0:T(8,128)(2,1)S(1)} custom-call(bf16[1024,2048]{1,0:T(8,128)(2,1)S(1)} %bitcast.317, bf16[1024,1024]{1,0:T(8,128)(2,1)S(1)} %copy-done.25, bf16[1024,2048]{1,0:T(8,128)(2,1)} %copy-done.17, bf16[1024,1024]{1,0:T(8,128)(2,1)S(1)} %copy-done.27), custom_call_target="tpu_custom_call" | custom-call | flops 1073741824 | tf_op jit(solution)/shard_map/pallas_call | solution.py:226
  429.5 6.9 shard_map.276
  436.4 6.9 shard_map.277
  443.6 6.7 shard_map.274
  455.7 11.8 %shard_map.278 = bf16[2048,1024]{1,0:T(8,128)(2,1)S(1)} custom-call(bf16[1024,2048]{1,0:T(8,128)(2,1)S(1)} %bitcast.320, bf16[1024,1024]{1,0:T(8,128)(2,1)S(1)} %copy-done.29, bf16[1024,2048]{1,0:T(8,128)(2,1)} %collective-permute-done.23.rows.left_two, bf16[1024,1024]{1,0:T(8,128)(2,1)S(1)} %get-tuple-element.82.left.right_two), custom_call_target="tpu_custom_call" | custom-call | flops 1073741824 | tf_op jit(solution)/shard_map/pallas_call | solution.py:226
  469.6 8.0 %collective-permute-done.36 = bf16[2,256,1024]{2,1,0:T(8,128)(2,1)} collective-permute-done((bf16[2,256,1024]{2,1,0:T(8,128)(2,1)}, bf16[2,256,1024]{2,1,0:T(8,128)(2,1)}, u32[]{:S(2)}, u32[]{:S(2)}) %collective-permute-start.36) | collective-permute-done | bytes 1048608 | tf_op jit(solution)/shard_map/ppermute | solution.py:267
  488.2 11.4 %collective-permute-done.39 = bf16[256,1024]{1,0:T(8,128)(2,1)} collective-permute-done((bf16[256,1024]{1,0:T(8,128)(2,1)}, bf16[256,1024]{1,0:T(8,128)(2,1)}, u32[]{:S(2)}, u32[]{:S(2)}) %collective-permute-start.39) | collective-permute-done | bytes 524320 | tf_op jit(solution)/shard_map/ppermute | solution.py:267
  509.6 10.8 %collective-permute-done.42 = bf16[256,1024]{1,0:T(8,128)(2,1)S(1)} collective-permute-done((bf16[256,1024]{1,0:T(8,128)(2,1)S(1)}, bf16[256,1024]{1,0:T(8,128)(2,1)S(1)}, u32[]{:S(2)}, u32[]{:S(2)}) %collective-permute-start.42) | collective-permute-done | bytes 524320 | tf_op jit(solution)/shard_map/ppermute | solution.py:267
  523.7 20.7 %collective-permute-done.43 = bf16[2,256,1024]{2,1,0:T(8,128)(2,1)S(1)} collective-permute-done((bf16[2,256,1024]{2,1,0:T(8,128)(2,1)S(1)}, bf16[2,256,1024]{2,1,0:T(8,128)(2,1)S(1)}, u32[]{:S(2)}, u32[]{:S(2)}) %collective-permute-start.43) | collective-permute-done | bytes 1048608 | tf_op jit(solution)/shard_map/ppermute | solution.py:273
  578.9 9.9 %shard_map.285 = bf16[2048,768]{1,0:T(8,128)(2,1)S(1)} custom-call(bf16[1024,2048]{1,0:T(8,128)(2,1)S(1)} %bitcast.311, bf16[1024,768]{1,0:T(8,128)(2,1)S(1)} %shard_map.280.left.right_one, bf16[1024,2048]{1,0:T(8,128)(2,1)} %collective-permute-done.13.left.left_two, bf16[1024,768]{1,0:T(8,128)(2,1)S(1)} %shard_map.283.left.right_two), custom_call_target="tpu_custom_call" | custom-call | flops 805306368 | tf_op jit(solution)/shard_map/pallas_call | solution.py:226
  601.1 8.2 %collective-permute-done.47 = bf16[256,1,1024]{2,0,1:T(8,128)(2,1)} collective-permute-done((bf16[256,1,1024]{2,0,1:T(8,128)(2,1)}, bf16[256,1,1024]{2,0,1:T(8,128)(2,1)}, u32[]{:S(2)}, u32[]{:S(2)}) %collective-permute-start.47) | collective-permute-done | bytes 524320 | tf_op jit(solution)/shard_map/ppermute | solution.py:267
  628.9 14.0 %collective-permute-done.53 = bf16[2,512,512]{2,1,0:T(8,128)(2,1)} collective-permute-done((bf16[2,512,512]{2,1,0:T(8,128)(2,1)}, bf16[2,512,512]{2,1,0:T(8,128)(2,1)}, u32[]{:S(2)}, u32[]{:S(2)}) %collective-permute-start.53) | collective-permute-done | bytes 1048608 | tf_op jit(solution)/shard_map/ppermute | solution.py:273
  684.3 6.9 collective-permute-done.58
  701.6 7.1 collective-permute-done.60
  (528 shorter events, 333.5 us)
Async XLA Ops:
  13.8 18.3 %collective-permute-start.1 = (bf16[256,4,256]{2,0,1:T(8,128)(2,1)}, bf16[256,4,256]{2,0,1:T(8,128)(2,1)}, u32[]{:S(2)}, u32[]{:S(2)}) collective-permute-start(bf16[256,4,256]{2,0,1:T(8,128)(2,1)} %fusion.53), channel_id=1, source_target_pairs={{0,4},{2,6},{4,0},{6,2},{8,12},{10,14},{12,8},{14,10},{16,20},{18,... | collective-permute-start | bytes 1572872 | tf_op jit(solution)/shard_map/ppermute | solution.py:267
  18.5 27.9 %all-to-all-start = ((bf16[32,16,1024]{2,0,1:T(8,128)(2,1)}), bf16[32,16,1024]{2,0,1:T(8,128)(2,1)S(1)}, u32[]{:S(2)}, u32[]{:S(2)}) async-start(bf16[32,16,1024]{2,0,1:T(8,128)(2,1)} %select_bitcast_fusion), calls=%async_computation | async-start | bytes 2097152 | tf_op jit(solution)/shard_map/all_to_all | solution.py:332
  23.5 97.4 %all-gather.3.cloned.1.call-start = ((), (), s32[]{:S(2)}) async-start(), calls=%async_computation.6 | async-start | bytes 5242880 | tf_op jit(solution)/shard_map/all_gather | solution.py:300
  37.1 233.6 %all-gather.5.cloned.1.call-start = ((), (), s32[]{:S(2)}) async-start(), calls=%async_computation.7 | async-start | bytes 10485760 | tf_op jit(solution)/shard_map/all_gather | solution.py:300
  45.5 23.2 %collective-permute-start.12 = (bf16[4,1152]{1,0:T(4,128)(2,1)S(1)}, bf16[4,1152]{1,0:T(4,128)(2,1)S(1)}, u32[]{:S(2)}, u32[]{:S(2)}) collective-permute-start(bf16[4,1152]{1,0:T(4,128)(2,1)S(1)} %get-tuple-element.271), channel_id=1, source_target_pairs={{0,24},{2,26},{4,28},{6,30},{8,0},{10,2},{12,4},{14,6},{16,8},{18,... | collective-permute-start | bytes 27656 | tf_op jit(solution)/shard_map/ppermute | solution.py:270
  63.1 25.3 %collective-permute-start.5 = (bf16[2,256,1024]{2,1,0:T(8,128)(2,1)S(1)}, bf16[2,256,1024]{2,1,0:T(8,128)(2,1)S(1)}, u32[]{:S(2)}, u32[]{:S(2)}) collective-permute-start(bf16[2,256,1024]{2,1,0:T(8,128)(2,1)S(1)} %pad_maximum_fusion.5), channel_id=1, source_target_pairs={{0,1},{1,0},{2,3},{3,2},{4,5},{5,4},{6,7},{7,6},{8,9},{9,8},{10,11... | collective-permute-start | bytes 3145736 | tf_op jit(solution)/shard_map/ppermute | solution.py:273
  66.0 26.1 %collective-permute-start.3 = (bf16[256,2048]{1,0:T(8,128)(2,1)S(1)}, bf16[256,2048]{1,0:T(8,128)(2,1)S(1)}, u32[]{:S(2)}, u32[]{:S(2)}) collective-permute-start(bf16[256,2048]{1,0:T(8,128)(2,1)S(1)} %get-tuple-element.251), channel_id=1, source_target_pairs={{0,4},{2,6},{4,0},{6,2},{8,12},{10,14},{12,8},{14,10},{16,20},{18,... | collective-permute-start | bytes 3145736 | tf_op jit(solution)/shard_map/ppermute | solution.py:267
  68.6 45.0 %collective-permute-start.7 = (bf16[256,2,1024]{0,2,1:T(8,128)(2,1)S(1)}, bf16[256,2,1024]{0,2,1:T(8,128)(2,1)S(1)}, u32[]{:S(2)}, u32[]{:S(2)}) collective-permute-start(bf16[256,2,1024]{0,2,1:T(8,128)(2,1)S(1)} %fusion.31), channel_id=1, source_target_pairs={{0,4},{2,6},{4,0},{6,2},{8,12},{10,14},{12,8},{14,10},{16,20},{18,... | collective-permute-start | bytes 3145736 | tf_op jit(solution)/shard_map/ppermute | solution.py:267
  117.5 382.1 %reduce-scatter.5.cloned.1.call-start = ((), (), s32[]{:S(2)}) async-start(), calls=%async_computation.8 | async-start | bytes 5242880 | tf_op jit(solution)/shard_map/reduce_scatter | solution.py:436
  153.8 25.3 %collective-permute-start.15 = (bf16[2,256,1024]{2,1,0:T(8,128)(2,1)S(1)}, bf16[2,256,1024]{2,1,0:T(8,128)(2,1)S(1)}, u32[]{:S(2)}, u32[]{:S(2)}) collective-permute-start(bf16[2,256,1024]{2,1,0:T(8,128)(2,1)S(1)} %fusion.25), channel_id=1, source_target_pairs={{0,4},{2,6},{4,0},{6,2},{8,12},{10,14},{12,8},{14,10},{16,20},{18,... | collective-permute-start | bytes 3145736 | tf_op jit(solution)/shard_map/ppermute | solution.py:267
  155.5 24.9 %collective-permute-start.17 = (bf16[2,256,1024]{2,1,0:T(8,128)(2,1)S(1)}, bf16[2,256,1024]{2,1,0:T(8,128)(2,1)S(1)}, u32[]{:S(2)}, u32[]{:S(2)}) collective-permute-start(bf16[2,256,1024]{2,1,0:T(8,128)(2,1)S(1)} %fusion.26), channel_id=1, source_target_pairs={{0,1},{1,0},{2,3},{3,2},{4,5},{5,4},{6,7},{7,6},{8,9},{9,8},{10,11... | collective-permute-start | bytes 3145736 | tf_op jit(solution)/shard_map/ppermute | solution.py:273
  214.1 22.9 %collective-permute-start.22 = (bf16[2,256,1024]{2,1,0:T(8,128)(2,1)S(1)}, bf16[2,256,1024]{2,1,0:T(8,128)(2,1)S(1)}, u32[]{:S(2)}, u32[]{:S(2)}) collective-permute-start(bf16[2,256,1024]{2,1,0:T(8,128)(2,1)S(1)} %get-tuple-element.249), channel_id=1, source_target_pairs={{0,1},{1,0},{2,3},{3,2},{4,5},{5,4},{6,7},{7,6},{8,9},{9,8},{10,11... | collective-permute-start | bytes 3145736 | tf_op jit(solution)/shard_map/ppermute | solution.py:273
  215.8 22.2 %collective-permute-start.20 = (bf16[2,256,1024]{2,1,0:T(8,128)(2,1)S(1)}, bf16[2,256,1024]{2,1,0:T(8,128)(2,1)S(1)}, u32[]{:S(2)}, u32[]{:S(2)}) collective-permute-start(bf16[2,256,1024]{2,1,0:T(8,128)(2,1)S(1)} %get-tuple-element.243), channel_id=1, source_target_pairs={{0,4},{2,6},{4,0},{6,2},{8,12},{10,14},{12,8},{14,10},{16,20},{18,... | collective-permute-start | bytes 3145736 | tf_op jit(solution)/shard_map/ppermute | solution.py:267
  306.5 43.6 %collective-permute-start.29 = (bf16[256,1024]{1,0:T(8,128)(2,1)}, bf16[256,1024]{1,0:T(8,128)(2,1)}, u32[]{:S(2)}, u32[]{:S(2)}) collective-permute-start(bf16[256,1024]{1,0:T(8,128)(2,1)} %constant_dynamic-slice_fusion.9), channel_id=1, source_target_pairs={{0,1},{1,0},{2,3},{3,2},{4,5},{5,4},{6,7},{7,6},{8,9},{9,8},{10,11... | collective-permute-start | bytes 1572872 | tf_op jit(solution)/shard_map/ppermute | solution.py:273
  319.7 24.9 %collective-permute-start.25 = (bf16[2,256,1024]{2,1,0:T(8,128)(2,1)S(1)}, bf16[2,256,1024]{2,1,0:T(8,128)(2,1)S(1)}, u32[]{:S(2)}, u32[]{:S(2)}) collective-permute-start(bf16[2,256,1024]{2,1,0:T(8,128)(2,1)S(1)} %fusion.27), channel_id=1, source_target_pairs={{0,4},{2,6},{4,0},{6,2},{8,12},{10,14},{12,8},{14,10},{16,20},{18,... | collective-permute-start | bytes 3145736 | tf_op jit(solution)/shard_map/ppermute | solution.py:267
  321.2 24.6 %collective-permute-start.27 = (bf16[2,256,1024]{2,1,0:T(8,128)(2,1)S(1)}, bf16[2,256,1024]{2,1,0:T(8,128)(2,1)S(1)}, u32[]{:S(2)}, u32[]{:S(2)}) collective-permute-start(bf16[2,256,1024]{2,1,0:T(8,128)(2,1)S(1)} %fusion.28), channel_id=1, source_target_pairs={{0,1},{1,0},{2,3},{3,2},{4,5},{5,4},{6,7},{7,6},{8,9},{9,8},{10,11... | collective-permute-start | bytes 3145736 | tf_op jit(solution)/shard_map/ppermute | solution.py:273
  376.4 23.4 %collective-permute-start.33 = (bf16[2,256,1024]{2,1,0:T(8,128)(2,1)S(1)}, bf16[2,256,1024]{2,1,0:T(8,128)(2,1)S(1)}, u32[]{:S(2)}, u32[]{:S(2)}) collective-permute-start(bf16[2,256,1024]{2,1,0:T(8,128)(2,1)S(1)} %get-tuple-element.241), channel_id=1, source_target_pairs={{0,1},{1,0},{2,3},{3,2},{4,5},{5,4},{6,7},{7,6},{8,9},{9,8},{10,11... | collective-permute-start | bytes 3145736 | tf_op jit(solution)/shard_map/ppermute | solution.py:273
  379.3 20.6 %collective-permute-start.31 = (bf16[2,256,1024]{2,1,0:T(8,128)(2,1)S(1)}, bf16[2,256,1024]{2,1,0:T(8,128)(2,1)S(1)}, u32[]{:S(2)}, u32[]{:S(2)}) collective-permute-start(bf16[2,256,1024]{2,1,0:T(8,128)(2,1)S(1)} %get-tuple-element.235), channel_id=1, source_target_pairs={{0,4},{2,6},{4,0},{6,2},{8,12},{10,14},{12,8},{14,10},{16,20},{18,... | collective-permute-start | bytes 3145736 | tf_op jit(solution)/shard_map/ppermute | solution.py:267
  425.1 167.8 %reduce-scatter.9.cloned.1.call-start = ((), (), s32[]{:S(2)}) async-start(), calls=%async_computation.10 | async-start | bytes 5242880 | tf_op jit(solution)/shard_map/reduce_scatter | solution.py:436
  451.9 25.7 %collective-permute-start.36 = (bf16[2,256,1024]{2,1,0:T(8,128)(2,1)}, bf16[2,256,1024]{2,1,0:T(8,128)(2,1)}, u32[]{:S(2)}, u32[]{:S(2)}) collective-permute-start(bf16[2,256,1024]{2,1,0:T(8,128)(2,1)} %fusion.29), channel_id=1, source_target_pairs={{0,4},{2,6},{4,0},{6,2},{8,12},{10,14},{12,8},{14,10},{16,20},{18,... | collective-permute-start | bytes 3145736 | tf_op jit(solution)/shard_map/ppermute | solution.py:267
  455.1 25.6 %collective-permute-start.38 = (bf16[2,256,1024]{2,1,0:T(8,128)(2,1)}, bf16[2,256,1024]{2,1,0:T(8,128)(2,1)}, u32[]{:S(2)}, u32[]{:S(2)}) collective-permute-start(bf16[2,256,1024]{2,1,0:T(8,128)(2,1)} %fusion.30), channel_id=1, source_target_pairs={{0,1},{1,0},{2,3},{3,2},{4,5},{5,4},{6,7},{7,6},{8,9},{9,8},{10,11... | collective-permute-start | bytes 3145736 | tf_op jit(solution)/shard_map/ppermute | solution.py:273
  488.1 182.5 %reduce-scatter.7.cloned.1.call-start = ((), (), s32[]{:S(2)}) async-start(), calls=%async_computation.9 | async-start | bytes 3932160 | tf_op jit(solution)/shard_map/reduce_scatter | solution.py:436
  520.5 23.9 %collective-permute-start.43 = (bf16[2,256,1024]{2,1,0:T(8,128)(2,1)S(1)}, bf16[2,256,1024]{2,1,0:T(8,128)(2,1)S(1)}, u32[]{:S(2)}, u32[]{:S(2)}) collective-permute-start(bf16[2,256,1024]{2,1,0:T(8,128)(2,1)S(1)} %get-tuple-element.233), channel_id=1, source_target_pairs={{0,1},{1,0},{2,3},{3,2},{4,5},{5,4},{6,7},{7,6},{8,9},{9,8},{10,11... | collective-permute-start | bytes 3145736 | tf_op jit(solution)/shard_map/ppermute | solution.py:273
  522.1 23.9 %collective-permute-start.41 = (bf16[2,256,1024]{2,1,0:T(8,128)(2,1)S(1)}, bf16[2,256,1024]{2,1,0:T(8,128)(2,1)S(1)}, u32[]{:S(2)}, u32[]{:S(2)}) collective-permute-start(bf16[2,256,1024]{2,1,0:T(8,128)(2,1)S(1)} %get-tuple-element.227), channel_id=1, source_target_pairs={{0,4},{2,6},{4,0},{6,2},{8,12},{10,14},{12,8},{14,10},{16,20},{18,... | collective-permute-start | bytes 3145736 | tf_op jit(solution)/shard_map/ppermute | solution.py:267
  590.4 93.9 %reduce-scatter.11.cloned.1.call-start = ((), (), s32[]{:S(2)}) async-start(), calls=%async_computation.11 | async-start | bytes 1310720 | tf_op jit(solution)/shard_map/reduce_scatter | solution.py:436
  590.5 24.7 %collective-permute-start.48 = (bf16[1024,2048]{1,0:T(8,128)(2,1)}, bf16[1024,2048]{1,0:T(8,128)(2,1)}, u32[]{:S(2)}, u32[]{:S(2)}) collective-permute-start(bf16[1024,2048]{1,0:T(8,128)(2,1)} %copy-done.38), channel_id=1, source_target_pairs={{0,2},{2,0},{4,6},{6,4},{8,10},{10,8},{12,14},{14,12},{16,18},{18,... | collective-permute-start | bytes 12582920 | tf_op jit(solution)/shard_map/ppermute | solution.py:264
  618.0 24.9 %collective-permute-start.53 = (bf16[2,512,512]{2,1,0:T(8,128)(2,1)}, bf16[2,512,512]{2,1,0:T(8,128)(2,1)}, u32[]{:S(2)}, u32[]{:S(2)}) collective-permute-start(bf16[2,512,512]{2,1,0:T(8,128)(2,1)} %add_convert_fusion), channel_id=1, source_target_pairs={{0,1},{1,0},{2,3},{3,2},{4,5},{5,4},{6,7},{7,6},{8,9},{9,8},{10,11... | collective-permute-start | bytes 3145736 | tf_op jit(solution)/shard_map/ppermute | solution.py:273
  625.5 25.8 %collective-permute-start.49 = (bf16[512,1024]{1,0:T(8,128)(2,1)}, bf16[512,1024]{1,0:T(8,128)(2,1)S(1)}, u32[]{:S(2)}, u32[]{:S(2)}) collective-permute-start(bf16[512,1024]{1,0:T(8,128)(2,1)} %add_convert_fusion.1), channel_id=1, source_target_pairs={{0,4},{2,6},{4,0},{6,2},{8,12},{10,14},{12,8},{14,10},{16,20},{18,... | collective-permute-start | bytes 3145736 | tf_op jit(solution)/shard_map/ppermute | solution.py:267
  647.3 20.4 %collective-permute-start.54 = (bf16[512,512]{1,0:T(8,128)(2,1)}, bf16[512,512]{1,0:T(8,128)(2,1)}, u32[]{:S(2)}, u32[]{:S(2)}) collective-permute-start(bf16[512,512]{1,0:T(8,128)(2,1)} %fusion.48), channel_id=1, source_target_pairs={{0,4},{2,6},{4,0},{6,2},{8,12},{10,14},{12,8},{14,10},{16,20},{18,... | collective-permute-start | bytes 1572872 | tf_op jit(solution)/shard_map/ppermute | solution.py:267
  673.9 42.5 %collective-permute-start.46 = (bf16[256,1024]{1,0:T(8,128)(2,1)}, bf16[256,1024]{1,0:T(8,128)(2,1)}, u32[]{:S(2)}, u32[]{:S(2)}) collective-permute-start(bf16[256,1024]{1,0:T(8,128)(2,1)} %constant_dynamic-slice_fusion.10), channel_id=1, source_target_pairs={{0,1},{1,0},{2,3},{3,2},{4,5},{5,4},{6,7},{7,6},{8,9},{9,8},{10,11... | collective-permute-start | bytes 1572872 | tf_op jit(solution)/shard_map/ppermute | solution.py:273
  676.6 44.1 %all-to-all-start.1 = ((bf16[32,16,1024]{2,0,1:T(8,128)(2,1)}), bf16[32,16,1024]{2,0,1:T(8,128)(2,1)}, u32[]{:S(2)}, u32[]{:S(2)}) async-start(bf16[32,16,1024]{2,0,1:T(8,128)(2,1)} %copy.171), calls=%async_computation.4 | async-start | bytes 2097152 | tf_op jit(solution)/shard_map/all_to_all | solution.py:566
  684.1 31.8 %collective-permute-start.55 = (bf16[256,3,256]{0,2,1:T(8,128)(2,1)S(1)}, bf16[256,3,256]{0,2,1:T(8,128)(2,1)S(1)}, u32[]{:S(2)}, u32[]{:S(2)}) collective-permute-start(bf16[256,3,256]{0,2,1:T(8,128)(2,1)S(1)} %constant_dynamic-slice_fusion.5), channel_id=1, source_target_pairs={{0,4},{2,6},{4,0},{6,2},{8,12},{10,14},{12,8},{14,10},{16,20},{18,... | collective-permute-start | bytes 1179656 | tf_op jit(solution)/shard_map/ppermute | solution.py:267
  (125 other events, 868.4 us)
Sparse Core Ops, SparseCore 0:
  37.2 83.6 all-gather.2
  122.5 148.1 all-gather.4
  425.2 73.4 reduce-scatter.4
  501.0 77.2 reduce-scatter.8
  590.6 59.9 reduce-scatter.6
  652.7 27.1 reduce-scatter.10

commit v5 on v4

--- a/solution.py
+++ b/solution.py
@@ -487,10 +487,8 @@
     qkv_partial = pair_matmul(all_rows, [after(grads, theirs) for grads in stacked])
     qkv_sum = scatter(qkv_partial)
     theirs = core_swap(theirs)
-    up_sum = side_send(up_sum, 1)
-    out_partial = pair_matmul(attended_grad, [after(rows, qkv_partial) for rows in context])
-    out_sum = scatter(out_partial)
-    theirs = after(theirs, out_partial, up_sum[1])
+    theirs = after(theirs, up_sum)
+
     quarter = half // 2
     both = tuple(array.reshape(2, seq_len, width) for array in (after(mine, up_sum[1]), theirs))
 
@@ -510,13 +508,14 @@
     one_sent = summed(lambda array: across(array[1])).astype(low)
     two_sent = summed(of_lane(1 - lane)).astype(low)
     one, two = side_swap(one_sent), lane_swap_rows(two_sent)
+    out_partial = pair_matmul(attended_grad, [after(rows, one_sent, two_sent) for rows in context])
+    out_sum = scatter(out_partial)
     one = summed(lambda array: across(array[0])) + one.astype(wide)
     two = summed(of_lane(lane)) + two.astype(wide)
     one_sent = take(one, (1 - lane) * quarter, quarter, 1).astype(low)
     two_sent = two[1].astype(low)
     down_weight_grad = core_join(after(side_join(*down_sum), one_sent))[:, 0].T
-    up_weight_grad = core_join(after(side_join(*up_sum), one_sent))[:, 0]
-    one_theirs = after(lane_swap(one_sent), down_weight_grad, up_weight_grad)
+    one_theirs = after(lane_swap(one_sent), down_weight_grad, out_partial)
     one_theirs = jnp.concatenate([one_theirs[token_half:], one_theirs[:token_half]], axis=0)
     one = take(one, lane * quarter, quarter, 1) + one_theirs.astype(wide)
     two = two[0] + side_swap(two_sent).astype(wide)
@@ -563,6 +562,7 @@
     packed = jnp.concatenate([qv_spread, up_spread, vector_spread], axis=1)
     packed = after(packed, qkv_sum)
 
+    up_weight_grad = core_join(side_join(*side_send(after(up_sum, two_sent), 1)))[:, 0]
     returned = lax.all_to_all(back_rows, "dp", split_axis=1, concat_axis=1, tiled=True)
     inverse_order = (
         jnp.zeros((groups,), jnp.int32).at[dealing].set(jnp.arange(groups, dtype=jnp.int32))

time: 740 us -> 737 us (level)
  transfers between devices with their start and end apart: 73 -> 73, of which waited for: 42 -> 43; matrix products, arithmetic and copies ran while one was open for 17% -> 16% of each run, Pallas kernels for 16% -> 16%
where the time goes in v5:
time: 737 us; the launch traced here: 728 us
  waiting for transfers between devices  320 us (43%)
  Pallas kernels  148 us (20%)
  local copies, waits for them, and re-layouts  89.5 us (12%)
  other arithmetic  79.2 us (11%)
  starting transfers between devices  74 us (10%)
  between operations  16.5 us (2%)
    ppermute x24, waiting for transfers between devices, side_swap(): return lax.ppermute(array, 'dp', side_pairs)  169 us
    ppermute x19, waiting for transfers between devices, lane_swap(): return lax.ppermute(array, 'tensor', [(0, 1), (1, 0)])  101 us
    pallas_call x12, Pallas kernels, matmul(): call(functools.partial(matmul_kernel, right_axis), 2 * rows * depth * siz...  59 us
    unnamed x181, local copies, waits for them, and re-layouts  47.4 us
    pallas_call x4, Pallas kernels, pair_matmul(): call(pair_kernel, 4 * rows * depth * columns, jax.ShapeDtypeStruct((depth...  41.5 us
    all_gather x2, waiting for transfers between devices, gather_weight(): lax.all_gather(piece, 'dp', axis=0, axis_index_groups=ring_groups, tiled=...  31.8 us
    ppermute x24, starting transfers between devices, side_swap(): return lax.ppermute(array, 'dp', side_pairs)  27.8 us
    ppermute x19, starting transfers between devices, lane_swap(): return lax.ppermute(array, 'tensor', [(0, 1), (1, 0)])  21.4 us
  transfers between devices with their start and end apart: 73, of which 43 were waited for; matrix products, arithmetic and copies ran while one was open for 16% of the time, Pallas kernels for 16%

profile of v5, /device:TPU:0, one launch (start us, length us, event | category | flops | bytes accessed | tf_op | source)
XLA Modules:
  0.0 727.9 jit_solution(2148750025592656386)
XLA Ops:
  25.6 6.4 collective-permute-done.1
  53.1 8.8 %collective-permute-done.4 = bf16[256,1024]{1,0:T(8,128)(2,1)} collective-permute-done((bf16[256,1024]{1,0:T(8,128)(2,1)S(1)}, bf16[256,1024]{1,0:T(8,128)(2,1)}, u32[]{:S(2)}, u32[]{:S(2)}) %collective-permute-start.4) | collective-permute-done | bytes 524320 | tf_op jit(solution)/shard_map/ppermute | solution.py:267
  68.7 19.7 %collective-permute-done.5 = bf16[2,256,1024]{2,1,0:T(8,128)(2,1)S(1)} collective-permute-done((bf16[2,256,1024]{2,1,0:T(8,128)(2,1)S(1)}, bf16[2,256,1024]{2,1,0:T(8,128)(2,1)S(1)}, u32[]{:S(2)}, u32[]{:S(2)}) %collective-permute-start.5) | collective-permute-done | bytes 1048608 | tf_op jit(solution)/shard_map/ppermute | solution.py:273
  95.5 18.1 %collective-permute-done.7 = bf16[256,2,1024]{0,2,1:T(8,128)(2,1)S(1)} collective-permute-done((bf16[256,2,1024]{0,2,1:T(8,128)(2,1)S(1)}, bf16[256,2,1024]{0,2,1:T(8,128)(2,1)S(1)}, u32[]{:S(2)}, u32[]{:S(2)}) %collective-permute-start.7) | collective-permute-done | bytes 1048608 | tf_op jit(solution)/shard_map/ppermute | solution.py:267
  133.5 6.5 shard_map.266.query.key.value
  156.9 22.1 %collective-permute-done.15 = bf16[2,256,1024]{2,1,0:T(8,128)(2,1)S(1)} collective-permute-done((bf16[2,256,1024]{2,1,0:T(8,128)(2,1)S(1)}, bf16[2,256,1024]{2,1,0:T(8,128)(2,1)S(1)}, u32[]{:S(2)}, u32[]{:S(2)}) %collective-permute-start.15) | collective-permute-done | bytes 1048608 | tf_op jit(solution)/shard_map/ppermute | solution.py:267
  185.7 10.2 %collective-permute-done.18 = bf16[256,1024]{1,0:T(8,128)(2,1)} collective-permute-done((bf16[256,1024]{1,0:T(8,128)(2,1)}, bf16[256,1024]{1,0:T(8,128)(2,1)}, u32[]{:S(2)}, u32[]{:S(2)}) %collective-permute-start.18) | collective-permute-done | bytes 524320 | tf_op jit(solution)/shard_map/ppermute | solution.py:267
  204.5 9.4 %collective-permute-done.21 = bf16[256,1024]{1,0:T(8,128)(2,1)S(1)} collective-permute-done((bf16[256,1024]{1,0:T(8,128)(2,1)S(1)}, bf16[256,1024]{1,0:T(8,128)(2,1)S(1)}, u32[]{:S(2)}, u32[]{:S(2)}) %collective-permute-start.21) | collective-permute-done | bytes 524320 | tf_op jit(solution)/shard_map/ppermute | solution.py:267
  216.9 20.0 %collective-permute-done.22 = bf16[2,256,1024]{2,1,0:T(8,128)(2,1)S(1)} collective-permute-done((bf16[2,256,1024]{2,1,0:T(8,128)(2,1)S(1)}, bf16[2,256,1024]{2,1,0:T(8,128)(2,1)S(1)}, u32[]{:S(2)}, u32[]{:S(2)}) %collective-permute-start.22) | collective-permute-done | bytes 1048608 | tf_op jit(solution)/shard_map/ppermute | solution.py:273
  240.7 30.0 %all-gather.5.cloned.1.call-done.weight.right = bf16[2048,2048]{1,0:T(8,128)(2,1)} async-done(((bf16[512,2048]{1,0:T(8,128)(2,1)}), bf16[2048,2048]{1,0:T(8,128)(2,1)}) %all-gather.5.cloned.1.call-update) | async-done | bytes 8388624 | tf_op jit(solution)/shard_map/all_gather | solution.py:300
  273.9 7.6 %shard_map.269 = (f32[1024,1024]{1,0:T(8,128)S(1)}, bf16[1024,1024]{1,0:T(8,128)(2,1)S(1)}) custom-call(bf16[1024,2048]{1,0:T(8,128)(2,1)S(1)} %bitcast.319, bf16[2048,2048]{1,0:T(8,128)(2,1)} %all-gather.5.cloned.1.call-done.weight.right, f32[1,1024]{1,0:T(1,128)S(1)} %bitcast.332), custom_call_target="tpu_custom_call" | custom-call | flops 536870912 | tf_op jit(solution)/shard_map/pallas_call | solution.py:177
  284.8 8.8 %shard_map.271 = (f32[1024,1024]{1,0:T(8,128)S(1)}, bf16[1024,1024]{1,0:T(8,128)(2,1)S(1)}) custom-call(bf16[1024,2048]{1,0:T(8,128)(2,1)} %collective-permute-done.23.rows.left_two, bf16[2048,2048]{1,0:T(8,128)(2,1)} %all-gather.5.cloned.1.call-done.weight.right, f32[1,1024]{1,0:T(1,128)S(1)} %bitcast.333), custom_call_target="tpu_custom_call" | custom-call | flops 536870912 | tf_op jit(solution)/shard_map/pallas_call | solution.py:177
  295.6 8.6 %shard_map.272 = bf16[1024,2048]{1,0:T(8,128)(2,1)} custom-call(bf16[1024,1024]{1,0:T(8,128)(2,1)S(1)} %get-tuple-element.69.left.right_two, bf16[2048,2048]{1,0:T(8,128)(2,1)} %all-gather.5.cloned.1.call-done.weight.right), custom_call_target="tpu_custom_call" | custom-call | flops 536870912 | tf_op jit(solution)/shard_map/pallas_call | solution.py:149
  309.6 6.8 shard_map.270
  328.0 16.8 %collective-permute-done.25 = bf16[2,256,1024]{2,1,0:T(8,128)(2,1)S(1)} collective-permute-done((bf16[2,256,1024]{2,1,0:T(8,128)(2,1)S(1)}, bf16[2,256,1024]{2,1,0:T(8,128)(2,1)S(1)}, u32[]{:S(2)}, u32[]{:S(2)}) %collective-permute-start.25) | collective-permute-done | bytes 1048608 | tf_op jit(solution)/shard_map/ppermute | solution.py:267
  351.6 9.8 %collective-permute-done.28 = bf16[256,1024]{1,0:T(8,128)(2,1)S(1)} collective-permute-done((bf16[256,1024]{1,0:T(8,128)(2,1)S(1)}, bf16[256,1024]{1,0:T(8,128)(2,1)S(1)}, u32[]{:S(2)}, u32[]{:S(2)}) %collective-permute-start.28) | collective-permute-done | bytes 524320 | tf_op jit(solution)/shard_map/ppermute | solution.py:267
  367.2 9.3 %collective-permute-done.32 = bf16[256,1024]{1,0:T(8,128)(2,1)S(1)} collective-permute-done((bf16[256,1024]{1,0:T(8,128)(2,1)S(1)}, bf16[256,1024]{1,0:T(8,128)(2,1)S(1)}, u32[]{:S(2)}, u32[]{:S(2)}) %collective-permute-start.32) | collective-permute-done | bytes 524320 | tf_op jit(solution)/shard_map/ppermute | solution.py:267
  379.5 20.5 %collective-permute-done.33 = bf16[2,256,1024]{2,1,0:T(8,128)(2,1)S(1)} collective-permute-done((bf16[2,256,1024]{2,1,0:T(8,128)(2,1)S(1)}, bf16[2,256,1024]{2,1,0:T(8,128)(2,1)S(1)}, u32[]{:S(2)}, u32[]{:S(2)}) %collective-permute-start.33) | collective-permute-done | bytes 1048608 | tf_op jit(solution)/shard_map/ppermute | solution.py:273
  401.1 6.8 shard_map.273
  411.3 11.9 %shard_map.275 = bf16[2048,1024]{1,0:T(8,128)(2,1)S(1)} custom-call(bf16[1024,2048]{1,0:T(8,128)(2,1)S(1)} %bitcast.317, bf16[1024,1024]{1,0:T(8,128)(2,1)S(1)} %copy-done.23, bf16[1024,2048]{1,0:T(8,128)(2,1)} %copy-done.14, bf16[1024,1024]{1,0:T(8,128)(2,1)S(1)} %copy-done.25), custom_call_target="tpu_custom_call" | custom-call | flops 1073741824 | tf_op jit(solution)/shard_map/pallas_call | solution.py:226
  429.6 6.9 shard_map.276
  436.5 6.9 shard_map.277
  443.8 6.7 shard_map.274
  455.8 11.8 %shard_map.278 = bf16[2048,1024]{1,0:T(8,128)(2,1)S(1)} custom-call(bf16[1024,2048]{1,0:T(8,128)(2,1)S(1)} %bitcast.320, bf16[1024,1024]{1,0:T(8,128)(2,1)S(1)} %copy-done.27, bf16[1024,2048]{1,0:T(8,128)(2,1)} %collective-permute-done.23.rows.left_two, bf16[1024,1024]{1,0:T(8,128)(2,1)S(1)} %get-tuple-element.81.left.right_two), custom_call_target="tpu_custom_call" | custom-call | flops 1073741824 | tf_op jit(solution)/shard_map/pallas_call | solution.py:226
  469.7 8.0 %collective-permute-done.36 = bf16[2,256,1024]{2,1,0:T(8,128)(2,1)} collective-permute-done((bf16[2,256,1024]{2,1,0:T(8,128)(2,1)}, bf16[2,256,1024]{2,1,0:T(8,128)(2,1)}, u32[]{:S(2)}, u32[]{:S(2)}) %collective-permute-start.36) | collective-permute-done | bytes 1048608 | tf_op jit(solution)/shard_map/ppermute | solution.py:267
  488.3 11.4 %collective-permute-done.39 = bf16[256,1024]{1,0:T(8,128)(2,1)} collective-permute-done((bf16[256,1024]{1,0:T(8,128)(2,1)}, bf16[256,1024]{1,0:T(8,128)(2,1)}, u32[]{:S(2)}, u32[]{:S(2)}) %collective-permute-start.39) | collective-permute-done | bytes 524320 | tf_op jit(solution)/shard_map/ppermute | solution.py:267
  509.7 10.7 %collective-permute-done.42 = bf16[256,1024]{1,0:T(8,128)(2,1)S(1)} collective-permute-done((bf16[256,1024]{1,0:T(8,128)(2,1)S(1)}, bf16[256,1024]{1,0:T(8,128)(2,1)S(1)}, u32[]{:S(2)}, u32[]{:S(2)}) %collective-permute-start.42) | collective-permute-done | bytes 524320 | tf_op jit(solution)/shard_map/ppermute | solution.py:267
  523.8 20.7 %collective-permute-done.43 = bf16[2,256,1024]{2,1,0:T(8,128)(2,1)S(1)} collective-permute-done((bf16[2,256,1024]{2,1,0:T(8,128)(2,1)S(1)}, bf16[2,256,1024]{2,1,0:T(8,128)(2,1)S(1)}, u32[]{:S(2)}, u32[]{:S(2)}) %collective-permute-start.43) | collective-permute-done | bytes 1048608 | tf_op jit(solution)/shard_map/ppermute | solution.py:273
  581.4 9.9 %shard_map.285 = bf16[2048,768]{1,0:T(8,128)(2,1)S(1)} custom-call(bf16[1024,2048]{1,0:T(8,128)(2,1)S(1)} %bitcast.311, bf16[1024,768]{1,0:T(8,128)(2,1)S(1)} %shard_map.280.left.right_one, bf16[1024,2048]{1,0:T(8,128)(2,1)} %collective-permute-done.13.left.left_two, bf16[1024,768]{1,0:T(8,128)(2,1)S(1)} %shard_map.283.left.right_two), custom_call_target="tpu_custom_call" | custom-call | flops 805306368 | tf_op jit(solution)/shard_map/pallas_call | solution.py:226
  614.7 7.9 %shard_map.286 = bf16[2048,256]{1,0:T(8,128)(2,1)} custom-call(bf16[1024,2048]{1,0:T(8,128)(2,1)S(1)} %bitcast.314, bf16[1024,256]{1,0:T(8,128)(2,1)S(1)} %copy-done.29, bf16[1024,2048]{1,0:T(8,128)(2,1)} %collective-permute-done.44.left.left_two, bf16[1024,256]{1,0:T(8,128)(2,1)S(1)} %copy-done.31), custom_call_target="tpu_custom_call" | custom-call | flops 268435456 | tf_op jit(solution)/shard_map/pallas_call | solution.py:226
  651.8 6.6 collective-permute-done.63
  683.3 12.4 %collective-permute-done.56 = f32[4,1,1152]{2,1,0:T(1,128)S(1)} collective-permute-done((f32[4,1,1152]{2,1,0:T(1,128)S(1)}, f32[4,1,1152]{2,1,0:T(1,128)S(1)}, u32[]{:S(2)}, u32[]{:S(2)}) %collective-permute-start.56) | collective-permute-done | bytes 18464 | tf_op jit(solution)/shard_map/ppermute | solution.py:267
  (528 shorter events, 333.1 us)
Async XLA Ops:
  13.8 18.3 %collective-permute-start.1 = (bf16[256,4,256]{2,0,1:T(8,128)(2,1)}, bf16[256,4,256]{2,0,1:T(8,128)(2,1)}, u32[]{:S(2)}, u32[]{:S(2)}) collective-permute-start(bf16[256,4,256]{2,0,1:T(8,128)(2,1)} %fusion.55), channel_id=1, source_target_pairs={{0,4},{2,6},{4,0},{6,2},{8,12},{10,14},{12,8},{14,10},{16,20},{18,... | collective-permute-start | bytes 1572872 | tf_op jit(solution)/shard_map/ppermute | solution.py:267
  18.5 27.9 %all-to-all-start = ((bf16[32,16,1024]{2,0,1:T(8,128)(2,1)}), bf16[32,16,1024]{2,0,1:T(8,128)(2,1)S(1)}, u32[]{:S(2)}, u32[]{:S(2)}) async-start(bf16[32,16,1024]{2,0,1:T(8,128)(2,1)} %select_bitcast_fusion), calls=%async_computation | async-start | bytes 2097152 | tf_op jit(solution)/shard_map/all_to_all | solution.py:332
  23.5 97.4 %all-gather.3.cloned.1.call-start = ((), (), s32[]{:S(2)}) async-start(), calls=%async_computation.6 | async-start | bytes 5242880 | tf_op jit(solution)/shard_map/all_gather | solution.py:300
  37.1 233.6 %all-gather.5.cloned.1.call-start = ((), (), s32[]{:S(2)}) async-start(), calls=%async_computation.7 | async-start | bytes 10485760 | tf_op jit(solution)/shard_map/all_gather | solution.py:300
  45.5 23.2 %collective-permute-start.12 = (bf16[4,1152]{1,0:T(4,128)(2,1)S(1)}, bf16[4,1152]{1,0:T(4,128)(2,1)S(1)}, u32[]{:S(2)}, u32[]{:S(2)}) collective-permute-start(bf16[4,1152]{1,0:T(4,128)(2,1)S(1)} %get-tuple-element.269), channel_id=1, source_target_pairs={{0,24},{2,26},{4,28},{6,30},{8,0},{10,2},{12,4},{14,6},{16,8},{18,... | collective-permute-start | bytes 27656 | tf_op jit(solution)/shard_map/ppermute | solution.py:270
  63.1 25.3 %collective-permute-start.5 = (bf16[2,256,1024]{2,1,0:T(8,128)(2,1)S(1)}, bf16[2,256,1024]{2,1,0:T(8,128)(2,1)S(1)}, u32[]{:S(2)}, u32[]{:S(2)}) collective-permute-start(bf16[2,256,1024]{2,1,0:T(8,128)(2,1)S(1)} %pad_maximum_fusion.5), channel_id=1, source_target_pairs={{0,1},{1,0},{2,3},{3,2},{4,5},{5,4},{6,7},{7,6},{8,9},{9,8},{10,11... | collective-permute-start | bytes 3145736 | tf_op jit(solution)/shard_map/ppermute | solution.py:273
  66.0 26.1 %collective-permute-start.3 = (bf16[256,2048]{1,0:T(8,128)(2,1)S(1)}, bf16[256,2048]{1,0:T(8,128)(2,1)S(1)}, u32[]{:S(2)}, u32[]{:S(2)}) collective-permute-start(bf16[256,2048]{1,0:T(8,128)(2,1)S(1)} %get-tuple-element.249), channel_id=1, source_target_pairs={{0,4},{2,6},{4,0},{6,2},{8,12},{10,14},{12,8},{14,10},{16,20},{18,... | collective-permute-start | bytes 3145736 | tf_op jit(solution)/shard_map/ppermute | solution.py:267
  68.6 45.0 %collective-permute-start.7 = (bf16[256,2,1024]{0,2,1:T(8,128)(2,1)S(1)}, bf16[256,2,1024]{0,2,1:T(8,128)(2,1)S(1)}, u32[]{:S(2)}, u32[]{:S(2)}) collective-permute-start(bf16[256,2,1024]{0,2,1:T(8,128)(2,1)S(1)} %fusion.31), channel_id=1, source_target_pairs={{0,4},{2,6},{4,0},{6,2},{8,12},{10,14},{12,8},{14,10},{16,20},{18,... | collective-permute-start | bytes 3145736 | tf_op jit(solution)/shard_map/ppermute | solution.py:267
  117.5 382.1 %reduce-scatter.5.cloned.1.call-start = ((), (), s32[]{:S(2)}) async-start(), calls=%async_computation.8 | async-start | bytes 5242880 | tf_op jit(solution)/shard_map/reduce_scatter | solution.py:436
  153.8 25.3 %collective-permute-start.15 = (bf16[2,256,1024]{2,1,0:T(8,128)(2,1)S(1)}, bf16[2,256,1024]{2,1,0:T(8,128)(2,1)S(1)}, u32[]{:S(2)}, u32[]{:S(2)}) collective-permute-start(bf16[2,256,1024]{2,1,0:T(8,128)(2,1)S(1)} %fusion.25), channel_id=1, source_target_pairs={{0,4},{2,6},{4,0},{6,2},{8,12},{10,14},{12,8},{14,10},{16,20},{18,... | collective-permute-start | bytes 3145736 | tf_op jit(solution)/shard_map/ppermute | solution.py:267
  155.5 24.9 %collective-permute-start.17 = (bf16[2,256,1024]{2,1,0:T(8,128)(2,1)S(1)}, bf16[2,256,1024]{2,1,0:T(8,128)(2,1)S(1)}, u32[]{:S(2)}, u32[]{:S(2)}) collective-permute-start(bf16[2,256,1024]{2,1,0:T(8,128)(2,1)S(1)} %fusion.26), channel_id=1, source_target_pairs={{0,1},{1,0},{2,3},{3,2},{4,5},{5,4},{6,7},{7,6},{8,9},{9,8},{10,11... | collective-permute-start | bytes 3145736 | tf_op jit(solution)/shard_map/ppermute | solution.py:273
  214.1 22.9 %collective-permute-start.22 = (bf16[2,256,1024]{2,1,0:T(8,128)(2,1)S(1)}, bf16[2,256,1024]{2,1,0:T(8,128)(2,1)S(1)}, u32[]{:S(2)}, u32[]{:S(2)}) collective-permute-start(bf16[2,256,1024]{2,1,0:T(8,128)(2,1)S(1)} %get-tuple-element.247), channel_id=1, source_target_pairs={{0,1},{1,0},{2,3},{3,2},{4,5},{5,4},{6,7},{7,6},{8,9},{9,8},{10,11... | collective-permute-start | bytes 3145736 | tf_op jit(solution)/shard_map/ppermute | solution.py:273
  215.8 22.2 %collective-permute-start.20 = (bf16[2,256,1024]{2,1,0:T(8,128)(2,1)S(1)}, bf16[2,256,1024]{2,1,0:T(8,128)(2,1)S(1)}, u32[]{:S(2)}, u32[]{:S(2)}) collective-permute-start(bf16[2,256,1024]{2,1,0:T(8,128)(2,1)S(1)} %get-tuple-element.241), channel_id=1, source_target_pairs={{0,4},{2,6},{4,0},{6,2},{8,12},{10,14},{12,8},{14,10},{16,20},{18,... | collective-permute-start | bytes 3145736 | tf_op jit(solution)/shard_map/ppermute | solution.py:267
  306.5 43.8 %collective-permute-start.29 = (bf16[256,1024]{1,0:T(8,128)(2,1)}, bf16[256,1024]{1,0:T(8,128)(2,1)}, u32[]{:S(2)}, u32[]{:S(2)}) collective-permute-start(bf16[256,1024]{1,0:T(8,128)(2,1)} %constant_dynamic-slice_fusion.8), channel_id=1, source_target_pairs={{0,1},{1,0},{2,3},{3,2},{4,5},{5,4},{6,7},{7,6},{8,9},{9,8},{10,11... | collective-permute-start | bytes 1572872 | tf_op jit(solution)/shard_map/ppermute | solution.py:273
  319.8 24.9 %collective-permute-start.25 = (bf16[2,256,1024]{2,1,0:T(8,128)(2,1)S(1)}, bf16[2,256,1024]{2,1,0:T(8,128)(2,1)S(1)}, u32[]{:S(2)}, u32[]{:S(2)}) collective-permute-start(bf16[2,256,1024]{2,1,0:T(8,128)(2,1)S(1)} %fusion.27), channel_id=1, source_target_pairs={{0,4},{2,6},{4,0},{6,2},{8,12},{10,14},{12,8},{14,10},{16,20},{18,... | collective-permute-start | bytes 3145736 | tf_op jit(solution)/shard_map/ppermute | solution.py:267
  321.4 24.6 %collective-permute-start.27 = (bf16[2,256,1024]{2,1,0:T(8,128)(2,1)S(1)}, bf16[2,256,1024]{2,1,0:T(8,128)(2,1)S(1)}, u32[]{:S(2)}, u32[]{:S(2)}) collective-permute-start(bf16[2,256,1024]{2,1,0:T(8,128)(2,1)S(1)} %fusion.28), channel_id=1, source_target_pairs={{0,1},{1,0},{2,3},{3,2},{4,5},{5,4},{6,7},{7,6},{8,9},{9,8},{10,11... | collective-permute-start | bytes 3145736 | tf_op jit(solution)/shard_map/ppermute | solution.py:273
  376.7 23.4 %collective-permute-start.33 = (bf16[2,256,1024]{2,1,0:T(8,128)(2,1)S(1)}, bf16[2,256,1024]{2,1,0:T(8,128)(2,1)S(1)}, u32[]{:S(2)}, u32[]{:S(2)}) collective-permute-start(bf16[2,256,1024]{2,1,0:T(8,128)(2,1)S(1)} %get-tuple-element.239), channel_id=1, source_target_pairs={{0,1},{1,0},{2,3},{3,2},{4,5},{5,4},{6,7},{7,6},{8,9},{9,8},{10,11... | collective-permute-start | bytes 3145736 | tf_op jit(solution)/shard_map/ppermute | solution.py:273
  379.4 20.6 %collective-permute-start.31 = (bf16[2,256,1024]{2,1,0:T(8,128)(2,1)S(1)}, bf16[2,256,1024]{2,1,0:T(8,128)(2,1)S(1)}, u32[]{:S(2)}, u32[]{:S(2)}) collective-permute-start(bf16[2,256,1024]{2,1,0:T(8,128)(2,1)S(1)} %get-tuple-element.233), channel_id=1, source_target_pairs={{0,4},{2,6},{4,0},{6,2},{8,12},{10,14},{12,8},{14,10},{16,20},{18,... | collective-permute-start | bytes 3145736 | tf_op jit(solution)/shard_map/ppermute | solution.py:267
  425.2 171.4 %reduce-scatter.9.cloned.1.call-start = ((), (), s32[]{:S(2)}) async-start(), calls=%async_computation.10 | async-start | bytes 5242880 | tf_op jit(solution)/shard_map/reduce_scatter | solution.py:436
  452.0 25.7 %collective-permute-start.36 = (bf16[2,256,1024]{2,1,0:T(8,128)(2,1)}, bf16[2,256,1024]{2,1,0:T(8,128)(2,1)}, u32[]{:S(2)}, u32[]{:S(2)}) collective-permute-start(bf16[2,256,1024]{2,1,0:T(8,128)(2,1)} %fusion.29), channel_id=1, source_target_pairs={{0,4},{2,6},{4,0},{6,2},{8,12},{10,14},{12,8},{14,10},{16,20},{18,... | collective-permute-start | bytes 3145736 | tf_op jit(solution)/shard_map/ppermute | solution.py:267
  455.3 25.6 %collective-permute-start.38 = (bf16[2,256,1024]{2,1,0:T(8,128)(2,1)}, bf16[2,256,1024]{2,1,0:T(8,128)(2,1)}, u32[]{:S(2)}, u32[]{:S(2)}) collective-permute-start(bf16[2,256,1024]{2,1,0:T(8,128)(2,1)} %fusion.30), channel_id=1, source_target_pairs={{0,1},{1,0},{2,3},{3,2},{4,5},{5,4},{6,7},{7,6},{8,9},{9,8},{10,11... | collective-permute-start | bytes 3145736 | tf_op jit(solution)/shard_map/ppermute | solution.py:273
  488.2 178.9 %reduce-scatter.7.cloned.1.call-start = ((), (), s32[]{:S(2)}) async-start(), calls=%async_computation.9 | async-start | bytes 3932160 | tf_op jit(solution)/shard_map/reduce_scatter | solution.py:436
  520.6 24.0 %collective-permute-start.43 = (bf16[2,256,1024]{2,1,0:T(8,128)(2,1)S(1)}, bf16[2,256,1024]{2,1,0:T(8,128)(2,1)S(1)}, u32[]{:S(2)}, u32[]{:S(2)}) collective-permute-start(bf16[2,256,1024]{2,1,0:T(8,128)(2,1)S(1)} %get-tuple-element.231), channel_id=1, source_target_pairs={{0,1},{1,0},{2,3},{3,2},{4,5},{5,4},{6,7},{7,6},{8,9},{9,8},{10,11... | collective-permute-start | bytes 3145736 | tf_op jit(solution)/shard_map/ppermute | solution.py:273
  522.3 23.9 %collective-permute-start.41 = (bf16[2,256,1024]{2,1,0:T(8,128)(2,1)S(1)}, bf16[2,256,1024]{2,1,0:T(8,128)(2,1)S(1)}, u32[]{:S(2)}, u32[]{:S(2)}) collective-permute-start(bf16[2,256,1024]{2,1,0:T(8,128)(2,1)S(1)} %get-tuple-element.225), channel_id=1, source_target_pairs={{0,4},{2,6},{4,0},{6,2},{8,12},{10,14},{12,8},{14,10},{16,20},{18,... | collective-permute-start | bytes 3145736 | tf_op jit(solution)/shard_map/ppermute | solution.py:267
  593.0 90.3 %reduce-scatter.11.cloned.1.call-start = ((), (), s32[]{:S(2)}) async-start(), calls=%async_computation.11 | async-start | bytes 1310720 | tf_op jit(solution)/shard_map/reduce_scatter | solution.py:436
  603.4 25.5 %collective-permute-start.51 = (bf16[2,512,512]{2,1,0:T(8,128)(2,1)}, bf16[2,512,512]{2,1,0:T(8,128)(2,1)}, u32[]{:S(2)}, u32[]{:S(2)}) collective-permute-start(bf16[2,512,512]{2,1,0:T(8,128)(2,1)} %add_convert_fusion), channel_id=1, source_target_pairs={{0,1},{1,0},{2,3},{3,2},{4,5},{5,4},{6,7},{7,6},{8,9},{9,8},{10,11... | collective-permute-start | bytes 3145736 | tf_op jit(solution)/shard_map/ppermute | solution.py:273
  610.8 25.7 %collective-permute-start.48 = (bf16[512,1024]{1,0:T(8,128)(2,1)}, bf16[512,1024]{1,0:T(8,128)(2,1)}, u32[]{:S(2)}, u32[]{:S(2)}) collective-permute-start(bf16[512,1024]{1,0:T(8,128)(2,1)} %add_convert_fusion.1), channel_id=1, source_target_pairs={{0,4},{2,6},{4,0},{6,2},{8,12},{10,14},{12,8},{14,10},{16,20},{18,... | collective-permute-start | bytes 3145736 | tf_op jit(solution)/shard_map/ppermute | solution.py:267
  633.3 27.7 %collective-permute-start.52 = (bf16[512,512]{1,0:T(8,128)(2,1)}, bf16[512,512]{1,0:T(8,128)(2,1)}, u32[]{:S(2)}, u32[]{:S(2)}) collective-permute-start(bf16[512,512]{1,0:T(8,128)(2,1)} %fusion.48), channel_id=1, source_target_pairs={{0,4},{2,6},{4,0},{6,2},{8,12},{10,14},{12,8},{14,10},{16,20},{18,... | collective-permute-start | bytes 1572872 | tf_op jit(solution)/shard_map/ppermute | solution.py:267
  659.6 18.9 %collective-permute-start.64 = (bf16[128,1,2048]{2,0,1:T(8,128)(2,1)}, bf16[128,1,2048]{2,0,1:T(8,128)(2,1)}, u32[]{:S(2)}, u32[]{:S(2)}) collective-permute-start(bf16[128,1,2048]{2,0,1:T(8,128)(2,1)} %fusion.53), channel_id=1, source_target_pairs={{0,2},{2,0},{4,6},{6,4},{8,10},{10,8},{12,14},{14,12},{16,18},{18,... | collective-permute-start | bytes 1572872 | tf_op jit(solution)/shard_map/ppermute | solution.py:264
  667.2 46.4 %collective-permute-start.46 = (bf16[256,1024]{1,0:T(8,128)(2,1)}, bf16[256,1024]{1,0:T(8,128)(2,1)}, u32[]{:S(2)}, u32[]{:S(2)}) collective-permute-start(bf16[256,1024]{1,0:T(8,128)(2,1)} %constant_dynamic-slice_fusion.9), channel_id=1, source_target_pairs={{0,1},{1,0},{2,3},{3,2},{4,5},{5,4},{6,7},{7,6},{8,9},{9,8},{10,11... | collective-permute-start | bytes 1572872 | tf_op jit(solution)/shard_map/ppermute | solution.py:273
  670.0 47.8 %all-to-all-start.1 = ((bf16[32,16,1024]{2,0,1:T(8,128)(2,1)}), bf16[32,16,1024]{2,0,1:T(8,128)(2,1)}, u32[]{:S(2)}, u32[]{:S(2)}) async-start(bf16[32,16,1024]{2,0,1:T(8,128)(2,1)} %copy.171), calls=%async_computation.4 | async-start | bytes 2097152 | tf_op jit(solution)/shard_map/all_to_all | solution.py:566
  676.4 36.7 %collective-permute-start.53 = (bf16[256,3,256]{0,2,1:T(8,128)(2,1)}, bf16[256,3,256]{0,2,1:T(8,128)(2,1)S(1)}, u32[]{:S(2)}, u32[]{:S(2)}) collective-permute-start(bf16[256,3,256]{0,2,1:T(8,128)(2,1)} %constant_dynamic-slice_fusion.6), channel_id=1, source_target_pairs={{0,4},{2,6},{4,0},{6,2},{8,12},{10,14},{12,8},{14,10},{16,20},{18,... | collective-permute-start | bytes 1179656 | tf_op jit(solution)/shard_map/ppermute | solution.py:267
  (125 other events, 831.4 us)
Sparse Core Ops, SparseCore 0:
  37.2 83.6 all-gather.2
  122.5 148.1 all-gather.4
  425.3 73.4 reduce-scatter.4
  501.1 77.2 reduce-scatter.8
  593.1 59.8 reduce-scatter.6
  655.2 28.0 reduce-scatter.10

commit v6 on v5

--- a/solution.py
+++ b/solution.py
@@ -296,11 +296,27 @@
         weight = in_order(side, mine, side_swap(sent), 0)
         return weight.reshape(4 * shard, -1)
 
+    def split_direct(weight):
+        def quarter_of(c, s):
+            size = weight.shape[2] // 4
+            return take(weight, (2 * c + s) * size, size, 2)
+
+        mine = quarter_of(core, side)
+        by_core = core_swap(quarter_of(1 - core, side))
+        by_side = side_swap(quarter_of(core, 1 - side))
+        by_both = lax.ppermute(
+            quarter_of(1 - core, 1 - side), "dp", [(i, i ^ 3) for i in range(groups)]
+        )
+        own_side = in_order(core, mine, by_core, 0)
+        return in_order(side, own_side, in_order(core, by_side, by_both, 0), 0).reshape(
+            4 * shard, -1
+        )
+
     def gather_weight(piece):
         return lax.all_gather(piece, "dp", axis=0, axis_index_groups=ring_groups, tiled=True)
 
     first_weights = jnp.concatenate([qkv_weight, out_weight.T[None]], axis=0).swapaxes(0, 1)
-    first_piece = split_weight(first_weights)
+    first_piece = split_direct(first_weights)
     first_full = gather_weight(first_piece)
 
     small = jnp.concatenate(
@@ -332,7 +348,7 @@
     arrived = lax.all_to_all(sending, "dp", split_axis=1, concat_axis=1, tiled=True)
     tokens = after(arrived, first_piece).reshape(seq_len, half)
     second_weights = after(up_weight, arrived), after(down_weight, arrived).T
-    second_piece = split_weight(jnp.stack(second_weights, axis=1))
+    second_piece = split_direct(jnp.stack(second_weights, axis=1))
     second_full = gather_weight(second_piece)
     early, late = tokens[:token_half], tokens[token_half:]
     early = in_order(lane, early, lane_swap(early), 1)

time: 737 us -> 740 us (level)
  waiting for transfers between devices: 320 us -> 311 us
    ppermute x19, waiting for transfers between devices: 101 us -> 83.6 us  [lane_swap(): return lax.ppermute(array, 'tensor', [(0, 1), (1, 0)])]
    ppermute x0 -> x2, waiting for transfers between devices: none -> 10.7 us  [split_direct(): lax.ppermute(quarter_of(1 - core, 1 - side), 'dp', [(i, i ^ 3) for i in r...]
    unnamed x181 -> x183, local copies, waits for them, and re-layouts: 47.4 us -> 42.4 us
  transfers between devices with their start and end apart: 73 -> 75, of which waited for: 43 -> 42; matrix products, arithmetic and copies ran while one was open for 16% -> 18% of each run, Pallas kernels for 16% -> 17%
where the time goes in v6:
time: 740 us; the launch traced here: 730 us
  waiting for transfers between devices  311 us (42%)
  Pallas kernels  155 us (21%)
  local copies, waits for them, and re-layouts  88.7 us (12%)
  other arithmetic  85.7 us (12%)
  starting transfers between devices  73 us (10%)
  between operations  16.5 us (2%)
    ppermute x24, waiting for transfers between devices, side_swap(): return lax.ppermute(array, 'dp', side_pairs)  167 us
    ppermute x19, waiting for transfers between devices, lane_swap(): return lax.ppermute(array, 'tensor', [(0, 1), (1, 0)])  83.6 us
    pallas_call x12, Pallas kernels, matmul(): call(functools.partial(matmul_kernel, right_axis), 2 * rows * depth * siz...  64.3 us
    unnamed x183, local copies, waits for them, and re-layouts  42.4 us
    pallas_call x4, Pallas kernels, pair_matmul(): call(pair_kernel, 4 * rows * depth * columns, jax.ShapeDtypeStruct((depth...  42.4 us
    all_gather x2, waiting for transfers between devices, gather_weight(): lax.all_gather(piece, 'dp', axis=0, axis_index_groups=ring_groups, tiled=...  29.1 us
    ppermute x24, starting transfers between devices, side_swap(): return lax.ppermute(array, 'dp', side_pairs)  24.1 us
    ppermute x19, starting transfers between devices, lane_swap(): return lax.ppermute(array, 'tensor', [(0, 1), (1, 0)])  19.1 us
  transfers between devices with their start and end apart: 75, of which 42 were waited for; matrix products, arithmetic and copies ran while one was open for 18% of the time, Pallas kernels for 17%

profile of v6, /device:TPU:0, one launch (start us, length us, event | category | flops | bytes accessed | tf_op | source)
XLA Modules:
  0.0 729.9 jit_solution(14796413322686335466)
XLA Ops:
  53.3 8.2 %collective-permute-done.5 = bf16[256,1024]{1,0:T(8,128)(2,1)S(1)} collective-permute-done((bf16[256,1024]{1,0:T(8,128)(2,1)S(1)}, bf16[256,1024]{1,0:T(8,128)(2,1)S(1)}, u32[]{:S(2)}, u32[]{:S(2)}) %collective-permute-start.5) | collective-permute-done | bytes 524320 | tf_op jit(solution)/shard_map/ppermute | solution.py:267
  70.1 10.3 %collective-permute-done.8 = bf16[128,2,1024]{0,2,1:T(8,128)(2,1)} collective-permute-done((bf16[128,2,1024]{0,2,1:T(8,128)(2,1)}, bf16[128,2,1024]{0,2,1:T(8,128)(2,1)}, u32[]{:S(2)}, u32[]{:S(2)}) %collective-permute-start.8) | collective-permute-done | bytes 524320 | tf_op jit(solution)/shard_map/ppermute | solution.py:267
  80.5 10.7 %collective-permute-done.9 = bf16[128,2,1024]{0,2,1:T(8,128)(2,1)} collective-permute-done((bf16[128,2,1024]{0,2,1:T(8,128)(2,1)}, bf16[128,2,1024]{0,2,1:T(8,128)(2,1)}, u32[]{:S(2)}, u32[]{:S(2)}) %collective-permute-start.9) | collective-permute-done | bytes 524320 | tf_op jit(solution)/shard_map/ppermute | solution.py:307
  101.2 12.0 %collective-permute-done.4 = bf16[256,2048]{1,0:T(8,128)(2,1)} collective-permute-done((bf16[256,2048]{1,0:T(8,128)(2,1)}, bf16[256,2048]{1,0:T(8,128)(2,1)}, u32[]{:S(2)}, u32[]{:S(2)}) %collective-permute-start.4) | collective-permute-done | bytes 1048608 | tf_op jit(solution)/shard_map/ppermute | solution.py:267
  122.2 6.8 shard_map.263.query.key.value
  155.1 23.1 %collective-permute-done.17 = bf16[2,256,1024]{2,1,0:T(8,128)(2,1)S(1)} collective-permute-done((bf16[2,256,1024]{2,1,0:T(8,128)(2,1)S(1)}, bf16[2,256,1024]{2,1,0:T(8,128)(2,1)S(1)}, u32[]{:S(2)}, u32[]{:S(2)}) %collective-permute-start.17) | collective-permute-done | bytes 1048608 | tf_op jit(solution)/shard_map/ppermute | solution.py:267
  184.1 11.3 %collective-permute-done.20 = bf16[256,1024]{1,0:T(8,128)(2,1)} collective-permute-done((bf16[256,1024]{1,0:T(8,128)(2,1)}, bf16[256,1024]{1,0:T(8,128)(2,1)}, u32[]{:S(2)}, u32[]{:S(2)}) %collective-permute-start.20) | collective-permute-done | bytes 524320 | tf_op jit(solution)/shard_map/ppermute | solution.py:267
  203.2 10.5 %collective-permute-done.23 = bf16[256,1024]{1,0:T(8,128)(2,1)S(1)} collective-permute-done((bf16[256,1024]{1,0:T(8,128)(2,1)S(1)}, bf16[256,1024]{1,0:T(8,128)(2,1)S(1)}, u32[]{:S(2)}, u32[]{:S(2)}) %collective-permute-start.23) | collective-permute-done | bytes 524320 | tf_op jit(solution)/shard_map/ppermute | solution.py:267
  216.4 20.3 %collective-permute-done.24 = bf16[2,256,1024]{2,1,0:T(8,128)(2,1)S(1)} collective-permute-done((bf16[2,256,1024]{2,1,0:T(8,128)(2,1)S(1)}, bf16[2,256,1024]{2,1,0:T(8,128)(2,1)S(1)}, u32[]{:S(2)}, u32[]{:S(2)}) %collective-permute-start.24) | collective-permute-done | bytes 1048608 | tf_op jit(solution)/shard_map/ppermute | solution.py:273
  239.9 29.1 %all-gather.5.cloned.1.call-done.weight.right = bf16[2048,2048]{1,0:T(8,128)(2,1)} async-done(((bf16[512,2048]{1,0:T(8,128)(2,1)}), bf16[2048,2048]{1,0:T(8,128)(2,1)}) %all-gather.5.cloned.1.call-update) | async-done | bytes 8388624 | tf_op jit(solution)/shard_map/all_gather | solution.py:316
  272.2 7.6 %shard_map.269 = (f32[1024,1024]{1,0:T(8,128)S(1)}, bf16[1024,1024]{1,0:T(8,128)(2,1)S(1)}) custom-call(bf16[1024,2048]{1,0:T(8,128)(2,1)S(1)} %bitcast.328, bf16[2048,2048]{1,0:T(8,128)(2,1)} %all-gather.5.cloned.1.call-done.weight.right, f32[1,1024]{1,0:T(1,128)S(1)} %bitcast.341), custom_call_target="tpu_custom_call" | custom-call | flops 536870912 | tf_op jit(solution)/shard_map/pallas_call | solution.py:177
  283.2 8.8 %shard_map.271 = (f32[1024,1024]{1,0:T(8,128)S(1)}, bf16[1024,1024]{1,0:T(8,128)(2,1)S(1)}) custom-call(bf16[1024,2048]{1,0:T(8,128)(2,1)} %collective-permute-done.25.rows.left_two, bf16[2048,2048]{1,0:T(8,128)(2,1)} %all-gather.5.cloned.1.call-done.weight.right, f32[1,1024]{1,0:T(1,128)S(1)} %bitcast.342), custom_call_target="tpu_custom_call" | custom-call | flops 536870912 | tf_op jit(solution)/shard_map/pallas_call | solution.py:177
  293.9 8.6 %shard_map.272 = bf16[1024,2048]{1,0:T(8,128)(2,1)} custom-call(bf16[1024,1024]{1,0:T(8,128)(2,1)S(1)} %get-tuple-element.69.left.right_two, bf16[2048,2048]{1,0:T(8,128)(2,1)} %all-gather.5.cloned.1.call-done.weight.right), custom_call_target="tpu_custom_call" | custom-call | flops 536870912 | tf_op jit(solution)/shard_map/pallas_call | solution.py:149
  307.9 6.7 shard_map.270
  326.3 16.5 %collective-permute-done.27 = bf16[2,256,1024]{2,1,0:T(8,128)(2,1)S(1)} collective-permute-done((bf16[2,256,1024]{2,1,0:T(8,128)(2,1)S(1)}, bf16[2,256,1024]{2,1,0:T(8,128)(2,1)S(1)}, u32[]{:S(2)}, u32[]{:S(2)}) %collective-permute-start.27) | collective-permute-done | bytes 1048608 | tf_op jit(solution)/shard_map/ppermute | solution.py:267
  349.8 9.8 %collective-permute-done.30 = bf16[256,1024]{1,0:T(8,128)(2,1)S(1)} collective-permute-done((bf16[256,1024]{1,0:T(8,128)(2,1)S(1)}, bf16[256,1024]{1,0:T(8,128)(2,1)S(1)}, u32[]{:S(2)}, u32[]{:S(2)}) %collective-permute-start.30) | collective-permute-done | bytes 524320 | tf_op jit(solution)/shard_map/ppermute | solution.py:267
  365.4 9.2 %collective-permute-done.34 = bf16[256,1024]{1,0:T(8,128)(2,1)S(1)} collective-permute-done((bf16[256,1024]{1,0:T(8,128)(2,1)S(1)}, bf16[256,1024]{1,0:T(8,128)(2,1)S(1)}, u32[]{:S(2)}, u32[]{:S(2)}) %collective-permute-start.34) | collective-permute-done | bytes 524320 | tf_op jit(solution)/shard_map/ppermute | solution.py:267
  377.7 20.5 %collective-permute-done.35 = bf16[2,256,1024]{2,1,0:T(8,128)(2,1)S(1)} collective-permute-done((bf16[2,256,1024]{2,1,0:T(8,128)(2,1)S(1)}, bf16[2,256,1024]{2,1,0:T(8,128)(2,1)S(1)}, u32[]{:S(2)}, u32[]{:S(2)}) %collective-permute-start.35) | collective-permute-done | bytes 1048608 | tf_op jit(solution)/shard_map/ppermute | solution.py:273
  399.3 6.8 shard_map.273
  409.4 11.9 %shard_map.275 = bf16[2048,1024]{1,0:T(8,128)(2,1)S(1)} custom-call(bf16[1024,2048]{1,0:T(8,128)(2,1)S(1)} %bitcast.326, bf16[1024,1024]{1,0:T(8,128)(2,1)S(1)} %copy-done.20, bf16[1024,2048]{1,0:T(8,128)(2,1)} %copy-done.11, bf16[1024,1024]{1,0:T(8,128)(2,1)S(1)} %copy-done.22), custom_call_target="tpu_custom_call" | custom-call | flops 1073741824 | tf_op jit(solution)/shard_map/pallas_call | solution.py:226
  427.7 6.9 shard_map.276
  434.7 6.9 shard_map.277
  454.0 11.8 %shard_map.278 = bf16[2048,1024]{1,0:T(8,128)(2,1)S(1)} custom-call(bf16[1024,2048]{1,0:T(8,128)(2,1)S(1)} %bitcast.329, bf16[1024,1024]{1,0:T(8,128)(2,1)S(1)} %copy-done.24, bf16[1024,2048]{1,0:T(8,128)(2,1)} %collective-permute-done.25.rows.left_two, bf16[1024,1024]{1,0:T(8,128)(2,1)S(1)} %get-tuple-element.81.left.right_two), custom_call_target="tpu_custom_call" | custom-call | flops 1073741824 | tf_op jit(solution)/shard_map/pallas_call | solution.py:226
  467.9 8.0 %collective-permute-done.38 = bf16[2,256,1024]{2,1,0:T(8,128)(2,1)} collective-permute-done((bf16[2,256,1024]{2,1,0:T(8,128)(2,1)}, bf16[2,256,1024]{2,1,0:T(8,128)(2,1)}, u32[]{:S(2)}, u32[]{:S(2)}) %collective-permute-start.38) | collective-permute-done | bytes 1048608 | tf_op jit(solution)/shard_map/ppermute | solution.py:267
  486.4 11.4 %collective-permute-done.41 = bf16[256,1024]{1,0:T(8,128)(2,1)} collective-permute-done((bf16[256,1024]{1,0:T(8,128)(2,1)}, bf16[256,1024]{1,0:T(8,128)(2,1)}, u32[]{:S(2)}, u32[]{:S(2)}) %collective-permute-start.41) | collective-permute-done | bytes 524320 | tf_op jit(solution)/shard_map/ppermute | solution.py:267
  507.8 10.8 %collective-permute-done.44 = bf16[256,1024]{1,0:T(8,128)(2,1)S(1)} collective-permute-done((bf16[256,1024]{1,0:T(8,128)(2,1)S(1)}, bf16[256,1024]{1,0:T(8,128)(2,1)S(1)}, u32[]{:S(2)}, u32[]{:S(2)}) %collective-permute-start.44) | collective-permute-done | bytes 524320 | tf_op jit(solution)/shard_map/ppermute | solution.py:267
  522.0 20.8 %collective-permute-done.45 = bf16[2,256,1024]{2,1,0:T(8,128)(2,1)S(1)} collective-permute-done((bf16[2,256,1024]{2,1,0:T(8,128)(2,1)S(1)}, bf16[2,256,1024]{2,1,0:T(8,128)(2,1)S(1)}, u32[]{:S(2)}, u32[]{:S(2)}) %collective-permute-start.45) | collective-permute-done | bytes 1048608 | tf_op jit(solution)/shard_map/ppermute | solution.py:273
  583.9 10.2 %shard_map.285 = bf16[2048,768]{1,0:T(8,128)(2,1)S(1)} custom-call(bf16[1024,2048]{1,0:T(8,128)(2,1)} %bitcast.18.left.left_one, bf16[1024,768]{1,0:T(8,128)(2,1)S(1)} %shard_map.280.left.right_one, bf16[1024,2048]{1,0:T(8,128)(2,1)} %collective-permute-done.15.left.left_two, bf16[1024,768]{1,0:T(8,128)(2,1)S(1)} %shard_map.283.left.right_two), custom_call_target="tpu_custom_call" | custom-call | flops 805306368 | tf_op jit(solution)/shard_map/pallas_call | solution.py:226
  615.8 8.4 %shard_map.286 = bf16[2048,256]{1,0:T(8,128)(2,1)} custom-call(bf16[1024,2048]{1,0:T(8,128)(2,1)} %bitcast.103.left.left_one, bf16[1024,256]{1,0:T(8,128)(2,1)S(1)} %copy-done.26, bf16[1024,2048]{1,0:T(8,128)(2,1)} %collective-permute-done.46.left.left_two, bf16[1024,256]{1,0:T(8,128)(2,1)S(1)} %copy-done.28), custom_call_target="tpu_custom_call" | custom-call | flops 268435456 | tf_op jit(solution)/shard_map/pallas_call | solution.py:226
  624.3 7.5 %collective-permute-done.53 = bf16[2,512,512]{2,1,0:T(8,128)(2,1)} collective-permute-done((bf16[2,512,512]{2,1,0:T(8,128)(2,1)}, bf16[2,512,512]{2,1,0:T(8,128)(2,1)}, u32[]{:S(2)}, u32[]{:S(2)}) %collective-permute-start.53) | collective-permute-done | bytes 1048608 | tf_op jit(solution)/shard_map/ppermute | solution.py:273
  654.4 6.8 collective-permute-done.65
  685.7 12.1 %collective-permute-done.58 = f32[4,1,1152]{2,1,0:T(1,128)S(1)} collective-permute-done((f32[4,1,1152]{2,1,0:T(1,128)S(1)}, f32[4,1,1152]{2,1,0:T(1,128)S(1)}, u32[]{:S(2)}, u32[]{:S(2)}) %collective-permute-start.58) | collective-permute-done | bytes 18464 | tf_op jit(solution)/shard_map/ppermute | solution.py:267
  (542 shorter events, 343.1 us)
Async XLA Ops:
  15.9 29.6 %all-to-all-start = ((bf16[32,16,1024]{2,0,1:T(8,128)(2,1)}), bf16[32,16,1024]{2,0,1:T(8,128)(2,1)S(1)}, u32[]{:S(2)}, u32[]{:S(2)}) async-start(bf16[32,16,1024]{2,0,1:T(8,128)(2,1)} %select_bitcast_fusion), calls=%async_computation | async-start | bytes 2097152 | tf_op jit(solution)/shard_map/all_to_all | solution.py:348
  22.4 97.7 %all-gather.3.cloned.1.call-start = ((), (), s32[]{:S(2)}) async-start(), calls=%async_computation.6 | async-start | bytes 5242880 | tf_op jit(solution)/shard_map/all_gather | solution.py:316
  36.9 232.1 %all-gather.5.cloned.1.call-start = ((), (), s32[]{:S(2)}) async-start(), calls=%async_computation.7 | async-start | bytes 10485760 | tf_op jit(solution)/shard_map/all_gather | solution.py:316
  62.6 37.2 %collective-permute-start.6 = (bf16[2,256,1024]{2,1,0:T(8,128)(2,1)}, bf16[2,256,1024]{2,1,0:T(8,128)(2,1)}, u32[]{:S(2)}, u32[]{:S(2)}) collective-permute-start(bf16[2,256,1024]{2,1,0:T(8,128)(2,1)} %pad_maximum_fusion.6), channel_id=1, source_target_pairs={{0,1},{1,0},{2,3},{3,2},{4,5},{5,4},{6,7},{7,6},{8,9},{9,8},{10,11... | collective-permute-start | bytes 3145736 | tf_op jit(solution)/shard_map/ppermute | solution.py:273
  67.2 23.9 %collective-permute-start.9 = (bf16[128,2,1024]{0,2,1:T(8,128)(2,1)}, bf16[128,2,1024]{0,2,1:T(8,128)(2,1)}, u32[]{:S(2)}, u32[]{:S(2)}) collective-permute-start(bf16[128,2,1024]{0,2,1:T(8,128)(2,1)} %get-tuple-element.199), channel_id=1, source_target_pairs={{0,6},{2,4},{4,2},{6,0},{8,14},{10,12},{12,10},{14,8},{16,22},{18,... | collective-permute-start | bytes 1572872 | tf_op jit(solution)/shard_map/ppermute | solution.py:307
  68.6 44.6 %collective-permute-start.4 = (bf16[256,2048]{1,0:T(8,128)(2,1)}, bf16[256,2048]{1,0:T(8,128)(2,1)}, u32[]{:S(2)}, u32[]{:S(2)}) collective-permute-start(bf16[256,2048]{1,0:T(8,128)(2,1)} %get-tuple-element.251), channel_id=1, source_target_pairs={{0,4},{2,6},{4,0},{6,2},{8,12},{10,14},{12,8},{14,10},{16,20},{18,... | collective-permute-start | bytes 3145736 | tf_op jit(solution)/shard_map/ppermute | solution.py:267
  118.5 379.3 %reduce-scatter.5.cloned.1.call-start = ((), (), s32[]{:S(2)}) async-start(), calls=%async_computation.8 | async-start | bytes 5242880 | tf_op jit(solution)/shard_map/reduce_scatter | solution.py:452
  152.7 25.5 %collective-permute-start.17 = (bf16[2,256,1024]{2,1,0:T(8,128)(2,1)S(1)}, bf16[2,256,1024]{2,1,0:T(8,128)(2,1)S(1)}, u32[]{:S(2)}, u32[]{:S(2)}) collective-permute-start(bf16[2,256,1024]{2,1,0:T(8,128)(2,1)S(1)} %fusion.25), channel_id=1, source_target_pairs={{0,4},{2,6},{4,0},{6,2},{8,12},{10,14},{12,8},{14,10},{16,20},{18,... | collective-permute-start | bytes 3145736 | tf_op jit(solution)/shard_map/ppermute | solution.py:267
  154.4 25.1 %collective-permute-start.19 = (bf16[2,256,1024]{2,1,0:T(8,128)(2,1)S(1)}, bf16[2,256,1024]{2,1,0:T(8,128)(2,1)S(1)}, u32[]{:S(2)}, u32[]{:S(2)}) collective-permute-start(bf16[2,256,1024]{2,1,0:T(8,128)(2,1)S(1)} %fusion.26), channel_id=1, source_target_pairs={{0,1},{1,0},{2,3},{3,2},{4,5},{5,4},{6,7},{7,6},{8,9},{9,8},{10,11... | collective-permute-start | bytes 3145736 | tf_op jit(solution)/shard_map/ppermute | solution.py:273
  213.8 22.9 %collective-permute-start.24 = (bf16[2,256,1024]{2,1,0:T(8,128)(2,1)S(1)}, bf16[2,256,1024]{2,1,0:T(8,128)(2,1)S(1)}, u32[]{:S(2)}, u32[]{:S(2)}) collective-permute-start(bf16[2,256,1024]{2,1,0:T(8,128)(2,1)S(1)} %get-tuple-element.247), channel_id=1, source_target_pairs={{0,1},{1,0},{2,3},{3,2},{4,5},{5,4},{6,7},{7,6},{8,9},{9,8},{10,11... | collective-permute-start | bytes 3145736 | tf_op jit(solution)/shard_map/ppermute | solution.py:273
  214.7 22.5 %collective-permute-start.22 = (bf16[2,256,1024]{2,1,0:T(8,128)(2,1)S(1)}, bf16[2,256,1024]{2,1,0:T(8,128)(2,1)S(1)}, u32[]{:S(2)}, u32[]{:S(2)}) collective-permute-start(bf16[2,256,1024]{2,1,0:T(8,128)(2,1)S(1)} %get-tuple-element.241), channel_id=1, source_target_pairs={{0,4},{2,6},{4,0},{6,2},{8,12},{10,14},{12,8},{14,10},{16,20},{18,... | collective-permute-start | bytes 3145736 | tf_op jit(solution)/shard_map/ppermute | solution.py:267
  304.8 43.6 %collective-permute-start.31 = (bf16[256,1024]{1,0:T(8,128)(2,1)}, bf16[256,1024]{1,0:T(8,128)(2,1)}, u32[]{:S(2)}, u32[]{:S(2)}) collective-permute-start(bf16[256,1024]{1,0:T(8,128)(2,1)} %constant_dynamic-slice_fusion.7), channel_id=1, source_target_pairs={{0,1},{1,0},{2,3},{3,2},{4,5},{5,4},{6,7},{7,6},{8,9},{9,8},{10,11... | collective-permute-start | bytes 1572872 | tf_op jit(solution)/shard_map/ppermute | solution.py:273
  318.0 24.9 %collective-permute-start.27 = (bf16[2,256,1024]{2,1,0:T(8,128)(2,1)S(1)}, bf16[2,256,1024]{2,1,0:T(8,128)(2,1)S(1)}, u32[]{:S(2)}, u32[]{:S(2)}) collective-permute-start(bf16[2,256,1024]{2,1,0:T(8,128)(2,1)S(1)} %fusion.27), channel_id=1, source_target_pairs={{0,4},{2,6},{4,0},{6,2},{8,12},{10,14},{12,8},{14,10},{16,20},{18,... | collective-permute-start | bytes 3145736 | tf_op jit(solution)/shard_map/ppermute | solution.py:267
  319.5 24.6 %collective-permute-start.29 = (bf16[2,256,1024]{2,1,0:T(8,128)(2,1)S(1)}, bf16[2,256,1024]{2,1,0:T(8,128)(2,1)S(1)}, u32[]{:S(2)}, u32[]{:S(2)}) collective-permute-start(bf16[2,256,1024]{2,1,0:T(8,128)(2,1)S(1)} %fusion.28), channel_id=1, source_target_pairs={{0,1},{1,0},{2,3},{3,2},{4,5},{5,4},{6,7},{7,6},{8,9},{9,8},{10,11... | collective-permute-start | bytes 3145736 | tf_op jit(solution)/shard_map/ppermute | solution.py:273
  374.7 23.4 %collective-permute-start.35 = (bf16[2,256,1024]{2,1,0:T(8,128)(2,1)S(1)}, bf16[2,256,1024]{2,1,0:T(8,128)(2,1)S(1)}, u32[]{:S(2)}, u32[]{:S(2)}) collective-permute-start(bf16[2,256,1024]{2,1,0:T(8,128)(2,1)S(1)} %get-tuple-element.239), channel_id=1, source_target_pairs={{0,1},{1,0},{2,3},{3,2},{4,5},{5,4},{6,7},{7,6},{8,9},{9,8},{10,11... | collective-permute-start | bytes 3145736 | tf_op jit(solution)/shard_map/ppermute | solution.py:273
  377.6 20.6 %collective-permute-start.33 = (bf16[2,256,1024]{2,1,0:T(8,128)(2,1)S(1)}, bf16[2,256,1024]{2,1,0:T(8,128)(2,1)S(1)}, u32[]{:S(2)}, u32[]{:S(2)}) collective-permute-start(bf16[2,256,1024]{2,1,0:T(8,128)(2,1)S(1)} %get-tuple-element.233), channel_id=1, source_target_pairs={{0,4},{2,6},{4,0},{6,2},{8,12},{10,14},{12,8},{14,10},{16,20},{18,... | collective-permute-start | bytes 3145736 | tf_op jit(solution)/shard_map/ppermute | solution.py:267
  423.4 176.0 %reduce-scatter.9.cloned.1.call-start = ((), (), s32[]{:S(2)}) async-start(), calls=%async_computation.10 | async-start | bytes 5242880 | tf_op jit(solution)/shard_map/reduce_scatter | solution.py:452
  450.2 25.7 %collective-permute-start.38 = (bf16[2,256,1024]{2,1,0:T(8,128)(2,1)}, bf16[2,256,1024]{2,1,0:T(8,128)(2,1)}, u32[]{:S(2)}, u32[]{:S(2)}) collective-permute-start(bf16[2,256,1024]{2,1,0:T(8,128)(2,1)} %fusion.29), channel_id=1, source_target_pairs={{0,4},{2,6},{4,0},{6,2},{8,12},{10,14},{12,8},{14,10},{16,20},{18,... | collective-permute-start | bytes 3145736 | tf_op jit(solution)/shard_map/ppermute | solution.py:267
  453.4 25.6 %collective-permute-start.40 = (bf16[2,256,1024]{2,1,0:T(8,128)(2,1)}, bf16[2,256,1024]{2,1,0:T(8,128)(2,1)}, u32[]{:S(2)}, u32[]{:S(2)}) collective-permute-start(bf16[2,256,1024]{2,1,0:T(8,128)(2,1)} %fusion.30), channel_id=1, source_target_pairs={{0,1},{1,0},{2,3},{3,2},{4,5},{5,4},{6,7},{7,6},{8,9},{9,8},{10,11... | collective-permute-start | bytes 3145736 | tf_op jit(solution)/shard_map/ppermute | solution.py:273
  486.4 183.6 %reduce-scatter.7.cloned.1.call-start = ((), (), s32[]{:S(2)}) async-start(), calls=%async_computation.9 | async-start | bytes 3932160 | tf_op jit(solution)/shard_map/reduce_scatter | solution.py:452
  518.7 24.0 %collective-permute-start.45 = (bf16[2,256,1024]{2,1,0:T(8,128)(2,1)S(1)}, bf16[2,256,1024]{2,1,0:T(8,128)(2,1)S(1)}, u32[]{:S(2)}, u32[]{:S(2)}) collective-permute-start(bf16[2,256,1024]{2,1,0:T(8,128)(2,1)S(1)} %get-tuple-element.231), channel_id=1, source_target_pairs={{0,1},{1,0},{2,3},{3,2},{4,5},{5,4},{6,7},{7,6},{8,9},{9,8},{10,11... | collective-permute-start | bytes 3145736 | tf_op jit(solution)/shard_map/ppermute | solution.py:273
  520.4 24.0 %collective-permute-start.43 = (bf16[2,256,1024]{2,1,0:T(8,128)(2,1)S(1)}, bf16[2,256,1024]{2,1,0:T(8,128)(2,1)S(1)}, u32[]{:S(2)}, u32[]{:S(2)}) collective-permute-start(bf16[2,256,1024]{2,1,0:T(8,128)(2,1)S(1)} %get-tuple-element.225), channel_id=1, source_target_pairs={{0,4},{2,6},{4,0},{6,2},{8,12},{10,14},{12,8},{14,10},{16,20},{18,... | collective-permute-start | bytes 3145736 | tf_op jit(solution)/shard_map/ppermute | solution.py:267
  548.2 18.5 %collective-permute-start.46 = (bf16[1024,2048]{1,0:T(8,128)(2,1)}, bf16[1024,2048]{1,0:T(8,128)(2,1)}, u32[]{:S(2)}, u32[]{:S(2)}) collective-permute-start(bf16[1024,2048]{1,0:T(8,128)(2,1)} %bitcast.103.left.left_one), channel_id=1, source_target_pairs={{0,2},{2,0},{4,6},{6,4},{8,10},{10,8},{12,14},{14,12},{16,18},{18,... | collective-permute-start | bytes 12582920 | tf_op jit(solution)/shard_map/ppermute | solution.py:264
  549.3 17.4 %collective-permute-start.47 = (bf16[256,1,1024]{2,0,1:T(8,128)(2,1)S(1)}, bf16[256,1,1024]{2,0,1:T(8,128)(2,1)S(1)}, u32[]{:S(2)}, u32[]{:S(2)}) collective-permute-start(bf16[256,1,1024]{2,0,1:T(8,128)(2,1)S(1)} %dynamic-slice_bitcast_fusion.1), channel_id=1, source_target_pairs={{0,4},{2,6},{4,0},{6,2},{8,12},{10,14},{12,8},{14,10},{16,20},{18,... | collective-permute-start | bytes 1572872 | tf_op jit(solution)/shard_map/ppermute | solution.py:267
  595.8 89.9 %reduce-scatter.11.cloned.1.call-start = ((), (), s32[]{:S(2)}) async-start(), calls=%async_computation.11 | async-start | bytes 1310720 | tf_op jit(solution)/shard_map/reduce_scatter | solution.py:452
  606.2 25.6 %collective-permute-start.53 = (bf16[2,512,512]{2,1,0:T(8,128)(2,1)}, bf16[2,512,512]{2,1,0:T(8,128)(2,1)}, u32[]{:S(2)}, u32[]{:S(2)}) collective-permute-start(bf16[2,512,512]{2,1,0:T(8,128)(2,1)} %add_convert_fusion), channel_id=1, source_target_pairs={{0,1},{1,0},{2,3},{3,2},{4,5},{5,4},{6,7},{7,6},{8,9},{9,8},{10,11... | collective-permute-start | bytes 3145736 | tf_op jit(solution)/shard_map/ppermute | solution.py:273
  613.2 25.4 %collective-permute-start.50 = (bf16[512,1024]{1,0:T(8,128)(2,1)}, bf16[512,1024]{1,0:T(8,128)(2,1)}, u32[]{:S(2)}, u32[]{:S(2)}) collective-permute-start(bf16[512,1024]{1,0:T(8,128)(2,1)} %add_convert_fusion.1), channel_id=1, source_target_pairs={{0,4},{2,6},{4,0},{6,2},{8,12},{10,14},{12,8},{14,10},{16,20},{18,... | collective-permute-start | bytes 3145736 | tf_op jit(solution)/shard_map/ppermute | solution.py:267
  636.1 27.7 %collective-permute-start.54 = (bf16[512,512]{1,0:T(8,128)(2,1)}, bf16[512,512]{1,0:T(8,128)(2,1)}, u32[]{:S(2)}, u32[]{:S(2)}) collective-permute-start(bf16[512,512]{1,0:T(8,128)(2,1)} %fusion.44), channel_id=1, source_target_pairs={{0,4},{2,6},{4,0},{6,2},{8,12},{10,14},{12,8},{14,10},{16,20},{18,... | collective-permute-start | bytes 1572872 | tf_op jit(solution)/shard_map/ppermute | solution.py:267
  662.3 18.2 %collective-permute-start.66 = (bf16[128,1,2048]{2,0,1:T(8,128)(2,1)}, bf16[128,1,2048]{2,0,1:T(8,128)(2,1)}, u32[]{:S(2)}, u32[]{:S(2)}) collective-permute-start(bf16[128,1,2048]{2,0,1:T(8,128)(2,1)} %fusion.45), channel_id=1, source_target_pairs={{0,2},{2,0},{4,6},{6,4},{8,10},{10,8},{12,14},{14,12},{16,18},{18,... | collective-permute-start | bytes 1572872 | tf_op jit(solution)/shard_map/ppermute | solution.py:264
  670.0 45.7 %collective-permute-start.48 = (bf16[256,1024]{1,0:T(8,128)(2,1)}, bf16[256,1024]{1,0:T(8,128)(2,1)}, u32[]{:S(2)}, u32[]{:S(2)}) collective-permute-start(bf16[256,1024]{1,0:T(8,128)(2,1)} %constant_dynamic-slice_fusion.8), channel_id=1, source_target_pairs={{0,1},{1,0},{2,3},{3,2},{4,5},{5,4},{6,7},{7,6},{8,9},{9,8},{10,11... | collective-permute-start | bytes 1572872 | tf_op jit(solution)/shard_map/ppermute | solution.py:273
  672.8 47.1 %all-to-all-start.1 = ((bf16[32,16,1024]{2,0,1:T(8,128)(2,1)}), bf16[32,16,1024]{2,0,1:T(8,128)(2,1)}, u32[]{:S(2)}, u32[]{:S(2)}) async-start(bf16[32,16,1024]{2,0,1:T(8,128)(2,1)} %copy.195), calls=%async_computation.4 | async-start | bytes 2097152 | tf_op jit(solution)/shard_map/all_to_all | solution.py:582
  678.5 36.7 %collective-permute-start.55 = (bf16[256,3,256]{0,2,1:T(8,128)(2,1)}, bf16[256,3,256]{0,2,1:T(8,128)(2,1)S(1)}, u32[]{:S(2)}, u32[]{:S(2)}) collective-permute-start(bf16[256,3,256]{0,2,1:T(8,128)(2,1)} %constant_dynamic-slice_fusion.5), channel_id=1, source_target_pairs={{0,4},{2,6},{4,0},{6,2},{8,12},{10,14},{12,8},{14,10},{16,20},{18,... | collective-permute-start | bytes 1179656 | tf_op jit(solution)/shard_map/ppermute | solution.py:267
  (127 other events, 866.7 us)
Sparse Core Ops, SparseCore 0:
  37.0 81.7 all-gather.2
  120.4 148.6 all-gather.4
  423.5 73.4 reduce-scatter.4
  499.2 77.2 reduce-scatter.8
  595.9 59.2 reduce-scatter.6
  657.4 28.2 reduce-scatter.10
